TPU v7x, 32 devices: a whole 2x2x4 slice. The times are simulated.
32 devices in a mesh: band: 4 (over y, core), grid: 8 (over z, x).
Axes of the slice: x: 2, y: 2, z: 4, core: 2. Of those that a mesh axis runs over, the one named last changes fastest.
Arguments:
- orbitals: float32 [32, 8, 6, 128], P(('band', 'grid')), may hold values from -6 to 6
- region: int32 [8, 6, 128], replicated, may hold values from 0 to 15
- potential_table: float32 [16], replicated, may hold values from -3 to 3
- counts: int32 [4], replicated, may hold values from 2 to 8, as said below
- ritz: float32 [32, 32], P('band', 'grid'), may hold values from -1.5 to 1.5
Outputs:
- rotated: float32 [32, 6144], P('band', 'grid')
Inputs may be any that keep to these rules, and one draw needn't show every extreme that they name: Some band block is full (counts equal to 8) in every draw.
All inputs are finite; a program needn't handle non-finite values.
Results may differ from a plain program's by a relative error of at most 0.000071.
Values sent between devices are 32-bit elements; how exact they have to be, the bound alone decides.
No kernel may reach another device: no remote copies, remote signals or barrier semaphores. Data moves between devices by JAX's collectives and lax.ppermute only.
A program may use at most 64 MiB of HBM per device.

v0:
```python
import jax
import jax.numpy as jnp
from jax import lax
from jax.sharding import PartitionSpec as P

DEGREE = 4


COEFFICIENTS = (
    -5369.0 / 1800.0,
    12.0 / 7.0,
    -15.0 / 56.0,
    10.0 / 189.0,
    -1.0 / 112.0,
    2.0 / 1925.0,
    -1.0 / 16632.0,
)
SPACING = 0.5
LOWER = 6.0
UPPER = 46.0


def laplace(field):
    summed = 3.0 * COEFFICIENTS[0] * field
    for offset in range(1, 7):
        for axis in (-3, -2, -1):
            summed = summed + COEFFICIENTS[offset] * (
                jnp.roll(field, offset, axis) + jnp.roll(field, -offset, axis)
            )
    return summed / (SPACING * SPACING)


def apply_hamiltonian(field, potential):
    return -0.5 * laplace(field) + potential * field


def chebyshev(start_field, potential):
    half_width = (UPPER - LOWER) / 2.0
    centre = (UPPER + LOWER) / 2.0
    previous = start_field
    current = (apply_hamiltonian(start_field, potential) - centre * start_field) / half_width
    for step in range(DEGREE - 1):
        following = (
            2.0 / half_width * (apply_hamiltonian(current, potential) - centre * current) - previous
        )
        previous = current
        current = following
    return current


def shards(orbitals, region, potential_table, counts, ritz):
    orb_local = orbitals.shape[0]
    band_pos = lax.axis_index("band")
    grid_pos = lax.axis_index("grid")
    own_count = jnp.sum(
        jnp.where(jnp.arange(counts.shape[0], dtype=jnp.int32) == band_pos, counts, 0)
    )
    slots = grid_pos * orb_local + jnp.arange(orb_local, dtype=jnp.int32)
    live = (slots < own_count).astype(jnp.float32)
    masked = orbitals * live[:, None, None, None]
    region_ids = jnp.arange(potential_table.shape[0], dtype=jnp.int32)
    potential = jnp.sum(
        jnp.where(
            region[None] == region_ids[:, None, None, None],
            potential_table[:, None, None, None],
            0.0,
        ),
        axis=0,
    )
    filtered = chebyshev(masked, potential)
    cells = filtered.shape[1] * filtered.shape[2] * filtered.shape[3]
    grouped = lax.all_to_all(
        filtered.reshape(orb_local, cells), "grid", split_axis=1, concat_axis=0, tiled=True
    )
    panel = lax.all_gather(ritz, "grid", axis=1, tiled=True)
    columns = lax.all_to_all(panel, "band", split_axis=1, concat_axis=0, tiled=True)
    return lax.dot_general(
        columns,
        lax.all_gather(grouped, "band", axis=0, tiled=True),
        (((0,), (0,)), ((), ())),
        precision=lax.Precision.HIGHEST,
        preferred_element_type=jnp.float32,
    )


def solution(mesh):
    return jax.shard_map(
        shards,
        mesh=mesh,
        in_specs=(P(("band", "grid"), None, None, None), P(), P(), P(), P("band", "grid")),
        out_specs=P("band", "grid"),
        check_vma=False,
    )
```

profile of v0, /device:TPU:0, one launch (start us, length us, event | category | flops | bytes accessed | tf_op | source)
XLA Modules:
  0.0 53.9 jit_solution(5022828610553432738)
XLA Ops:
  0.0 0.7 %copy-done.4 = s32[4]{0:T(128)S(1)} copy-done((s32[4]{0:T(128)S(1)}, s32[4]{0:T(128)}, u32[]{:S(2)}) %copy-start.4) | copy-done | bytes 40
  0.7 0.6 %fusion.126 = s32[]{:T(128)} fusion(s32[4]{0:T(128)S(1)} %copy-done.4, s32[]{:T(128)S(6)} %axis_index.25), kind=kLoop, calls=%fused_computation.188 | loop fusion | flops 11 | bytes 24 | tf_op jit(solution)/shard_map/reduce_sum | solution.py:55
  1.9 0.7 %broadcast_multiply_fusion.1 = f32[1,8,6,128]{3,1,2,0:T(8,128)S(1)} fusion(f32[1,8,6,128]{3,1,2,0:T(8,128)} %param.5, f32[]{:T(128)S(6)} %convert_element_type.4), kind=kLoop, calls=%fused_computation.186 | loop fusion | flops 6144 | bytes 49156 | tf_op jit(solution)/shard_map/mul | solution.py:60
  2.7 0.1 fusion.204
  2.8 0.1 fusion.210
  3.0 0.1 fusion.215
  3.7 0.7 %copy-done.1 = s32[8,6,128]{2,0,1:T(8,128)S(1)} copy-done((s32[8,6,128]{2,0,1:T(8,128)S(1)}, s32[8,6,128]{2,0,1:T(8,128)}, u32[]{:S(2)}) %copy-start.1) | copy-done | bytes 24600
  4.4 0.1 select_reduce_fusion
  4.5 0.7 %copy-done = f32[1,8,6,128]{3,1,2,0:T(8,128)S(1)} copy-done((f32[1,8,6,128]{3,1,2,0:T(8,128)S(1)}, f32[1,8,6,128]{3,1,2,0:T(8,128)}, u32[]{:S(2)}) %copy-start) | copy-done | bytes 24600
  5.3 0.2 broadcast_multiply_fusion
  5.5 0.1 fusion.186
  6.5 0.2 fusion.115
  6.7 0.1 fusion.174
  6.9 0.1 fusion.162
  7.7 0.2 fusion.119
  9.0 0.2 fusion.124
  9.2 0.6 %copy.26 = f32[1,8,768]{2,0,1:T(1,128)} copy(f32[1,8,768]{2,1,0:T(8,128)S(1)} %fusion.124) | data formatting | bytes 49152 | tf_op jit(solution)/shard_map/all_to_all | solution.py:72
  9.8 7.3 %all-to-all-start = ((f32[1,8,768]{2,0,1:T(1,128)}), f32[1,8,768]{2,0,1:T(1,128)S(1)}, u32[]{:S(2)}, u32[]{:S(2)}) async-start(f32[1,8,768]{2,0,1:T(1,128)} %copy.26), calls=%async_computation | async-start | bytes 49152 | tf_op jit(solution)/shard_map/all_to_all | solution.py:72
  17.1 26.5 %all-gather.1 = f32[8,4,8]{2,1,0:T(4,128)S(1)} all-gather(f32[1,4,8]{2,1,0:T(4,128)S(1)} %bitcast.55), channel_id=1, replica_groups=mesh['band'=4,'grid'=8] {'grid'}, dimensions={0}, use_global_device_ids=true | all-gather | bytes 1152 | tf_op jit(solution)/shard_map/all_gather | solution.py:75
  43.7 0.1 all_to_all.29
  43.8 0.6 %copy.28 = f32[8,4,8]{2,0,1:T(8,128)} copy(f32[8,4,8]{2,1,0:T(4,128)S(1)} %all_to_all.29) | data formatting | bytes 2048 | tf_op jit(solution)/shard_map/all_to_all | solution.py:76
  44.4 3.2 %all-to-all-start.1 = ((f32[8,4,8]{2,0,1:T(8,128)}), f32[8,4,8]{2,0,1:T(8,128)S(1)}, u32[]{:S(2)}, u32[]{:S(2)}) async-start(f32[8,4,8]{2,0,1:T(8,128)} %copy.28), calls=%async_computation.1 | async-start | bytes 32768 | tf_op jit(solution)/shard_map/all_to_all | solution.py:76
  47.7 5.4 %all-gather = f32[1,32,768]{2,0,1:T(1,128)S(1)} all-gather(f32[1,8,768]{2,0,1:T(1,128)S(1)} %all-to-all-done), channel_id=2, replica_groups=mesh['band'=4,'grid'=8] {'band'}, dimensions={1}, use_global_device_ids=true | all-gather | bytes 122880 | tf_op jit(solution)/shard_map/all_gather | solution.py:79
  53.1 0.8 %convolution_bitcast_fusion = f32[8,768]{1,0:T(8,128)} fusion(f32[1,32,768]{2,0,1:T(1,128)S(1)} %all-gather, f32[8,4,8]{2,0,1:T(8,128)S(1)} %all-to-all-done.1), kind=kOutput, calls=%fused_computation | convolution fusion | flops 2359296 | bytes 123904 | tf_op jit(solution)/shard_map/dot_general | solution.py:77
  (100 shorter events, 3.5 us)
Async XLA Ops:
  0.0 0.7 %copy-start.4 = (s32[4]{0:T(128)S(1)}, s32[4]{0:T(128)}, u32[]{:S(2)}) copy-start(s32[4]{0:T(128)} %param.8) | copy-start | bytes 52
  3.7 0.7 %copy-start.1 = (s32[8,6,128]{2,0,1:T(8,128)S(1)}, s32[8,6,128]{2,0,1:T(8,128)}, u32[]{:S(2)}) copy-start(s32[8,6,128]{2,0,1:T(8,128)} %param.6) | copy-start | bytes 73732
  3.7 0.7 %copy-start.3 = (f32[16]{0:T(128)S(1)}, f32[16]{0:T(128)}, u32[]{:S(2)}) copy-start(f32[16]{0:T(128)} %param.7) | copy-start | bytes 196
  4.5 0.7 %copy-start = (f32[1,8,6,128]{3,1,2,0:T(8,128)S(1)}, f32[1,8,6,128]{3,1,2,0:T(8,128)}, u32[]{:S(2)}) copy-start(f32[1,8,6,128]{3,1,2,0:T(8,128)} %param.5) | copy-start | bytes 73732
  9.0 8.1 %copy-start.2 = (f32[8,4]{0,1:T(4,128)S(1)}, f32[8,4]{0,1:T(4,128)}, u32[]{:S(2)}) copy-start(f32[8,4]{0,1:T(4,128)} %param.9) | copy-start | bytes 388
  9.8 34.6 %all-to-all-start = ((f32[1,8,768]{2,0,1:T(1,128)}), f32[1,8,768]{2,0,1:T(1,128)S(1)}, u32[]{:S(2)}, u32[]{:S(2)}) async-start(f32[1,8,768]{2,0,1:T(1,128)} %copy.26), calls=%async_computation | async-start | bytes 49152 | tf_op jit(solution)/shard_map/all_to_all | solution.py:72
  44.4 8.7 %all-to-all-start.1 = ((f32[8,4,8]{2,0,1:T(8,128)}), f32[8,4,8]{2,0,1:T(8,128)S(1)}, u32[]{:S(2)}, u32[]{:S(2)}) async-start(f32[8,4,8]{2,0,1:T(8,128)} %copy.28), calls=%async_computation.1 | async-start | bytes 32768 | tf_op jit(solution)/shard_map/all_to_all | solution.py:76
where the time goes:
time: 54.4 us; the launch traced here: 53.9 us
  blocking collectives  31.9 us (59%)
  starting transfers between devices  10.5 us (19%)
  local copies, waits for them, and re-layouts  7.33 us (13%)
  other arithmetic  2.22 us (4%)
  between operations  1.07 us (2%)
  matrix products  0.83 us (2%)
    all_gather x1, blocking collectives, shards(): panel = lax.all_gather(ritz, 'grid', axis=1, tiled=True)  26.5 us
    all_to_all x1, starting transfers between devices, shards(): lax.all_to_all(filtered.reshape(orb_local, cells), 'grid', split_axis=1,...  7.25 us
    all_gather x1, blocking collectives, shards(): lax.all_gather(grouped, 'band', axis=0, tiled=True)  5.4 us
    slice x96, local copies, waits for them, and re-layouts, laplace(): jnp.roll(field, offset, axis) + jnp.roll(field, -offset, axis)  3.86 us
    all_to_all x1, starting transfers between devices, shards(): lax.all_to_all(panel, 'band', split_axis=1, concat_axis=0, tiled=True)  3.25 us
    unnamed x11, local copies, waits for them, and re-layouts  2.15 us
  transfers between devices with their start and end apart: 2, of which 0 were waited for; matrix products, arithmetic and copies ran while one was open for 1% of the time, Pallas kernels for 0%

commit v1 on v0

v1 whole, which is shorter than its diff:
```python
import functools

import jax
import jax.numpy as jnp
from jax import lax
from jax.experimental import pallas as pl
from jax.experimental.pallas import tpu as pltpu
from jax.sharding import PartitionSpec as P

DEGREE = 4

COEFFICIENTS = (
    -5369.0 / 1800.0,
    12.0 / 7.0,
    -15.0 / 56.0,
    10.0 / 189.0,
    -1.0 / 112.0,
    2.0 / 1925.0,
    -1.0 / 16632.0,
)
SPACING = 0.5
LOWER = 6.0
UPPER = 46.0
HALF = (UPPER - LOWER) / 2.0
CENTRE = (UPPER + LOWER) / 2.0
LANES = 128
SUBLANES = 8


def ring_weights(length):
    weights = [0.0] * length
    for offset in range(1, 7):
        weights[offset % length] += COEFFICIENTS[offset]
        weights[-offset % length] += COEFFICIENTS[offset]
    return weights


def pair_weights(length):
    weights = ring_weights(length)
    pairs = []
    for distance in range(1, length // 2 + 1):
        if weights[distance] != 0.0:
            pairs.append((sorted({distance, length - distance}), weights[distance]))
    return weights[0], pairs


def off_diagonal(field, planes, xs):
    ys = len(field)
    _, x_pairs = pair_weights(xs)
    _, y_pairs = pair_weights(ys)
    _, p_pairs = pair_weights(planes)
    results = []
    for y in range(ys):
        tile = field[y]
        total = None
        terms = []
        for shifts, weight in x_pairs:
            terms.append((weight, [pltpu.roll(tile, shift, 1) for shift in shifts]))
        for shifts, weight in p_pairs:
            terms.append((weight, [pltpu.roll(tile, shift, 0) for shift in shifts]))
        for shifts, weight in y_pairs:
            terms.append((weight, [field[(y - shift) % ys] for shift in shifts]))
        for weight, parts in terms:
            value = weight * functools.reduce(jnp.add, parts)
            total = value if total is None else total + value
        results.append(total)
    return results


def filter_kernel(nb, ng, rows, run, width, orb_ref, region_ref, ritz_ref, table_ref, counts_ref, out_ref):
    ys, planes, xs = orb_ref.shape
    band_pos = lax.axis_index("band")
    grid_pos = lax.axis_index("grid")
    live = (grid_pos < counts_ref[band_pos]).astype(jnp.float32)

    centre_weight = 3.0 * COEFFICIENTS[0] + sum(pair_weights(n)[0] for n in (planes, ys, xs))
    scale = 2.0 / HALF
    hop = -0.5 / (SPACING * SPACING) * scale
    diagonal = []
    for y in range(ys):
        region = region_ref[y]
        potential = jnp.zeros((planes, xs), jnp.float32)
        for index in range(table_ref.shape[0]):
            potential = jnp.where(region == index, table_ref[index], potential)
        diagonal.append(scale * potential + (hop * centre_weight - scale * CENTRE))

    def doubled(field):
        away = off_diagonal(field, planes, xs)
        return [diagonal[y] * field[y] + hop * away[y] for y in range(ys)]

    previous = [orb_ref[y] * live for y in range(ys)]
    current = [0.5 * value for value in doubled(previous)]
    for _ in range(DEGREE - 1):
        following = [value - before for value, before in zip(doubled(current), previous)]
        previous, current = current, following

    blocks = ys // run
    for b in range(nb):
        for y in range(ys):
            start = (b * ng + y // run) * rows + y % run
            out_ref[pl.ds(start, planes, stride=blocks * rows), :] = current[y]

    columns, panel = ritz_ref.shape
    per_row = LANES // width
    lane = lax.broadcasted_iota(jnp.int32, (1, LANES), 1)
    for row in range(-(-columns // per_row)):
        line = jnp.zeros((1, LANES), jnp.float32)
        for slot in range(min(per_row, columns - row * per_row)):
            piece = jnp.concatenate(
                [ritz_ref[pl.ds(row * per_row + slot, 1), :], jnp.zeros((1, LANES - panel), jnp.float32)], axis=1
            )
            line = line + (pltpu.roll(piece, slot * width, 1) if slot else piece)
        out_ref[pl.ds(run + row, nb * ng, stride=rows), :] = jnp.broadcast_to(line, (nb * ng, LANES))


def rotate_kernel(nb, ng, run, width, columns, got_ref, out_ref):
    wanted = out_ref.shape[0]
    panel = ng
    holders = wanted // columns
    first = lax.axis_index("band") * holders
    sublane = lax.broadcasted_iota(jnp.int32, (wanted, LANES), 0)
    lane = lax.broadcasted_iota(jnp.int32, (wanted, LANES), 1)
    own = lane // width == sublane % columns
    acc = [jnp.zeros((wanted, LANES), jnp.float32) for _ in range(run)]
    for b in range(nb):
        lines = jnp.zeros((wanted, LANES), jnp.float32)
        for k in range(holders):
            line = got_ref[b * ng + first + k, pl.ds(run, 1), :]
            lines = jnp.where(sublane // columns == k, jnp.broadcast_to(line, (wanted, LANES)), lines)
        lines = jnp.where(own, lines, 0.0)
        gathered = lines
        for slot in range(1, columns):
            gathered = gathered + pltpu.roll(lines, LANES - slot * width, 1)
        for r in range(panel):
            weight = jnp.broadcast_to(gathered[:, r : r + 1], (wanted, LANES))
            for y in range(run):
                acc[y] = acc[y] + weight * got_ref[b * ng + r, pl.ds(y, 1), :]
    for y in range(run):
        out_ref[:, pl.ds(y * LANES, LANES)] = acc[y]


def shards(nb, ng, orbitals, region, potential_table, counts, ritz):
    _, planes, ys, xs = orbitals.shape
    cells = planes * ys * xs
    panel, columns = ritz.shape
    run = cells // ng // xs
    width = 1
    while width < panel:
        width *= 2
    per_row = LANES // width
    ritz_rows = -(-columns // per_row)
    rows = -(-(run + ritz_rows) // SUBLANES) * SUBLANES
    devices = nb * ng
    vmem = pl.BlockSpec(memory_space=pltpu.VMEM)
    smem = pl.BlockSpec(memory_space=pltpu.SMEM)
    packed = pl.pallas_call(
        functools.partial(filter_kernel, nb, ng, rows, run, width),
        out_shape=jax.ShapeDtypeStruct((devices * rows, LANES), jnp.float32),
        in_specs=[vmem, vmem, vmem, smem, smem],
        out_specs=vmem,
        name="chebyshev_filter",
    )(
        jnp.transpose(orbitals[0], (1, 0, 2)),
        jnp.transpose(region, (1, 0, 2)),
        ritz.T,
        potential_table,
        counts,
    )
    got = lax.all_to_all(
        packed.reshape(devices, rows, LANES), ("band", "grid"), split_axis=0, concat_axis=0, tiled=True
    )
    if columns * width <= LANES and devices <= 64 and panel == ng:
        return pl.pallas_call(
            functools.partial(rotate_kernel, nb, ng, run, width, columns),
            out_shape=jax.ShapeDtypeStruct((panel, run * LANES), jnp.float32),
            in_specs=[vmem],
            out_specs=vmem,
            name="ritz_rotation",
        )(got)
    holders = panel // columns
    mine = lax.dynamic_slice_in_dim(
        got[:, run : run + ritz_rows].reshape(nb, ng, ritz_rows * per_row, width),
        lax.axis_index("band") * holders,
        holders,
        axis=1,
    )
    weights = jnp.transpose(mine[:, :, :columns, :panel], (0, 3, 1, 2)).reshape(devices, panel)
    return lax.dot_general(
        weights,
        got[:, :run].reshape(devices, run * LANES),
        (((0,), (0,)), ((), ())),
        precision=lax.Precision.HIGHEST,
        preferred_element_type=jnp.float32,
    )


def solution(mesh):
    return jax.shard_map(
        functools.partial(shards, mesh.shape["band"], mesh.shape["grid"]),
        mesh=mesh,
        in_specs=(P(("band", "grid"), None, None, None), P(), P(), P(), P("band", "grid")),
        out_specs=P("band", "grid"),
        check_vma=False,
    )
```

time: 54.4 us -> 19 us (0.35)
  blocking collectives: 31.9 us -> 15.1 us
  starting transfers between devices: 10.5 us -> 0 us
  local copies, waits for them, and re-layouts: 7.33 us -> 0 us
  Pallas kernels: 0 us -> 3.65 us
  other arithmetic: 2.22 us -> 0 us
  between operations: 1.07 us -> 0.01 us
  matrix products: 0.83 us -> 0 us
    all_gather x2 -> x0, blocking collectives: 31.9 us -> none  [the longest x1 26.5 us: shards(): panel = lax.all_gather(ritz, 'grid', axis=1, tiled=True)]
    all_to_all x0 -> x1, blocking collectives: none -> 15.1 us  [shards(): lax.all_to_all(packed.reshape(devices, rows, LANES), ('band', 'grid'), sp...]
    all_to_all x2 -> x0, starting transfers between devices: 10.5 us -> none  [the longest x1 7.25 us: shards(): lax.all_to_all(filtered.reshape(orb_local, cells), 'grid', split_axis=1,...]
    slice x96 -> x0, local copies, waits for them, and re-layouts: 3.86 us -> none  [laplace(): jnp.roll(field, offset, axis) + jnp.roll(field, -offset, axis)]
    pallas_call x0 -> x2, Pallas kernels: none -> 3.65 us  [the longest x1 1.93 us: shards(): pl.pallas_call(functools.partial(filter_kernel, nb, ng, rows, run, width)...]
    unnamed x11 -> x0, local copies, waits for them, and re-layouts: 2.15 us -> none
    all_to_all x3 -> x0, local copies, waits for them, and re-layouts: 1.32 us -> none  [the longest x2 0.69 us: shards(): lax.all_to_all(panel, 'band', split_axis=1, concat_axis=0, tiled=True)]
    dot_general x1 -> x0, matrix products: 0.83 us -> none  [shards(): lax.dot_general(columns, lax.all_gather(grouped, 'band', axis=0, tiled=Tr...]
  transfers between devices with their start and end apart: 2 -> 0, of which waited for: 0 -> 0; matrix products, arithmetic and copies ran while one was open for 1% -> 0% of each run, Pallas kernels for 0% -> 0%
where the time goes in v1:
time: 19 us; the launch traced here: 18.8 us
  blocking collectives  15.1 us (79%)
  Pallas kernels  3.65 us (19%)
    all_to_all x1, blocking collectives, shards(): lax.all_to_all(packed.reshape(devices, rows, LANES), ('band', 'grid'), sp...  15.1 us
    pallas_call x1, Pallas kernels, shards(): pl.pallas_call(functools.partial(filter_kernel, nb, ng, rows, run, width)...  1.93 us
    pallas_call x1, Pallas kernels, shards(): pl.pallas_call(functools.partial(rotate_kernel, nb, ng, run, width, colum...  1.71 us

profile of v1, /device:TPU:0, one launch (start us, length us, event | category | flops | bytes accessed | tf_op | source)
XLA Modules:
  0.0 18.8 jit_solution(7415200934995399978)
XLA Ops:
  0.0 1.9 %chebyshev_filter.1 = f32[256,128]{1,0:T(8,128)} custom-call(f32[6,8,128]{2,1,0:T(8,128)} %bitcast.7, s32[6,8,128]{2,1,0:T(8,128)} %bitcast.8, f32[4,8]{1,0:T(4,128)} %bitcast.9, f32[16]{0:T(128)} %table_ref.1, s32[4]{0:T(128)} %counts_ref.1), custom_call_target="tpu_custom_call" | custom-call | tf_op jit(solution)/shard_map/chebyshev_filter/pallas_call | solution.py:156
  1.9 15.1 %all_to_all.5.got_ref = f32[32,8,128]{2,1,0:T(8,128)} all-to-all(f32[32,8,128]{2,1,0:T(8,128)} %bitcast.6), channel_id=1, replica_groups=mesh['band'=4,'grid'=8] {'band','grid'}, dimensions={0} | all-to-all | bytes 262144 | tf_op jit(solution)/shard_map/all_to_all | solution.py:169
  17.1 1.7 %ritz_rotation.1 = f32[8,768]{1,0:T(8,128)} custom-call(f32[32,8,128]{2,1,0:T(8,128)} %all_to_all.5.got_ref), custom_call_target="tpu_custom_call" | custom-call | tf_op jit(solution)/shard_map/ritz_rotation/pallas_call | solution.py:173

commit v2 on v1

--- a/solution.py
+++ b/solution.py
@@ -67,7 +67,17 @@
     return results
 
 
-def filter_kernel(nb, ng, rows, run, width, orb_ref, region_ref, ritz_ref, table_ref, counts_ref, out_ref):
+def filter_kernel(nb, ng, rows, run, width, *refs):
+    sources, out_ref, held, sems = refs[:5], refs[5], refs[6:11], refs[11]
+    orb_ref, region_ref, ritz_ref, table_ref, counts_ref = held
+    copies = [
+        pltpu.make_async_copy(source, target, sems.at[index])
+        for index, (source, target) in enumerate(zip(sources, held))
+    ]
+    for copy in copies:
+        copy.start()
+    for copy in copies:
+        copy.wait()
     ys, planes, xs = orb_ref.shape
     band_pos = lax.axis_index("band")
     grid_pos = lax.axis_index("grid")
@@ -152,12 +162,22 @@
     rows = -(-(run + ritz_rows) // SUBLANES) * SUBLANES
     devices = nb * ng
     vmem = pl.BlockSpec(memory_space=pltpu.VMEM)
-    smem = pl.BlockSpec(memory_space=pltpu.SMEM)
+    hbm = pl.BlockSpec(memory_space=pltpu.HBM)
+    packed_bytes = 4 * devices * rows * LANES
     packed = pl.pallas_call(
         functools.partial(filter_kernel, nb, ng, rows, run, width),
         out_shape=jax.ShapeDtypeStruct((devices * rows, LANES), jnp.float32),
-        in_specs=[vmem, vmem, vmem, smem, smem],
+        in_specs=[hbm] * 5,
         out_specs=vmem,
+        scratch_shapes=[
+            pltpu.VMEM((ys, planes, xs), jnp.float32),
+            pltpu.VMEM((ys, planes, xs), jnp.int32),
+            pltpu.VMEM((columns, panel), jnp.float32),
+            pltpu.SMEM(potential_table.shape, jnp.float32),
+            pltpu.SMEM(counts.shape, jnp.int32),
+            pltpu.SemaphoreType.DMA((5,)),
+        ],
+        compiler_params=pltpu.CompilerParams(vmem_limit_bytes=packed_bytes + 32 * cells + 2**20),
         name="chebyshev_filter",
     )(
         jnp.transpose(orbitals[0], (1, 0, 2)),
@@ -175,6 +195,7 @@
             out_shape=jax.ShapeDtypeStruct((panel, run * LANES), jnp.float32),
             in_specs=[vmem],
             out_specs=vmem,
+            compiler_params=pltpu.CompilerParams(vmem_limit_bytes=packed_bytes + 2**20),
             name="ritz_rotation",
         )(got)
     holders = panel // columns

time: 19 us -> 19.2 us (1.011)
  local copies, waits for them, and re-layouts: 0 us -> 2.16 us
  Pallas kernels: 3.65 us -> 1.92 us
  blocking collectives: 15.1 us -> 14.8 us
    unnamed x0 -> x10, local copies, waits for them, and re-layouts: none -> 2.16 us
    pallas_call x1, Pallas kernels: 1.71 us -> 0.81 us  [shards(): pl.pallas_call(functools.partial(rotate_kernel, nb, ng, run, width, colum...]
    pallas_call x1, Pallas kernels: 1.93 us -> 1.11 us  [shards(): pl.pallas_call(functools.partial(filter_kernel, nb, ng, rows, run, width)...]
    all_to_all x1, blocking collectives: 15.1 us -> 14.8 us  [shards(): lax.all_to_all(packed.reshape(devices, rows, LANES), ('band', 'grid'), sp...]
where the time goes in v2:
time: 19.2 us; the launch traced here: 18.9 us
  blocking collectives  14.8 us (77%)
  local copies, waits for them, and re-layouts  2.16 us (11%)
  Pallas kernels  1.92 us (10%)
    all_to_all x1, blocking collectives, shards(): lax.all_to_all(packed.reshape(devices, rows, LANES), ('band', 'grid'), sp...  14.8 us
    unnamed x10, local copies, waits for them, and re-layouts  2.16 us
    pallas_call x1, Pallas kernels, shards(): pl.pallas_call(functools.partial(filter_kernel, nb, ng, rows, run, width)...  1.11 us
    pallas_call x1, Pallas kernels, shards(): pl.pallas_call(functools.partial(rotate_kernel, nb, ng, run, width, colum...  0.81 us

profile of v2, /device:TPU:0, one launch (start us, length us, event | category | flops | bytes accessed | tf_op | source)
XLA Modules:
  0.0 18.9 jit_solution(6360242898759592189)
XLA Ops:
  0.0 0.0 copy-start.2
  0.0 0.0 copy-start.3
  0.0 0.0 copy-start.4
  0.0 0.7 %copy-done.2 = f32[8,4]{0,1:T(4,128)S(1)} copy-done((f32[8,4]{0,1:T(4,128)S(1)}, f32[8,4]{0,1:T(4,128)}, u32[]{:S(2)}) %copy-start.2) | copy-done | bytes 152
  0.7 0.0 copy-done.3
  0.7 0.0 copy-done.4
  0.7 0.0 copy-start
  0.7 0.7 %copy-done = f32[1,8,6,128]{3,1,2,0:T(8,128)S(1)} copy-done((f32[1,8,6,128]{3,1,2,0:T(8,128)S(1)}, f32[1,8,6,128]{3,1,2,0:T(8,128)}, u32[]{:S(2)}) %copy-start) | copy-done | bytes 24600
  1.4 0.0 copy-start.1
  1.4 0.7 %copy-done.1 = s32[8,6,128]{2,0,1:T(8,128)S(1)} copy-done((s32[8,6,128]{2,0,1:T(8,128)S(1)}, s32[8,6,128]{2,0,1:T(8,128)}, u32[]{:S(2)}) %copy-start.1) | copy-done | bytes 24600
  2.2 1.1 %chebyshev_filter.1 = f32[256,128]{1,0:T(8,128)S(1)} custom-call(f32[6,8,128]{2,1,0:T(8,128)S(1)} %bitcast.7, s32[6,8,128]{2,1,0:T(8,128)S(1)} %bitcast.8, f32[4,8]{1,0:T(4,128)S(1)} %bitcast.9, f32[16]{0:T(128)S(1)} %copy-done.3, s32[4]{0:T(128)S(1)} %copy-done.4), custom_call_target="tpu_custom_call" | custom-call | tf_op jit(solution)/shard_map/chebyshev_filter/pallas_call | solution.py:167
  3.3 14.8 %all_to_all.5.got_ref = f32[32,8,128]{2,1,0:T(8,128)S(1)} all-to-all(f32[32,8,128]{2,1,0:T(8,128)S(1)} %bitcast.6), channel_id=1, replica_groups=mesh['band'=4,'grid'=8] {'band','grid'}, dimensions={0} | all-to-all | bytes 262144 | tf_op jit(solution)/shard_map/all_to_all | solution.py:189
  18.1 0.8 %ritz_rotation.1 = f32[8,768]{1,0:T(8,128)} custom-call(f32[32,8,128]{2,1,0:T(8,128)S(1)} %all_to_all.5.got_ref), custom_call_target="tpu_custom_call" | custom-call | tf_op jit(solution)/shard_map/ritz_rotation/pallas_call | solution.py:193
Async XLA Ops:
  0.0 0.7 %copy-start.2 = (f32[8,4]{0,1:T(4,128)S(1)}, f32[8,4]{0,1:T(4,128)}, u32[]{:S(2)}) copy-start(f32[8,4]{0,1:T(4,128)} %param.9) | copy-start | bytes 388
  0.0 0.7 %copy-start.3 = (f32[16]{0:T(128)S(1)}, f32[16]{0:T(128)}, u32[]{:S(2)}) copy-start(f32[16]{0:T(128)} %refs_3_.1) | copy-start | bytes 196
  0.0 0.7 %copy-start.4 = (s32[4]{0:T(128)S(1)}, s32[4]{0:T(128)}, u32[]{:S(2)}) copy-start(s32[4]{0:T(128)} %refs_4_.1) | copy-start | bytes 52
  0.7 0.7 %copy-start = (f32[1,8,6,128]{3,1,2,0:T(8,128)S(1)}, f32[1,8,6,128]{3,1,2,0:T(8,128)}, u32[]{:S(2)}) copy-start(f32[1,8,6,128]{3,1,2,0:T(8,128)} %param.5) | copy-start | bytes 73732
  1.4 0.7 %copy-start.1 = (s32[8,6,128]{2,0,1:T(8,128)S(1)}, s32[8,6,128]{2,0,1:T(8,128)}, u32[]{:S(2)}) copy-start(s32[8,6,128]{2,0,1:T(8,128)} %param.6) | copy-start | bytes 73732

commit v3 on v2

--- a/solution.py
+++ b/solution.py
@@ -67,8 +67,10 @@
     return results
 
 
-def filter_kernel(nb, ng, rows, run, width, *refs):
-    sources, out_ref, held, sems = refs[:5], refs[5], refs[6:11], refs[11]
+def filter_kernel(nb, ng, rows, run, width, pairwise, *refs):
+    sources, outs, held, sems = refs[:5], refs[5:-6], refs[-6:-1], refs[-1]
+    out_ref = outs[-1]
+    copies_of_tiles = 1 if pairwise else nb
     orb_ref, region_ref, ritz_ref, table_ref, counts_ref = held
     copies = [
         pltpu.make_async_copy(source, target, sems.at[index])
@@ -105,7 +107,7 @@
         previous, current = current, following
 
     blocks = ys // run
-    for b in range(nb):
+    for b in range(copies_of_tiles):
         for y in range(ys):
             start = (b * ng + y // run) * rows + y % run
             out_ref[pl.ds(start, planes, stride=blocks * rows), :] = current[y]
@@ -120,33 +122,50 @@
                 [ritz_ref[pl.ds(row * per_row + slot, 1), :], jnp.zeros((1, LANES - panel), jnp.float32)], axis=1
             )
             line = line + (pltpu.roll(piece, slot * width, 1) if slot else piece)
-        out_ref[pl.ds(run + row, nb * ng, stride=rows), :] = jnp.broadcast_to(line, (nb * ng, LANES))
-
-
-def rotate_kernel(nb, ng, run, width, columns, got_ref, out_ref):
-    wanted = out_ref.shape[0]
-    panel = ng
+        tiles = copies_of_tiles * ng
+        out_ref[pl.ds(run + row, tiles, stride=rows), :] = jnp.broadcast_to(line, (tiles, LANES))
+    if pairwise:
+        for distance, tile_ref in enumerate(outs[:-1]):
+            start = pl.multiple_of((grid_pos ^ distance) * rows, rows)
+            tile_ref[...] = out_ref[pl.ds(start, rows), :]
+
+
+def partial_kernel(nb, ng, run, width, columns, *refs):
+    tiles, outs, held_ref = refs[:ng], refs[ng:-1], refs[-1]
+    band_pos = lax.axis_index("band")
+    grid_pos = lax.axis_index("grid")
+    for distance, tile_ref in enumerate(tiles):
+        held_ref[grid_pos ^ distance] = tile_ref[...]
+    wanted = outs[0].shape[0]
     holders = wanted // columns
-    first = lax.axis_index("band") * holders
     sublane = lax.broadcasted_iota(jnp.int32, (wanted, LANES), 0)
     lane = lax.broadcasted_iota(jnp.int32, (wanted, LANES), 1)
     own = lane // width == sublane % columns
-    acc = [jnp.zeros((wanted, LANES), jnp.float32) for _ in range(run)]
-    for b in range(nb):
+    for distance, out_ref in enumerate(outs):
+        first = (band_pos ^ distance) * holders
         lines = jnp.zeros((wanted, LANES), jnp.float32)
         for k in range(holders):
-            line = got_ref[b * ng + first + k, pl.ds(run, 1), :]
+            line = held_ref[first + k, pl.ds(run, 1), :]
             lines = jnp.where(sublane // columns == k, jnp.broadcast_to(line, (wanted, LANES)), lines)
         lines = jnp.where(own, lines, 0.0)
         gathered = lines
         for slot in range(1, columns):
             gathered = gathered + pltpu.roll(lines, LANES - slot * width, 1)
-        for r in range(panel):
+        acc = [jnp.zeros((wanted, LANES), jnp.float32) for _ in range(run)]
+        for r in range(ng):
             weight = jnp.broadcast_to(gathered[:, r : r + 1], (wanted, LANES))
             for y in range(run):
-                acc[y] = acc[y] + weight * got_ref[b * ng + r, pl.ds(y, 1), :]
-    for y in range(run):
-        out_ref[:, pl.ds(y * LANES, LANES)] = acc[y]
+                acc[y] = acc[y] + weight * held_ref[r, pl.ds(y, 1), :]
+        for y in range(run):
+            out_ref[:, pl.ds(y * LANES, LANES)] = acc[y]
+
+
+def sum_kernel(*refs):
+    refs[-1][...] = functools.reduce(jnp.add, [ref[...] for ref in refs[:-1]])
+
+
+def exchange(value, axis, size, distance):
+    return lax.ppermute(value, axis, [(place, place ^ distance) for place in range(size)])
 
 
 def shards(nb, ng, orbitals, region, potential_table, counts, ritz):
@@ -163,13 +182,26 @@
     devices = nb * ng
     vmem = pl.BlockSpec(memory_space=pltpu.VMEM)
     hbm = pl.BlockSpec(memory_space=pltpu.HBM)
+    pairwise = (
+        columns * width <= LANES and panel == ng and run + 1 <= rows == SUBLANES
+        and ng & (ng - 1) == 0 and nb & (nb - 1) == 0 and devices <= 64
+    )
+    inputs = [
+        pltpu.with_memory_space_constraint(value, pltpu.HBM)
+        for value in (
+            jnp.transpose(orbitals[0], (1, 0, 2)), jnp.transpose(region, (1, 0, 2)), ritz.T, potential_table, counts
+        )
+    ]
     packed_bytes = 4 * devices * rows * LANES
-    packed = pl.pallas_call(
-        functools.partial(filter_kernel, nb, ng, rows, run, width),
-        out_shape=jax.ShapeDtypeStruct((devices * rows, LANES), jnp.float32),
+    packed = jax.ShapeDtypeStruct((devices * rows, LANES), jnp.float32)
+    tile = jax.ShapeDtypeStruct((rows, LANES), jnp.float32)
+    filtered = pl.pallas_call(
+        functools.partial(filter_kernel, nb, ng, rows, run, width, pairwise),
+        out_shape=[tile] * ng if pairwise else [packed],
         in_specs=[hbm] * 5,
-        out_specs=vmem,
-        scratch_shapes=[
+        out_specs=[vmem] * (ng if pairwise else 1),
+        scratch_shapes=[pltpu.VMEM((ng * rows, LANES), jnp.float32)] * int(pairwise)
+        + [
             pltpu.VMEM((ys, planes, xs), jnp.float32),
             pltpu.VMEM((ys, planes, xs), jnp.int32),
             pltpu.VMEM((columns, panel), jnp.float32),
@@ -179,25 +211,31 @@
         ],
         compiler_params=pltpu.CompilerParams(vmem_limit_bytes=packed_bytes + 32 * cells + 2**20),
         name="chebyshev_filter",
-    )(
-        jnp.transpose(orbitals[0], (1, 0, 2)),
-        jnp.transpose(region, (1, 0, 2)),
-        ritz.T,
-        potential_table,
-        counts,
-    )
+    )(*inputs)
+    if pairwise:
+        tiles = [filtered[0]] + [exchange(filtered[d], "grid", ng, d) for d in range(1, ng)]
+        sums = pl.pallas_call(
+            functools.partial(partial_kernel, nb, ng, run, width, columns),
+            out_shape=[jax.ShapeDtypeStruct((panel, run * LANES), jnp.float32)] * nb,
+            in_specs=[vmem] * ng,
+            out_specs=[vmem] * nb,
+            scratch_shapes=[pltpu.VMEM((ng, rows, LANES), jnp.float32)],
+            compiler_params=pltpu.CompilerParams(vmem_limit_bytes=packed_bytes + 2**20),
+            name="ritz_partial_sums",
+        )(*tiles)
+        terms = [sums[0]] + [exchange(sums[d], "band", nb, d) for d in range(1, nb)]
+        return pl.pallas_call(
+            sum_kernel,
+            out_shape=jax.ShapeDtypeStruct((panel, run * LANES), jnp.float32),
+            in_specs=[vmem] * nb,
+            out_specs=vmem,
+            compiler_params=pltpu.CompilerParams(vmem_limit_bytes=packed_bytes + 2**20),
+            name="band_sum",
+        )(*terms)
+    packed = filtered[0]
     got = lax.all_to_all(
         packed.reshape(devices, rows, LANES), ("band", "grid"), split_axis=0, concat_axis=0, tiled=True
     )
-    if columns * width <= LANES and devices <= 64 and panel == ng:
-        return pl.pallas_call(
-            functools.partial(rotate_kernel, nb, ng, run, width, columns),
-            out_shape=jax.ShapeDtypeStruct((panel, run * LANES), jnp.float32),
-            in_specs=[vmem],
-            out_specs=vmem,
-            compiler_params=pltpu.CompilerParams(vmem_limit_bytes=packed_bytes + 2**20),
-            name="ritz_rotation",
-        )(got)
     holders = panel // columns
     mine = lax.dynamic_slice_in_dim(
         got[:, run : run + ritz_rows].reshape(nb, ng, ritz_rows * per_row, width),

time: 19.2 us -> 26 us (1.35)
  blocking collectives: 14.8 us -> 0 us
  starting transfers between devices: 0 us -> 14.4 us
  waiting for transfers between devices: 0 us -> 9.24 us
  local copies, waits for them, and re-layouts: 2.16 us -> 0 us
    all_to_all x1 -> x0, blocking collectives: 14.8 us -> none  [shards(): lax.all_to_all(packed.reshape(devices, rows, LANES), ('band', 'grid'), sp...]
    ppermute x0 -> x10, starting transfers between devices: none -> 14.4 us  [exchange(): lax.ppermute(value, axis, [(place, place ^ distance) for place in range(s...]
    ppermute x0 -> x10, waiting for transfers between devices: none -> 9.24 us  [exchange(): lax.ppermute(value, axis, [(place, place ^ distance) for place in range(s...]
    unnamed x10 -> x0, local copies, waits for them, and re-layouts: 2.16 us -> none
    pallas_call x2 -> x3, Pallas kernels: 1.92 us -> 2.17 us  [the longest x1 1.35 us: shards(): pl.pallas_call(functools.partial(filter_kernel, nb, ng, rows, run, width,...]
  transfers between devices with their start and end apart: 0 -> 10, of which waited for: 0 -> 5; matrix products, arithmetic and copies ran while one was open for 0% -> 0% of each run, Pallas kernels for 0% -> 0%
where the time goes in v3:
time: 26 us; the launch traced here: 25.9 us
  starting transfers between devices  14.4 us (55%)
  waiting for transfers between devices  9.24 us (36%)
  Pallas kernels  2.17 us (8%)
    ppermute x10, starting transfers between devices, exchange(): lax.ppermute(value, axis, [(place, place ^ distance) for place in range(s...  14.4 us
    ppermute x10, waiting for transfers between devices, exchange(): lax.ppermute(value, axis, [(place, place ^ distance) for place in range(s...  9.24 us
    pallas_call x1, Pallas kernels, shards(): pl.pallas_call(functools.partial(filter_kernel, nb, ng, rows, run, width,...  1.35 us
    pallas_call x1, Pallas kernels, shards(): pl.pallas_call(sum_kernel, out_shape=jax.ShapeDtypeStruct((panel, run * L...  0.62 us
  transfers between devices with their start and end apart: 10, of which 5 were waited for; matrix products, arithmetic and copies ran while one was open for 0% of the time, Pallas kernels for 0%

profile of v3, /device:TPU:0, one launch (start us, length us, event | category | flops | bytes accessed | tf_op | source)
XLA Modules:
  0.0 25.9 jit_solution(15657999379185826047)
XLA Ops:
  0.0 1.3 %chebyshev_filter.1 = (f32[8,128]{1,0:T(8,128)S(1)}, f32[8,128]{1,0:T(8,128)S(1)}, f32[8,128]{1,0:T(8,128)S(1)}, f32[8,128]{1,0:T(8,128)S(1)}, f32[8,128]{1,0:T(...) custom-call(f32[6,8,128]{2,1,0:T(8,128)} %bitcast.5, s32[6,8,128]{2,1,0:T(8,128)} %bitcast.6, ...), custom_call_target="tpu_custom_call" | custom-call | tf_op jit(solution)/shard_map/chebyshev_filter/pallas_call | solution.py:198
  1.4 3.0 %collective-permute-start = (f32[8,128]{1,0:T(8,128)S(1)}, f32[8,128]{1,0:T(8,128)S(1)}, u32[]{:S(2)}, u32[]{:S(2)}) collective-permute-start(f32[8,128]{1,0:T(8,128)S(1)} %get-tuple-element.18), channel_id=1, source_target_pairs={{0,1},{1,0},{2,3},{3,2},{4,5},{5,4},{6,7},{7,6},{8,9},{9,8},{10,11... | collective-permute-start | bytes 12296 | tf_op jit(solution)/shard_map/ppermute | solution.py:168
  4.4 1.6 %collective-permute-start.1 = (f32[8,128]{1,0:T(8,128)S(1)}, f32[8,128]{1,0:T(8,128)S(1)}, u32[]{:S(2)}, u32[]{:S(2)}) collective-permute-start(f32[8,128]{1,0:T(8,128)S(1)} %get-tuple-element.19), channel_id=1, source_target_pairs={{0,2},{1,3},{2,0},{3,1},{4,6},{5,7},{6,4},{7,5},{8,10},{9,11},{10,... | collective-permute-start | bytes 12296 | tf_op jit(solution)/shard_map/ppermute | solution.py:168
  5.9 0.0 collective-permute-start.2
  5.9 3.0 %collective-permute-start.3 = (f32[8,128]{1,0:T(8,128)S(1)}, f32[8,128]{1,0:T(8,128)S(1)}, u32[]{:S(2)}, u32[]{:S(2)}) collective-permute-start(f32[8,128]{1,0:T(8,128)S(1)} %get-tuple-element.21), channel_id=1, source_target_pairs={{0,4},{1,5},{2,6},{3,7},{4,0},{5,1},{6,2},{7,3},{8,12},{9,13},{10,... | collective-permute-start | bytes 12296 | tf_op jit(solution)/shard_map/ppermute | solution.py:168
  8.9 1.3 %collective-permute-start.4 = (f32[8,128]{1,0:T(8,128)S(1)}, f32[8,128]{1,0:T(8,128)S(1)}, u32[]{:S(2)}, u32[]{:S(2)}) collective-permute-start(f32[8,128]{1,0:T(8,128)S(1)} %get-tuple-element.22), channel_id=1, source_target_pairs={{0,5},{1,4},{2,7},{3,6},{4,1},{5,0},{6,3},{7,2},{8,13},{9,12},{10,... | collective-permute-start | bytes 12296 | tf_op jit(solution)/shard_map/ppermute | solution.py:168
  10.2 0.0 collective-permute-done.refs_1_
  10.2 3.6 %collective-permute-start.5 = (f32[8,128]{1,0:T(8,128)S(1)}, f32[8,128]{1,0:T(8,128)S(1)}, u32[]{:S(2)}, u32[]{:S(2)}) collective-permute-start(f32[8,128]{1,0:T(8,128)S(1)} %get-tuple-element.23), channel_id=1, source_target_pairs={{0,6},{1,7},{2,4},{3,5},{4,2},{5,3},{6,0},{7,1},{8,14},{9,15},{10,... | collective-permute-start | bytes 12296 | tf_op jit(solution)/shard_map/ppermute | solution.py:168
  13.8 0.0 collective-permute-done.1.refs_2_
  13.8 0.0 collective-permute-start.6
  13.9 0.0 collective-permute-done.2.refs_3_
  13.9 0.0 collective-permute-done.3.refs_4_
  13.9 0.5 %collective-permute-done.4.refs_5_ = f32[8,128]{1,0:T(8,128)S(1)} collective-permute-done((f32[8,128]{1,0:T(8,128)S(1)}, f32[8,128]{1,0:T(8,128)S(1)}, u32[]{:S(2)}, u32[]{:S(2)}) %collective-permute-start.4) | collective-permute-done | bytes 4128 | tf_op jit(solution)/shard_map/ppermute | solution.py:168
  14.4 1.3 %collective-permute-done.5.refs_6_ = f32[8,128]{1,0:T(8,128)S(1)} collective-permute-done((f32[8,128]{1,0:T(8,128)S(1)}, f32[8,128]{1,0:T(8,128)S(1)}, u32[]{:S(2)}, u32[]{:S(2)}) %collective-permute-start.5) | collective-permute-done | bytes 4128 | tf_op jit(solution)/shard_map/ppermute | solution.py:168
  15.6 4.5 %collective-permute-done.6.refs_7_ = f32[8,128]{1,0:T(8,128)S(1)} collective-permute-done((f32[8,128]{1,0:T(8,128)S(1)}, f32[8,128]{1,0:T(8,128)S(1)}, u32[]{:S(2)}, u32[]{:S(2)}) %collective-permute-start.6) | collective-permute-done | bytes 4128 | tf_op jit(solution)/shard_map/ppermute | solution.py:168
  20.1 0.2 ritz_partial_sums.1
  20.3 0.1 collective-permute-start.7
  20.4 1.6 %collective-permute-start.8 = (f32[8,768]{1,0:T(8,128)S(1)}, f32[8,768]{1,0:T(8,128)S(1)}, u32[]{:S(2)}, u32[]{:S(2)}) collective-permute-start(f32[8,768]{1,0:T(8,128)S(1)} %get-tuple-element.27), channel_id=1, source_target_pairs={{0,16},{8,24},{16,0},{24,8},{1,17},{9,25},{17,1},{25,9},{2,18},{10... | collective-permute-start | bytes 73736 | tf_op jit(solution)/shard_map/ppermute | solution.py:168
  22.0 0.3 %collective-permute-start.9 = (f32[8,768]{1,0:T(8,128)S(1)}, f32[8,768]{1,0:T(8,128)S(1)}, u32[]{:S(2)}, u32[]{:S(2)}) collective-permute-start(f32[8,768]{1,0:T(8,128)S(1)} %get-tuple-element.28), channel_id=1, source_target_pairs={{0,24},{8,16},{16,8},{24,0},{1,25},{9,17},{17,9},{25,1},{2,26},{10... | collective-permute-start | bytes 73736 | tf_op jit(solution)/shard_map/ppermute | solution.py:168
  22.3 0.0 collective-permute-done.7.refs_1_
  22.3 2.0 %collective-permute-done.8.refs_2_ = f32[8,768]{1,0:T(8,128)S(1)} collective-permute-done((f32[8,768]{1,0:T(8,128)S(1)}, f32[8,768]{1,0:T(8,128)S(1)}, u32[]{:S(2)}, u32[]{:S(2)}) %collective-permute-start.8) | collective-permute-done | bytes 24608 | tf_op jit(solution)/shard_map/ppermute | solution.py:168
  24.3 0.9 %collective-permute-done.9.refs_3_ = f32[8,768]{1,0:T(8,128)S(1)} collective-permute-done((f32[8,768]{1,0:T(8,128)S(1)}, f32[8,768]{1,0:T(8,128)S(1)}, u32[]{:S(2)}, u32[]{:S(2)}) %collective-permute-start.9) | collective-permute-done | bytes 24608 | tf_op jit(solution)/shard_map/ppermute | solution.py:168
  25.3 0.6 %band_sum.1 = f32[8,768]{1,0:T(8,128)} custom-call(f32[8,768]{1,0:T(8,128)S(1)} %get-tuple-element.25.refs_0_, f32[8,768]{1,0:T(8,128)S(1)} %collective-permute-done.7.refs_1_, f32[8,768]{1,0:T(8,128)S(1)} %collective-permute-done.8.refs_2_, f32[8,768]{1,0:T(8,128)S(1)} %collective-permute-done.9.refs_3_), custom_call_target="tpu_custom_call" | custom-call | tf_op jit(solution)/shard_map/band_sum/pallas_call | solution.py:227
Async XLA Ops:
  1.4 8.9 %collective-permute-start = (f32[8,128]{1,0:T(8,128)S(1)}, f32[8,128]{1,0:T(8,128)S(1)}, u32[]{:S(2)}, u32[]{:S(2)}) collective-permute-start(f32[8,128]{1,0:T(8,128)S(1)} %get-tuple-element.18), channel_id=1, source_target_pairs={{0,1},{1,0},{2,3},{3,2},{4,5},{5,4},{6,7},{7,6},{8,9},{9,8},{10,11... | collective-permute-start | bytes 12296 | tf_op jit(solution)/shard_map/ppermute | solution.py:168
  4.4 9.5 %collective-permute-start.1 = (f32[8,128]{1,0:T(8,128)S(1)}, f32[8,128]{1,0:T(8,128)S(1)}, u32[]{:S(2)}, u32[]{:S(2)}) collective-permute-start(f32[8,128]{1,0:T(8,128)S(1)} %get-tuple-element.19), channel_id=1, source_target_pairs={{0,2},{1,3},{2,0},{3,1},{4,6},{5,7},{6,4},{7,5},{8,10},{9,11},{10,... | collective-permute-start | bytes 12296 | tf_op jit(solution)/shard_map/ppermute | solution.py:168
  5.9 7.9 %collective-permute-start.2 = (f32[8,128]{1,0:T(8,128)S(1)}, f32[8,128]{1,0:T(8,128)S(1)}, u32[]{:S(2)}, u32[]{:S(2)}) collective-permute-start(f32[8,128]{1,0:T(8,128)S(1)} %get-tuple-element.20), channel_id=1, source_target_pairs={{0,3},{1,2},{2,1},{3,0},{4,7},{5,6},{6,5},{7,4},{8,11},{9,10},{10,... | collective-permute-start | bytes 12296 | tf_op jit(solution)/shard_map/ppermute | solution.py:168
  5.9 7.9 %collective-permute-start.3 = (f32[8,128]{1,0:T(8,128)S(1)}, f32[8,128]{1,0:T(8,128)S(1)}, u32[]{:S(2)}, u32[]{:S(2)}) collective-permute-start(f32[8,128]{1,0:T(8,128)S(1)} %get-tuple-element.21), channel_id=1, source_target_pairs={{0,4},{1,5},{2,6},{3,7},{4,0},{5,1},{6,2},{7,3},{8,12},{9,13},{10,... | collective-permute-start | bytes 12296 | tf_op jit(solution)/shard_map/ppermute | solution.py:168
  8.9 5.4 %collective-permute-start.4 = (f32[8,128]{1,0:T(8,128)S(1)}, f32[8,128]{1,0:T(8,128)S(1)}, u32[]{:S(2)}, u32[]{:S(2)}) collective-permute-start(f32[8,128]{1,0:T(8,128)S(1)} %get-tuple-element.22), channel_id=1, source_target_pairs={{0,5},{1,4},{2,7},{3,6},{4,1},{5,0},{6,3},{7,2},{8,13},{9,12},{10,... | collective-permute-start | bytes 12296 | tf_op jit(solution)/shard_map/ppermute | solution.py:168
  10.2 5.4 %collective-permute-start.5 = (f32[8,128]{1,0:T(8,128)S(1)}, f32[8,128]{1,0:T(8,128)S(1)}, u32[]{:S(2)}, u32[]{:S(2)}) collective-permute-start(f32[8,128]{1,0:T(8,128)S(1)} %get-tuple-element.23), channel_id=1, source_target_pairs={{0,6},{1,7},{2,4},{3,5},{4,2},{5,3},{6,0},{7,1},{8,14},{9,15},{10,... | collective-permute-start | bytes 12296 | tf_op jit(solution)/shard_map/ppermute | solution.py:168
  13.8 6.3 %collective-permute-start.6 = (f32[8,128]{1,0:T(8,128)S(1)}, f32[8,128]{1,0:T(8,128)S(1)}, u32[]{:S(2)}, u32[]{:S(2)}) collective-permute-start(f32[8,128]{1,0:T(8,128)S(1)} %get-tuple-element.24), channel_id=1, source_target_pairs={{0,7},{1,6},{2,5},{3,4},{4,3},{5,2},{6,1},{7,0},{8,15},{9,14},{10,... | collective-permute-start | bytes 12296 | tf_op jit(solution)/shard_map/ppermute | solution.py:168
  20.3 1.9 %collective-permute-start.7 = (f32[8,768]{1,0:T(8,128)S(1)}, f32[8,768]{1,0:T(8,128)S(1)}, u32[]{:S(2)}, u32[]{:S(2)}) collective-permute-start(f32[8,768]{1,0:T(8,128)S(1)} %get-tuple-element.26), channel_id=1, source_target_pairs={{0,8},{8,0},{16,24},{24,16},{1,9},{9,1},{17,25},{25,17},{2,10},{10... | collective-permute-start | bytes 73736 | tf_op jit(solution)/shard_map/ppermute | solution.py:168
  20.4 3.9 %collective-permute-start.8 = (f32[8,768]{1,0:T(8,128)S(1)}, f32[8,768]{1,0:T(8,128)S(1)}, u32[]{:S(2)}, u32[]{:S(2)}) collective-permute-start(f32[8,768]{1,0:T(8,128)S(1)} %get-tuple-element.27), channel_id=1, source_target_pairs={{0,16},{8,24},{16,0},{24,8},{1,17},{9,25},{17,1},{25,9},{2,18},{10... | collective-permute-start | bytes 73736 | tf_op jit(solution)/shard_map/ppermute | solution.py:168
  22.0 3.3 %collective-permute-start.9 = (f32[8,768]{1,0:T(8,128)S(1)}, f32[8,768]{1,0:T(8,128)S(1)}, u32[]{:S(2)}, u32[]{:S(2)}) collective-permute-start(f32[8,768]{1,0:T(8,128)S(1)} %get-tuple-element.28), channel_id=1, source_target_pairs={{0,24},{8,16},{16,8},{24,0},{1,25},{9,17},{17,9},{25,1},{2,26},{10... | collective-permute-start | bytes 73736 | tf_op jit(solution)/shard_map/ppermute | solution.py:168

commit v4 on v2

v4 whole, which is shorter than its diff:
```python
import functools

import jax
import jax.numpy as jnp
from jax import lax
from jax.experimental import pallas as pl
from jax.experimental.pallas import tpu as pltpu
from jax.sharding import PartitionSpec as P

DEGREE = 4

COEFFICIENTS = (
    -5369.0 / 1800.0,
    12.0 / 7.0,
    -15.0 / 56.0,
    10.0 / 189.0,
    -1.0 / 112.0,
    2.0 / 1925.0,
    -1.0 / 16632.0,
)
SPACING = 0.5
LOWER = 6.0
UPPER = 46.0
HALF = (UPPER - LOWER) / 2.0
CENTRE = (UPPER + LOWER) / 2.0
LANES = 128
SUBLANES = 8


def ring_weights(length):
    weights = [0.0] * length
    for offset in range(1, 7):
        weights[offset % length] += COEFFICIENTS[offset]
        weights[-offset % length] += COEFFICIENTS[offset]
    return weights


def pair_weights(length):
    weights = ring_weights(length)
    pairs = []
    for distance in range(1, length // 2 + 1):
        if weights[distance] != 0.0:
            pairs.append((sorted({distance, length - distance}), weights[distance]))
    return weights[0], pairs


def off_diagonal(field, planes, xs):
    ys = len(field)
    _, x_pairs = pair_weights(xs)
    _, y_pairs = pair_weights(ys)
    _, p_pairs = pair_weights(planes)
    results = []
    for y in range(ys):
        tile = field[y]
        total = None
        terms = []
        for shifts, weight in x_pairs:
            terms.append((weight, [pltpu.roll(tile, shift, 1) for shift in shifts]))
        for shifts, weight in p_pairs:
            terms.append((weight, [pltpu.roll(tile, shift, 0) for shift in shifts]))
        for shifts, weight in y_pairs:
            terms.append((weight, [field[(y - shift) % ys] for shift in shifts]))
        for weight, parts in terms:
            value = weight * functools.reduce(jnp.add, parts)
            total = value if total is None else total + value
        results.append(total)
    return results


def filter_kernel(ng, copies, rows, run, width, cores, *refs):
    sources, out_ref, held, sems = refs[:5], refs[5], refs[6:11], refs[11]
    orb_ref, region_ref, ritz_ref, table_ref, counts_ref = held
    transfers = [
        pltpu.make_async_copy(source, target, sems.at[index])
        for index, (source, target) in enumerate(zip(sources, held))
    ]
    for transfer in transfers:
        transfer.start()
    for transfer in transfers:
        transfer.wait()
    ys, planes, xs = orb_ref.shape
    band_pos = lax.axis_index("row") * cores + lax.axis_index("core")
    live = (lax.axis_index("grid") < counts_ref[band_pos]).astype(jnp.float32)

    centre_weight = 3.0 * COEFFICIENTS[0] + sum(pair_weights(n)[0] for n in (planes, ys, xs))
    scale = 2.0 / HALF
    hop = -0.5 / (SPACING * SPACING) * scale
    diagonal = []
    for y in range(ys):
        region = region_ref[y]
        potential = jnp.zeros((planes, xs), jnp.float32)
        for index in range(table_ref.shape[0]):
            potential = jnp.where(region == index, table_ref[index], potential)
        diagonal.append(scale * potential + (hop * centre_weight - scale * CENTRE))

    def doubled(field):
        away = off_diagonal(field, planes, xs)
        return [diagonal[y] * field[y] + hop * away[y] for y in range(ys)]

    previous = [orb_ref[y] * live for y in range(ys)]
    current = [0.5 * value for value in doubled(previous)]
    for _ in range(DEGREE - 1):
        following = [value - before for value, before in zip(doubled(current), previous)]
        previous, current = current, following

    blocks = ys // run
    for copy in range(copies):
        for y in range(ys):
            start = (copy * ng + y // run) * rows + y % run
            out_ref[pl.ds(start, planes, stride=blocks * rows), :] = current[y]

    columns, panel = ritz_ref.shape
    per_row = LANES // width
    tiles = copies * ng
    for row in range(-(-columns // per_row)):
        line = jnp.zeros((1, LANES), jnp.float32)
        for slot in range(min(per_row, columns - row * per_row)):
            piece = jnp.concatenate(
                [ritz_ref[pl.ds(row * per_row + slot, 1), :], jnp.zeros((1, LANES - panel), jnp.float32)], axis=1
            )
            line = line + (pltpu.roll(piece, slot * width, 1) if slot else piece)
        out_ref[pl.ds(run + row, tiles, stride=rows), :] = jnp.broadcast_to(line, (tiles, LANES))


def partial_kernel(nrow, ng, run, width, columns, cores, got_ref, *outs):
    wanted = outs[0].shape[0]
    holders = wanted // columns
    sublane = lax.broadcasted_iota(jnp.int32, (wanted, LANES), 0)
    lane = lax.broadcasted_iota(jnp.int32, (wanted, LANES), 1)
    own = lane // width == sublane % columns
    weights = []
    for distance in range(cores):
        block = lax.axis_index("row") * cores + lax.rem(lax.axis_index("core") + distance, cores)
        gathered = []
        for row in range(nrow):
            lines = jnp.zeros((wanted, LANES), jnp.float32)
            for k in range(holders):
                line = got_ref[row * ng + block * holders + k, pl.ds(run, 1), :]
                lines = jnp.where(sublane // columns == k, jnp.broadcast_to(line, (wanted, LANES)), lines)
            lines = jnp.where(own, lines, 0.0)
            total = lines
            for slot in range(1, columns):
                total = total + pltpu.roll(lines, LANES - slot * width, 1)
            gathered.append(total)
        weights.append(gathered)
    for distance, out_ref in enumerate(outs):
        acc = [jnp.zeros((wanted, LANES), jnp.float32) for _ in range(run)]
        for row in range(nrow):
            for r in range(ng):
                weight = jnp.broadcast_to(weights[distance][row][:, r : r + 1], (wanted, LANES))
                for y in range(run):
                    acc[y] = acc[y] + weight * got_ref[row * ng + r, pl.ds(y, 1), :]
        for y in range(run):
            out_ref[:, pl.ds(y * LANES, LANES)] = acc[y]


def sum_kernel(*refs):
    refs[-1][...] = functools.reduce(jnp.add, [ref[...] for ref in refs[:-1]])


def shards(nrow, cores, ng, orbitals, region, potential_table, counts, ritz):
    _, planes, ys, xs = orbitals.shape
    cells = planes * ys * xs
    panel, columns = ritz.shape
    run = cells // ng // xs
    width = 1
    while width < panel:
        width *= 2
    per_row = LANES // width
    ritz_rows = -(-columns // per_row)
    rows = -(-(run + ritz_rows) // SUBLANES) * SUBLANES
    tiles = nrow * ng
    vmem = pl.BlockSpec(memory_space=pltpu.VMEM)
    hbm = pl.BlockSpec(memory_space=pltpu.HBM)
    inputs = [
        pltpu.with_memory_space_constraint(value, pltpu.HBM)
        for value in (
            jnp.transpose(orbitals[0], (1, 0, 2)), jnp.transpose(region, (1, 0, 2)), ritz.T, potential_table, counts
        )
    ]
    packed_bytes = 4 * tiles * rows * LANES
    packed = pl.pallas_call(
        functools.partial(filter_kernel, ng, nrow, rows, run, width, cores),
        out_shape=jax.ShapeDtypeStruct((tiles * rows, LANES), jnp.float32),
        in_specs=[hbm] * 5,
        out_specs=vmem,
        scratch_shapes=[
            pltpu.VMEM((ys, planes, xs), jnp.float32),
            pltpu.VMEM((ys, planes, xs), jnp.int32),
            pltpu.VMEM((columns, panel), jnp.float32),
            pltpu.SMEM(potential_table.shape, jnp.float32),
            pltpu.SMEM(counts.shape, jnp.int32),
            pltpu.SemaphoreType.DMA((5,)),
        ],
        compiler_params=pltpu.CompilerParams(vmem_limit_bytes=packed_bytes + 32 * cells + 2**20),
        name="chebyshev_filter",
    )(*inputs)
    got = lax.all_to_all(
        packed.reshape(tiles, rows, LANES), ("row", "grid"), split_axis=0, concat_axis=0, tiled=True
    )
    sum_shape = jax.ShapeDtypeStruct((panel, run * LANES), jnp.float32)
    if columns * width <= LANES and tiles <= 64 and panel == ng and panel <= 16:
        sums = pl.pallas_call(
            functools.partial(partial_kernel, nrow, ng, run, width, columns, cores),
            out_shape=[sum_shape] * cores,
            in_specs=[vmem],
            out_specs=[vmem] * cores,
            compiler_params=pltpu.CompilerParams(vmem_limit_bytes=packed_bytes + 2**20),
            name="ritz_partial_sums",
        )(got)
    else:
        holders = panel // columns
        by_source = got.reshape(nrow, ng, rows, LANES)
        fields = by_source[:, :, :run].reshape(tiles, run * LANES)
        blocks = by_source[:, :, run : run + ritz_rows].reshape(nrow, ng, ritz_rows * per_row, width)
        sums = []
        for distance in range(cores):
            block = lax.axis_index("row") * cores + lax.rem(lax.axis_index("core") + distance, cores)
            mine = lax.dynamic_slice_in_dim(blocks, block * holders, holders, axis=1)
            weights = jnp.transpose(mine[:, :, :columns, :panel], (0, 3, 1, 2)).reshape(tiles, panel)
            sums.append(
                lax.dot_general(
                    weights,
                    fields,
                    (((0,), (0,)), ((), ())),
                    precision=lax.Precision.HIGHEST,
                    preferred_element_type=jnp.float32,
                )
            )
    terms = [sums[0]]
    for distance in range(1, cores):
        pairs = [(core, (core + distance) % cores) for core in range(cores)]
        terms.append(lax.ppermute(sums[distance], "core", pairs))
    return pl.pallas_call(
        sum_kernel,
        out_shape=sum_shape,
        in_specs=[vmem] * cores,
        out_specs=vmem,
        compiler_params=pltpu.CompilerParams(vmem_limit_bytes=4 * (cores + 1) * panel * run * LANES + 2**20),
        name="core_sum",
    )(*terms)


def solution(mesh):
    bands, ng = mesh.shape["band"], mesh.shape["grid"]
    cores = 2 if bands % 2 == 0 else 1
    nrow = bands // cores
    split = jax.sharding.Mesh(mesh.devices.reshape(nrow, cores, ng), ("row", "core", "grid"))
    return jax.shard_map(
        functools.partial(shards, nrow, cores, ng),
        mesh=split,
        in_specs=(P(("row", "core", "grid"), None, None, None), P(), P(), P(), P(("row", "core"), "grid")),
        out_specs=P(("row", "core"), "grid"),
        check_vma=False,
    )
```

time: 19.2 us -> 19.3 us (level)
  local copies, waits for them, and re-layouts: 2.16 us -> 0 us
  waiting for transfers between devices: 0 us -> 1.18 us
  blocking collectives: 14.8 us -> 15.6 us
  Pallas kernels: 1.92 us -> 2.15 us
    unnamed x10 -> x0, local copies, waits for them, and re-layouts: 2.16 us -> none
    ppermute x0 -> x1, waiting for transfers between devices: none -> 1.18 us  [shards(): terms.append(lax.ppermute(sums[distance], 'core', pairs))]
    all_to_all x1, blocking collectives: 14.8 us -> 15.6 us  [shards(): lax.all_to_all(packed.reshape(tiles, rows, LANES), ('row', 'grid'), split...]
    pallas_call x2 -> x3, Pallas kernels: 1.92 us -> 2.15 us  [the longest x1 1.33 us: shards(): pl.pallas_call(functools.partial(filter_kernel, ng, nrow, rows, run, widt...]
  transfers between devices with their start and end apart: 0 -> 1, of which waited for: 0 -> 1; matrix products, arithmetic and copies ran while one was open for 0% -> 0% of each run, Pallas kernels for 0% -> 0%
where the time goes in v4:
time: 19.3 us; the launch traced here: 19.1 us
  blocking collectives  15.6 us (81%)
  Pallas kernels  2.15 us (11%)
  waiting for transfers between devices  1.18 us (6%)
    all_to_all x1, blocking collectives, shards(): lax.all_to_all(packed.reshape(tiles, rows, LANES), ('row', 'grid'), split...  15.6 us
    pallas_call x1, Pallas kernels, shards(): pl.pallas_call(functools.partial(filter_kernel, ng, nrow, rows, run, widt...  1.33 us
    ppermute x1, waiting for transfers between devices, shards(): terms.append(lax.ppermute(sums[distance], 'core', pairs))  1.18 us
    pallas_call x1, Pallas kernels, shards(): pl.pallas_call(sum_kernel, out_shape=sum_shape, in_specs=[vmem] * cores,...  0.61 us
  transfers between devices with their start and end apart: 1, of which 1 were waited for; matrix products, arithmetic and copies ran while one was open for 0% of the time, Pallas kernels for 0%

profile of v4, /device:TPU:0, one launch (start us, length us, event | category | flops | bytes accessed | tf_op | source)
XLA Modules:
  0.0 19.1 jit_solution(7587438665781024580)
XLA Ops:
  0.0 1.3 %chebyshev_filter.1 = f32[128,128]{1,0:T(8,128)S(1)} custom-call(f32[6,8,128]{2,1,0:T(8,128)} %bitcast.7, s32[6,8,128]{2,1,0:T(8,128)} %bitcast.8, f32[4,8]{1,0:T(4,128)} %bitcast.9, f32[16]{0:T(128)} %refs_3_.1, s32[4]{0:T(128)} %refs_4_.1), custom_call_target="tpu_custom_call" | custom-call | tf_op jit(solution)/shard_map/chebyshev_filter/pallas_call | solution.py:182
  1.3 15.6 %all_to_all.5.got_ref = f32[16,8,128]{2,1,0:T(8,128)S(1)} all-to-all(f32[16,8,128]{2,1,0:T(8,128)S(1)} %bitcast.6), channel_id=1, replica_groups=mesh['row'=2,'core'=2,'grid'=8] {'row','grid'}, dimensions={0} | all-to-all | bytes 131072 | tf_op jit(solution)/shard_map/all_to_all | solution.py:198
  17.0 0.2 %ritz_partial_sums.1 = (f32[8,768]{1,0:T(8,128)S(1)}, f32[8,768]{1,0:T(8,128)S(1)}) custom-call(f32[16,8,128]{2,1,0:T(8,128)S(1)} %all_to_all.5.got_ref), custom_call_target="tpu_custom_call" | custom-call | tf_op jit(solution)/shard_map/ritz_partial_sums/pallas_call | solution.py:203
  17.2 0.1 collective-permute-start
  17.3 1.2 %collective-permute-done.refs_1_ = f32[8,768]{1,0:T(8,128)S(1)} collective-permute-done((f32[8,768]{1,0:T(8,128)S(1)}, f32[8,768]{1,0:T(8,128)S(1)}, u32[]{:S(2)}, u32[]{:S(2)}) %collective-permute-start) | collective-permute-done | bytes 24608 | tf_op jit(solution)/shard_map/ppermute | solution.py:233
  18.5 0.6 %core_sum.1 = f32[8,768]{1,0:T(8,128)} custom-call(f32[8,768]{1,0:T(8,128)S(1)} %get-tuple-element.7.refs_0_, f32[8,768]{1,0:T(8,128)S(1)} %collective-permute-done.refs_1_), custom_call_target="tpu_custom_call" | custom-call | tf_op jit(solution)/shard_map/core_sum/pallas_call | solution.py:234
Async XLA Ops:
  17.2 1.3 %collective-permute-start = (f32[8,768]{1,0:T(8,128)S(1)}, f32[8,768]{1,0:T(8,128)S(1)}, u32[]{:S(2)}, u32[]{:S(2)}) collective-permute-start(f32[8,768]{1,0:T(8,128)S(1)} %get-tuple-element.8), channel_id=1, source_target_pairs={{0,8},{8,0},{1,9},{9,1},{2,10},{10,2},{3,11},{11,3},{4,12},{12,4},... | collective-permute-start | bytes 73736 | tf_op jit(solution)/shard_map/ppermute | solution.py:233

commit v5 on v2

--- a/solution.py
+++ b/solution.py
@@ -67,21 +67,20 @@
     return results
 
 
-def filter_kernel(nb, ng, rows, run, width, *refs):
+def filter_kernel(ng, copies, rows, run, width, *refs):
     sources, out_ref, held, sems = refs[:5], refs[5], refs[6:11], refs[11]
     orb_ref, region_ref, ritz_ref, table_ref, counts_ref = held
-    copies = [
+    transfers = [
         pltpu.make_async_copy(source, target, sems.at[index])
         for index, (source, target) in enumerate(zip(sources, held))
     ]
-    for copy in copies:
-        copy.start()
-    for copy in copies:
-        copy.wait()
+    for transfer in transfers:
+        transfer.start()
+    for transfer in transfers:
+        transfer.wait()
     ys, planes, xs = orb_ref.shape
     band_pos = lax.axis_index("band")
-    grid_pos = lax.axis_index("grid")
-    live = (grid_pos < counts_ref[band_pos]).astype(jnp.float32)
+    live = (lax.axis_index("grid") < counts_ref[band_pos]).astype(jnp.float32)
 
     centre_weight = 3.0 * COEFFICIENTS[0] + sum(pair_weights(n)[0] for n in (planes, ys, xs))
     scale = 2.0 / HALF
@@ -105,14 +104,14 @@
         previous, current = current, following
 
     blocks = ys // run
-    for b in range(nb):
+    for copy in range(copies):
         for y in range(ys):
-            start = (b * ng + y // run) * rows + y % run
+            start = (copy * ng + y // run) * rows + y % run
             out_ref[pl.ds(start, planes, stride=blocks * rows), :] = current[y]
 
     columns, panel = ritz_ref.shape
     per_row = LANES // width
-    lane = lax.broadcasted_iota(jnp.int32, (1, LANES), 1)
+    tiles = copies * ng
     for row in range(-(-columns // per_row)):
         line = jnp.zeros((1, LANES), jnp.float32)
         for slot in range(min(per_row, columns - row * per_row)):
@@ -120,28 +119,31 @@
                 [ritz_ref[pl.ds(row * per_row + slot, 1), :], jnp.zeros((1, LANES - panel), jnp.float32)], axis=1
             )
             line = line + (pltpu.roll(piece, slot * width, 1) if slot else piece)
-        out_ref[pl.ds(run + row, nb * ng, stride=rows), :] = jnp.broadcast_to(line, (nb * ng, LANES))
-
-
-def rotate_kernel(nb, ng, run, width, columns, got_ref, out_ref):
+        out_ref[pl.ds(run + row, tiles, stride=rows), :] = jnp.broadcast_to(line, (tiles, LANES))
+
+
+def start_kernel(packed_ref, out_ref):
+    out_ref[...] = jnp.zeros_like(out_ref)
+
+
+def rotate_kernel(nb, ng, run, width, columns, got_ref, start_ref, out_ref):
     wanted = out_ref.shape[0]
-    panel = ng
     holders = wanted // columns
-    first = lax.axis_index("band") * holders
     sublane = lax.broadcasted_iota(jnp.int32, (wanted, LANES), 0)
     lane = lax.broadcasted_iota(jnp.int32, (wanted, LANES), 1)
     own = lane // width == sublane % columns
-    acc = [jnp.zeros((wanted, LANES), jnp.float32) for _ in range(run)]
+    block = lax.axis_index("band")
+    acc = [start_ref[:, pl.ds(y * LANES, LANES)] for y in range(run)]
     for b in range(nb):
         lines = jnp.zeros((wanted, LANES), jnp.float32)
         for k in range(holders):
-            line = got_ref[b * ng + first + k, pl.ds(run, 1), :]
+            line = got_ref[b * ng + block * holders + k, pl.ds(run, 1), :]
             lines = jnp.where(sublane // columns == k, jnp.broadcast_to(line, (wanted, LANES)), lines)
         lines = jnp.where(own, lines, 0.0)
         gathered = lines
         for slot in range(1, columns):
             gathered = gathered + pltpu.roll(lines, LANES - slot * width, 1)
-        for r in range(panel):
+        for r in range(ng):
             weight = jnp.broadcast_to(gathered[:, r : r + 1], (wanted, LANES))
             for y in range(run):
                 acc[y] = acc[y] + weight * got_ref[b * ng + r, pl.ds(y, 1), :]
@@ -160,13 +162,19 @@
     per_row = LANES // width
     ritz_rows = -(-columns // per_row)
     rows = -(-(run + ritz_rows) // SUBLANES) * SUBLANES
-    devices = nb * ng
+    tiles = nb * ng
     vmem = pl.BlockSpec(memory_space=pltpu.VMEM)
     hbm = pl.BlockSpec(memory_space=pltpu.HBM)
-    packed_bytes = 4 * devices * rows * LANES
+    inputs = [
+        pltpu.with_memory_space_constraint(value, pltpu.HBM)
+        for value in (
+            jnp.transpose(orbitals[0], (1, 0, 2)), jnp.transpose(region, (1, 0, 2)), ritz.T, potential_table, counts
+        )
+    ]
+    packed_bytes = 4 * tiles * rows * LANES
     packed = pl.pallas_call(
-        functools.partial(filter_kernel, nb, ng, rows, run, width),
-        out_shape=jax.ShapeDtypeStruct((devices * rows, LANES), jnp.float32),
+        functools.partial(filter_kernel, ng, nb, rows, run, width),
+        out_shape=jax.ShapeDtypeStruct((tiles * rows, LANES), jnp.float32),
         in_specs=[hbm] * 5,
         out_specs=vmem,
         scratch_shapes=[
@@ -179,36 +187,36 @@
         ],
         compiler_params=pltpu.CompilerParams(vmem_limit_bytes=packed_bytes + 32 * cells + 2**20),
         name="chebyshev_filter",
-    )(
-        jnp.transpose(orbitals[0], (1, 0, 2)),
-        jnp.transpose(region, (1, 0, 2)),
-        ritz.T,
-        potential_table,
-        counts,
+    )(*inputs)
+    got = lax.all_to_all(
+        packed.reshape(tiles, rows, LANES), ("band", "grid"), split_axis=0, concat_axis=0, tiled=True
     )
-    got = lax.all_to_all(
-        packed.reshape(devices, rows, LANES), ("band", "grid"), split_axis=0, concat_axis=0, tiled=True
-    )
-    if columns * width <= LANES and devices <= 64 and panel == ng:
+    if columns * width <= LANES and tiles <= 64 and panel == ng and panel <= 16:
+        sum_shape = jax.ShapeDtypeStruct((panel, run * LANES), jnp.float32)
+        limit = pltpu.CompilerParams(vmem_limit_bytes=packed_bytes + 2**20)
+        start = pl.pallas_call(
+            start_kernel,
+            out_shape=sum_shape,
+            in_specs=[pl.BlockSpec(memory_space=pl.ANY)],
+            out_specs=vmem,
+            compiler_params=limit,
+            name="sums_start",
+        )(packed)
         return pl.pallas_call(
             functools.partial(rotate_kernel, nb, ng, run, width, columns),
-            out_shape=jax.ShapeDtypeStruct((panel, run * LANES), jnp.float32),
-            in_specs=[vmem],
+            out_shape=sum_shape,
+            in_specs=[vmem] * 2,
             out_specs=vmem,
-            compiler_params=pltpu.CompilerParams(vmem_limit_bytes=packed_bytes + 2**20),
+            compiler_params=limit,
             name="ritz_rotation",
-        )(got)
+        )(got, start)
     holders = panel // columns
-    mine = lax.dynamic_slice_in_dim(
-        got[:, run : run + ritz_rows].reshape(nb, ng, ritz_rows * per_row, width),
-        lax.axis_index("band") * holders,
-        holders,
-        axis=1,
-    )
-    weights = jnp.transpose(mine[:, :, :columns, :panel], (0, 3, 1, 2)).reshape(devices, panel)
+    by_source = got.reshape(nb, ng, rows, LANES)
+    blocks = by_source[:, :, run : run + ritz_rows].reshape(nb, ng, ritz_rows * per_row, width)
+    mine = lax.dynamic_slice_in_dim(blocks, lax.axis_index("band") * holders, holders, axis=1)
     return lax.dot_general(
-        weights,
-        got[:, :run].reshape(devices, run * LANES),
+        jnp.transpose(mine[:, :, :columns, :panel], (0, 3, 1, 2)).reshape(tiles, panel),
+        by_source[:, :, :run].reshape(tiles, run * LANES),
         (((0,), (0,)), ((), ())),
         precision=lax.Precision.HIGHEST,
         preferred_element_type=jnp.float32,

time: 19.2 us -> 18.1 us (0.943)
  blocking collectives: 14.8 us -> 0 us
  waiting for transfers between devices: 0 us -> 7.73 us
  starting transfers between devices: 0 us -> 7.3 us
  local copies, waits for them, and re-layouts: 2.16 us -> 0 us
  Pallas kernels: 1.92 us -> 2.78 us
    all_to_all x1 -> x0, blocking collectives: 14.8 us -> none  [shards(): lax.all_to_all(packed.reshape(devices, rows, LANES), ('band', 'grid'), sp...]
    all_to_all x0 -> x1, waiting for transfers between devices: none -> 7.73 us  [shards(): lax.all_to_all(packed.reshape(tiles, rows, LANES), ('band', 'grid'), spli...]
    all_to_all x0 -> x1, starting transfers between devices: none -> 7.3 us  [shards(): lax.all_to_all(packed.reshape(tiles, rows, LANES), ('band', 'grid'), spli...]
    unnamed x10 -> x0, local copies, waits for them, and re-layouts: 2.16 us -> none
    pallas_call x1 -> x2, Pallas kernels: 1.11 us -> 1.97 us  [the longest x1 1.97 us: shards(): pl.pallas_call(functools.partial(filter_kernel, ng, nb, rows, run, width)...]
  transfers between devices with their start and end apart: 0 -> 1, of which waited for: 0 -> 1; matrix products, arithmetic and copies ran while one was open for 0% -> 0% of each run, Pallas kernels for 0% -> 0%
where the time goes in v5:
time: 18.1 us; the launch traced here: 17.8 us
  waiting for transfers between devices  7.73 us (43%)
  starting transfers between devices  7.3 us (40%)
  Pallas kernels  2.78 us (15%)
    all_to_all x1, waiting for transfers between devices, shards(): lax.all_to_all(packed.reshape(tiles, rows, LANES), ('band', 'grid'), spli...  7.73 us
    all_to_all x1, starting transfers between devices, shards(): lax.all_to_all(packed.reshape(tiles, rows, LANES), ('band', 'grid'), spli...  7.3 us
    pallas_call x1, Pallas kernels, shards(): pl.pallas_call(functools.partial(filter_kernel, ng, nb, rows, run, width)...  1.97 us
    pallas_call x1, Pallas kernels, shards(): pl.pallas_call(functools.partial(rotate_kernel, nb, ng, run, width, colum...  0.81 us
  transfers between devices with their start and end apart: 1, of which 1 were waited for; matrix products, arithmetic and copies ran while one was open for 0% of the time, Pallas kernels for 0%

profile of v5, /device:TPU:0, one launch (start us, length us, event | category | flops | bytes accessed | tf_op | source)
XLA Modules:
  0.0 17.8 jit_solution(4600283947764792837)
XLA Ops:
  0.0 2.0 %chebyshev_filter.1.packed_ref = f32[256,128]{1,0:T(8,128)} custom-call(f32[6,8,128]{2,1,0:T(8,128)} %bitcast.6, s32[6,8,128]{2,1,0:T(8,128)} %bitcast.7, f32[4,8]{1,0:T(4,128)} %bitcast.8, f32[16]{0:T(128)} %refs_3_.1, s32[4]{0:T(128)} %refs_4_.1), custom_call_target="tpu_custom_call" | custom-call | tf_op jit(solution)/shard_map/chebyshev_filter/pallas_call | solution.py:175
  2.0 7.3 %all-to-all-start = ((f32[32,8,128]{2,1,0:T(8,128)}), f32[32,8,128]{2,1,0:T(8,128)S(1)}, u32[]{:S(2)}, u32[]{:S(2)}) async-start(f32[32,8,128]{2,1,0:T(8,128)} %bitcast.4), calls=%async_computation | async-start | bytes 262144 | tf_op jit(solution)/shard_map/all_to_all | solution.py:191
  9.3 7.7 %all-to-all-done.got_ref = f32[32,8,128]{2,1,0:T(8,128)S(1)} async-done(((f32[32,8,128]{2,1,0:T(8,128)}), f32[32,8,128]{2,1,0:T(8,128)S(1)}, u32[]{:S(2)}, u32[]{:S(2)}) %all-to-all-start) | async-done | bytes 131104 | tf_op jit(solution)/shard_map/all_to_all | solution.py:191
  17.0 0.8 %ritz_rotation.1 = f32[8,768]{1,0:T(8,128)} custom-call(f32[32,8,128]{2,1,0:T(8,128)S(1)} %all-to-all-done.got_ref, f32[8,768]{1,0:T(8,128)S(1)} %sums_start.1.start_ref), custom_call_target="tpu_custom_call" | custom-call | tf_op jit(solution)/shard_map/ritz_rotation/pallas_call | solution.py:205
  (1 shorter events, 0.0 us)
Async XLA Ops:
  2.0 15.1 %all-to-all-start = ((f32[32,8,128]{2,1,0:T(8,128)}), f32[32,8,128]{2,1,0:T(8,128)S(1)}, u32[]{:S(2)}, u32[]{:S(2)}) async-start(f32[32,8,128]{2,1,0:T(8,128)} %bitcast.4), calls=%async_computation | async-start | bytes 262144 | tf_op jit(solution)/shard_map/all_to_all | solution.py:191

commit v6 on v5

--- a/solution.py
+++ b/solution.py
@@ -68,7 +68,7 @@
 
 
 def filter_kernel(ng, copies, rows, run, width, *refs):
-    sources, out_ref, held, sems = refs[:5], refs[5], refs[6:11], refs[11]
+    sources, out_ref, held, sems, natural_ref = refs[:5], refs[5], refs[6:11], refs[11], refs[12]
     orb_ref, region_ref, ritz_ref, table_ref, counts_ref = held
     transfers = [
         pltpu.make_async_copy(source, target, sems.at[index])
@@ -104,14 +104,11 @@
         previous, current = current, following
 
     blocks = ys // run
-    for copy in range(copies):
-        for y in range(ys):
-            start = (copy * ng + y // run) * rows + y % run
-            out_ref[pl.ds(start, planes, stride=blocks * rows), :] = current[y]
+    for y in range(ys):
+        natural_ref[pl.ds((y // run) * rows + y % run, planes, stride=blocks * rows), :] = current[y]
 
     columns, panel = ritz_ref.shape
     per_row = LANES // width
-    tiles = copies * ng
     for row in range(-(-columns // per_row)):
         line = jnp.zeros((1, LANES), jnp.float32)
         for slot in range(min(per_row, columns - row * per_row)):
@@ -119,25 +116,26 @@
                 [ritz_ref[pl.ds(row * per_row + slot, 1), :], jnp.zeros((1, LANES - panel), jnp.float32)], axis=1
             )
             line = line + (pltpu.roll(piece, slot * width, 1) if slot else piece)
-        out_ref[pl.ds(run + row, tiles, stride=rows), :] = jnp.broadcast_to(line, (tiles, LANES))
-
-
-def start_kernel(packed_ref, out_ref):
-    out_ref[...] = jnp.zeros_like(out_ref)
-
-
-def rotate_kernel(nb, ng, run, width, columns, got_ref, start_ref, out_ref):
+        natural_ref[pl.ds(run + row, ng, stride=rows), :] = jnp.broadcast_to(line, (ng, LANES))
+    for copy in range(copies):
+        for tile in range(ng):
+            place = (copies - 1 - copy) * ng + ng - 1 - tile
+            out_ref[pl.ds(place * rows, rows), :] = natural_ref[pl.ds(tile * rows, rows), :]
+
+
+def rotate_kernel(nb, ng, run, width, columns, got_ref, out_ref):
     wanted = out_ref.shape[0]
     holders = wanted // columns
     sublane = lax.broadcasted_iota(jnp.int32, (wanted, LANES), 0)
     lane = lax.broadcasted_iota(jnp.int32, (wanted, LANES), 1)
     own = lane // width == sublane % columns
     block = lax.axis_index("band")
-    acc = [start_ref[:, pl.ds(y * LANES, LANES)] for y in range(run)]
+    acc = [jnp.zeros((wanted, LANES), jnp.float32) for _ in range(run)]
+    last = nb * ng - 1
     for b in range(nb):
         lines = jnp.zeros((wanted, LANES), jnp.float32)
         for k in range(holders):
-            line = got_ref[b * ng + block * holders + k, pl.ds(run, 1), :]
+            line = got_ref[last - b * ng - block * holders - k, pl.ds(run, 1), :]
             lines = jnp.where(sublane // columns == k, jnp.broadcast_to(line, (wanted, LANES)), lines)
         lines = jnp.where(own, lines, 0.0)
         gathered = lines
@@ -146,7 +144,7 @@
         for r in range(ng):
             weight = jnp.broadcast_to(gathered[:, r : r + 1], (wanted, LANES))
             for y in range(run):
-                acc[y] = acc[y] + weight * got_ref[b * ng + r, pl.ds(y, 1), :]
+                acc[y] = acc[y] + weight * got_ref[last - b * ng - r, pl.ds(y, 1), :]
     for y in range(run):
         out_ref[:, pl.ds(y * LANES, LANES)] = acc[y]
 
@@ -184,34 +182,28 @@
             pltpu.SMEM(potential_table.shape, jnp.float32),
             pltpu.SMEM(counts.shape, jnp.int32),
             pltpu.SemaphoreType.DMA((5,)),
+            pltpu.VMEM((ng * rows, LANES), jnp.float32),
         ],
         compiler_params=pltpu.CompilerParams(vmem_limit_bytes=packed_bytes + 32 * cells + 2**20),
         name="chebyshev_filter",
     )(*inputs)
     got = lax.all_to_all(
-        packed.reshape(tiles, rows, LANES), ("band", "grid"), split_axis=0, concat_axis=0, tiled=True
+        packed.reshape(tiles, rows, LANES), ("band", "grid"), split_axis=0, concat_axis=0, tiled=True,
+        axis_index_groups=[list(range(tiles))[::-1]],
     )
     if columns * width <= LANES and tiles <= 64 and panel == ng and panel <= 16:
         sum_shape = jax.ShapeDtypeStruct((panel, run * LANES), jnp.float32)
         limit = pltpu.CompilerParams(vmem_limit_bytes=packed_bytes + 2**20)
-        start = pl.pallas_call(
-            start_kernel,
-            out_shape=sum_shape,
-            in_specs=[pl.BlockSpec(memory_space=pl.ANY)],
-            out_specs=vmem,
-            compiler_params=limit,
-            name="sums_start",
-        )(packed)
         return pl.pallas_call(
             functools.partial(rotate_kernel, nb, ng, run, width, columns),
             out_shape=sum_shape,
-            in_specs=[vmem] * 2,
+            in_specs=[vmem],
             out_specs=vmem,
             compiler_params=limit,
             name="ritz_rotation",
-        )(got, start)
+        )(got)
     holders = panel // columns
-    by_source = got.reshape(nb, ng, rows, LANES)
+    by_source = got[::-1].reshape(nb, ng, rows, LANES)
     blocks = by_source[:, :, run : run + ritz_rows].reshape(nb, ng, ritz_rows * per_row, width)
     mine = lax.dynamic_slice_in_dim(blocks, lax.axis_index("band") * holders, holders, axis=1)
     return lax.dot_general(

time: 18.1 us -> 17.8 us (0.983)
  blocking collectives: 0 us -> 15.5 us
  waiting for transfers between devices: 7.73 us -> 0 us
  starting transfers between devices: 7.3 us -> 0 us
  Pallas kernels: 2.78 us -> 2.16 us
    all_to_all x0 -> x1, blocking collectives: none -> 15.5 us  [shards(): lax.all_to_all(packed.reshape(tiles, rows, LANES), ('band', 'grid'), spli...]
    all_to_all x1 -> x0, waiting for transfers between devices: 7.73 us -> none  [shards(): lax.all_to_all(packed.reshape(tiles, rows, LANES), ('band', 'grid'), spli...]
    all_to_all x1 -> x0, starting transfers between devices: 7.3 us -> none  [shards(): lax.all_to_all(packed.reshape(tiles, rows, LANES), ('band', 'grid'), spli...]
    pallas_call x1, Pallas kernels: 1.97 us -> 1.35 us  [shards(): pl.pallas_call(functools.partial(filter_kernel, ng, nb, rows, run, width)...]
  transfers between devices with their start and end apart: 1 -> 0, of which waited for: 1 -> 0; matrix products, arithmetic and copies ran while one was open for 0% -> 0% of each run, Pallas kernels for 0% -> 0%
where the time goes in v6:
time: 17.8 us; the launch traced here: 17.6 us
  blocking collectives  15.5 us (87%)
  Pallas kernels  2.16 us (12%)
    all_to_all x1, blocking collectives, shards(): lax.all_to_all(packed.reshape(tiles, rows, LANES), ('band', 'grid'), spli...  15.5 us
    pallas_call x1, Pallas kernels, shards(): pl.pallas_call(functools.partial(filter_kernel, ng, nb, rows, run, width)...  1.35 us
    pallas_call x1, Pallas kernels, shards(): pl.pallas_call(functools.partial(rotate_kernel, nb, ng, run, width, colum...  0.81 us

profile of v6, /device:TPU:0, one launch (start us, length us, event | category | flops | bytes accessed | tf_op | source)
XLA Modules:
  0.0 17.6 jit_solution(17261985149712012577)
XLA Ops:
  0.0 1.4 %chebyshev_filter.1 = f32[256,128]{1,0:T(8,128)S(1)} custom-call(f32[6,8,128]{2,1,0:T(8,128)} %bitcast.7, s32[6,8,128]{2,1,0:T(8,128)} %bitcast.8, f32[4,8]{1,0:T(4,128)} %bitcast.9, f32[16]{0:T(128)} %refs_3_.1, s32[4]{0:T(128)} %refs_4_.1), custom_call_target="tpu_custom_call" | custom-call | tf_op jit(solution)/shard_map/chebyshev_filter/pallas_call | solution.py:173
  1.4 15.5 %all_to_all.5.got_ref = f32[32,8,128]{2,1,0:T(8,128)S(1)} all-to-all(f32[32,8,128]{2,1,0:T(8,128)S(1)} %bitcast.6), channel_id=1, replica_groups={{31,30,29,28,27,26,25,24,23,22,21,20,19,18,17,16,15,14,13,12,11,10,9,8,..., dimensions={0} | all-to-all | bytes 262144 | tf_op jit(solution)/shard_map/all_to_all | solution.py:190
  16.8 0.8 %ritz_rotation.1 = f32[8,768]{1,0:T(8,128)} custom-call(f32[32,8,128]{2,1,0:T(8,128)S(1)} %all_to_all.5.got_ref), custom_call_target="tpu_custom_call" | custom-call | tf_op jit(solution)/shard_map/ritz_rotation/pallas_call | solution.py:197

commit v7 on v4

--- a/solution.py
+++ b/solution.py
@@ -68,7 +68,7 @@
 
 
 def filter_kernel(ng, copies, rows, run, width, cores, *refs):
-    sources, out_ref, held, sems = refs[:5], refs[5], refs[6:11], refs[11]
+    sources, out_ref, held, sems, natural_ref = refs[:5], refs[5], refs[6:11], refs[11], refs[12]
     orb_ref, region_ref, ritz_ref, table_ref, counts_ref = held
     transfers = [
         pltpu.make_async_copy(source, target, sems.at[index])
@@ -104,14 +104,11 @@
         previous, current = current, following
 
     blocks = ys // run
-    for copy in range(copies):
-        for y in range(ys):
-            start = (copy * ng + y // run) * rows + y % run
-            out_ref[pl.ds(start, planes, stride=blocks * rows), :] = current[y]
+    for y in range(ys):
+        natural_ref[pl.ds((y // run) * rows + y % run, planes, stride=blocks * rows), :] = current[y]
 
     columns, panel = ritz_ref.shape
     per_row = LANES // width
-    tiles = copies * ng
     for row in range(-(-columns // per_row)):
         line = jnp.zeros((1, LANES), jnp.float32)
         for slot in range(min(per_row, columns - row * per_row)):
@@ -119,11 +116,16 @@
                 [ritz_ref[pl.ds(row * per_row + slot, 1), :], jnp.zeros((1, LANES - panel), jnp.float32)], axis=1
             )
             line = line + (pltpu.roll(piece, slot * width, 1) if slot else piece)
-        out_ref[pl.ds(run + row, tiles, stride=rows), :] = jnp.broadcast_to(line, (tiles, LANES))
+        natural_ref[pl.ds(run + row, ng, stride=rows), :] = jnp.broadcast_to(line, (ng, LANES))
+    for copy in range(copies):
+        for tile in range(ng):
+            place = (copies - 1 - copy) * ng + ng - 1 - tile
+            out_ref[pl.ds(place * rows, rows), :] = natural_ref[pl.ds(tile * rows, rows), :]
 
 
 def partial_kernel(nrow, ng, run, width, columns, cores, got_ref, *outs):
     wanted = outs[0].shape[0]
+    last = nrow * ng - 1
     holders = wanted // columns
     sublane = lax.broadcasted_iota(jnp.int32, (wanted, LANES), 0)
     lane = lax.broadcasted_iota(jnp.int32, (wanted, LANES), 1)
@@ -135,7 +137,7 @@
         for row in range(nrow):
             lines = jnp.zeros((wanted, LANES), jnp.float32)
             for k in range(holders):
-                line = got_ref[row * ng + block * holders + k, pl.ds(run, 1), :]
+                line = got_ref[last - row * ng - block * holders - k, pl.ds(run, 1), :]
                 lines = jnp.where(sublane // columns == k, jnp.broadcast_to(line, (wanted, LANES)), lines)
             lines = jnp.where(own, lines, 0.0)
             total = lines
@@ -149,7 +151,7 @@
             for r in range(ng):
                 weight = jnp.broadcast_to(weights[distance][row][:, r : r + 1], (wanted, LANES))
                 for y in range(run):
-                    acc[y] = acc[y] + weight * got_ref[row * ng + r, pl.ds(y, 1), :]
+                    acc[y] = acc[y] + weight * got_ref[last - row * ng - r, pl.ds(y, 1), :]
         for y in range(run):
             out_ref[:, pl.ds(y * LANES, LANES)] = acc[y]
 
@@ -191,12 +193,14 @@
             pltpu.SMEM(potential_table.shape, jnp.float32),
             pltpu.SMEM(counts.shape, jnp.int32),
             pltpu.SemaphoreType.DMA((5,)),
+            pltpu.VMEM((ng * rows, LANES), jnp.float32),
         ],
         compiler_params=pltpu.CompilerParams(vmem_limit_bytes=packed_bytes + 32 * cells + 2**20),
         name="chebyshev_filter",
     )(*inputs)
     got = lax.all_to_all(
-        packed.reshape(tiles, rows, LANES), ("row", "grid"), split_axis=0, concat_axis=0, tiled=True
+        packed.reshape(tiles, rows, LANES), ("row", "grid"), split_axis=0, concat_axis=0, tiled=True,
+        axis_index_groups=[list(range(tiles))[::-1]],
     )
     sum_shape = jax.ShapeDtypeStruct((panel, run * LANES), jnp.float32)
     if columns * width <= LANES and tiles <= 64 and panel == ng and panel <= 16:
@@ -210,7 +214,7 @@
         )(got)
     else:
         holders = panel // columns
-        by_source = got.reshape(nrow, ng, rows, LANES)
+        by_source = got[::-1].reshape(nrow, ng, rows, LANES)
         fields = by_source[:, :, :run].reshape(tiles, run * LANES)
         blocks = by_source[:, :, run : run + ritz_rows].reshape(nrow, ng, ritz_rows * per_row, width)
         sums = []

time: 19.3 us -> 15.9 us (0.82)
  blocking collectives: 15.6 us -> 12.3 us
    all_to_all x1, blocking collectives: 15.6 us -> 12.3 us  [shards(): lax.all_to_all(packed.reshape(tiles, rows, LANES), ('row', 'grid'), split...]
where the time goes in v7:
time: 15.9 us; the launch traced here: 15.7 us
  blocking collectives  12.3 us (77%)
  Pallas kernels  2.16 us (14%)
  waiting for transfers between devices  1.18 us (7%)
    all_to_all x1, blocking collectives, shards(): lax.all_to_all(packed.reshape(tiles, rows, LANES), ('row', 'grid'), split...  12.3 us
    pallas_call x1, Pallas kernels, shards(): pl.pallas_call(functools.partial(filter_kernel, ng, nrow, rows, run, widt...  1.35 us
    ppermute x1, waiting for transfers between devices, shards(): terms.append(lax.ppermute(sums[distance], 'core', pairs))  1.18 us
    pallas_call x1, Pallas kernels, shards(): pl.pallas_call(sum_kernel, out_shape=sum_shape, in_specs=[vmem] * cores,...  0.61 us
  transfers between devices with their start and end apart: 1, of which 1 were waited for; matrix products, arithmetic and copies ran while one was open for 0% of the time, Pallas kernels for 0%

profile of v7, /device:TPU:0, one launch (start us, length us, event | category | flops | bytes accessed | tf_op | source)
XLA Modules:
  0.0 15.7 jit_solution(14716955212239371637)
XLA Ops:
  0.0 1.4 %chebyshev_filter.1 = f32[128,128]{1,0:T(8,128)S(1)} custom-call(f32[6,8,128]{2,1,0:T(8,128)} %bitcast.7, s32[6,8,128]{2,1,0:T(8,128)} %bitcast.8, f32[4,8]{1,0:T(4,128)} %bitcast.9, f32[16]{0:T(128)} %refs_3_.1, s32[4]{0:T(128)} %refs_4_.1), custom_call_target="tpu_custom_call" | custom-call | tf_op jit(solution)/shard_map/chebyshev_filter/pallas_call | solution.py:184
  1.4 12.3 %all_to_all.5.got_ref = f32[16,8,128]{2,1,0:T(8,128)S(1)} all-to-all(f32[16,8,128]{2,1,0:T(8,128)S(1)} %bitcast.6), channel_id=1, replica_groups={{23,22,21,20,19,18,17,16,7,6,5,4,3,2,1,0},{31,30,29,28,27,26,25,24,15,1..., dimensions={0} | all-to-all | bytes 131072 | tf_op jit(solution)/shard_map/all_to_all | solution.py:201
  13.6 0.2 %ritz_partial_sums.1 = (f32[8,768]{1,0:T(8,128)S(1)}, f32[8,768]{1,0:T(8,128)S(1)}) custom-call(f32[16,8,128]{2,1,0:T(8,128)S(1)} %all_to_all.5.got_ref), custom_call_target="tpu_custom_call" | custom-call | tf_op jit(solution)/shard_map/ritz_partial_sums/pallas_call | solution.py:207
  13.8 0.1 collective-permute-start
  13.9 1.2 %collective-permute-done.refs_1_ = f32[8,768]{1,0:T(8,128)S(1)} collective-permute-done((f32[8,768]{1,0:T(8,128)S(1)}, f32[8,768]{1,0:T(8,128)S(1)}, u32[]{:S(2)}, u32[]{:S(2)}) %collective-permute-start) | collective-permute-done | bytes 24608 | tf_op jit(solution)/shard_map/ppermute | solution.py:237
  15.1 0.6 %core_sum.1 = f32[8,768]{1,0:T(8,128)} custom-call(f32[8,768]{1,0:T(8,128)S(1)} %get-tuple-element.7.refs_0_, f32[8,768]{1,0:T(8,128)S(1)} %collective-permute-done.refs_1_), custom_call_target="tpu_custom_call" | custom-call | tf_op jit(solution)/shard_map/core_sum/pallas_call | solution.py:238
Async XLA Ops:
  13.8 1.3 %collective-permute-start = (f32[8,768]{1,0:T(8,128)S(1)}, f32[8,768]{1,0:T(8,128)S(1)}, u32[]{:S(2)}, u32[]{:S(2)}) collective-permute-start(f32[8,768]{1,0:T(8,128)S(1)} %get-tuple-element.8), channel_id=1, source_target_pairs={{0,8},{8,0},{1,9},{9,1},{2,10},{10,2},{3,11},{11,3},{4,12},{12,4},... | collective-permute-start | bytes 73736 | tf_op jit(solution)/shard_map/ppermute | solution.py:237

commit v8 on v6

--- a/solution.py
+++ b/solution.py
@@ -67,7 +67,7 @@
     return results
 
 
-def filter_kernel(ng, copies, rows, run, width, *refs):
+def filter_kernel(ng, rows, run, width, *refs):
     sources, out_ref, held, sems, natural_ref = refs[:5], refs[5], refs[6:11], refs[11], refs[12]
     orb_ref, region_ref, ritz_ref, table_ref, counts_ref = held
     transfers = [
@@ -79,8 +79,7 @@
     for transfer in transfers:
         transfer.wait()
     ys, planes, xs = orb_ref.shape
-    band_pos = lax.axis_index("band")
-    live = (lax.axis_index("grid") < counts_ref[band_pos]).astype(jnp.float32)
+    live = (lax.axis_index("grid") < counts_ref[lax.axis_index("band")]).astype(jnp.float32)
 
     centre_weight = 3.0 * COEFFICIENTS[0] + sum(pair_weights(n)[0] for n in (planes, ys, xs))
     scale = 2.0 / HALF
@@ -117,36 +116,36 @@
             )
             line = line + (pltpu.roll(piece, slot * width, 1) if slot else piece)
         natural_ref[pl.ds(run + row, ng, stride=rows), :] = jnp.broadcast_to(line, (ng, LANES))
-    for copy in range(copies):
-        for tile in range(ng):
-            place = (copies - 1 - copy) * ng + ng - 1 - tile
-            out_ref[pl.ds(place * rows, rows), :] = natural_ref[pl.ds(tile * rows, rows), :]
-
-
-def rotate_kernel(nb, ng, run, width, columns, got_ref, out_ref):
-    wanted = out_ref.shape[0]
+    for tile in range(ng):
+        out_ref[pl.ds((ng - 1 - tile) * rows, rows), :] = natural_ref[pl.ds(tile * rows, rows), :]
+
+
+def partial_kernel(order, ng, run, width, columns, got_ref, out_ref):
+    wanted = out_ref.shape[1]
     holders = wanted // columns
     sublane = lax.broadcasted_iota(jnp.int32, (wanted, LANES), 0)
     lane = lax.broadcasted_iota(jnp.int32, (wanted, LANES), 1)
     own = lane // width == sublane % columns
-    block = lax.axis_index("band")
-    acc = [jnp.zeros((wanted, LANES), jnp.float32) for _ in range(run)]
-    last = nb * ng - 1
-    for b in range(nb):
+    for place, block in enumerate(order):
         lines = jnp.zeros((wanted, LANES), jnp.float32)
         for k in range(holders):
-            line = got_ref[last - b * ng - block * holders - k, pl.ds(run, 1), :]
+            line = got_ref[ng - 1 - block * holders - k, pl.ds(run, 1), :]
             lines = jnp.where(sublane // columns == k, jnp.broadcast_to(line, (wanted, LANES)), lines)
         lines = jnp.where(own, lines, 0.0)
-        gathered = lines
+        weights = lines
         for slot in range(1, columns):
-            gathered = gathered + pltpu.roll(lines, LANES - slot * width, 1)
+            weights = weights + pltpu.roll(lines, LANES - slot * width, 1)
+        acc = [jnp.zeros((wanted, LANES), jnp.float32) for _ in range(run)]
         for r in range(ng):
-            weight = jnp.broadcast_to(gathered[:, r : r + 1], (wanted, LANES))
+            weight = jnp.broadcast_to(weights[:, r : r + 1], (wanted, LANES))
             for y in range(run):
-                acc[y] = acc[y] + weight * got_ref[last - b * ng - r, pl.ds(y, 1), :]
-    for y in range(run):
-        out_ref[:, pl.ds(y * LANES, LANES)] = acc[y]
+                acc[y] = acc[y] + weight * got_ref[ng - 1 - r, pl.ds(y, 1), :]
+        for y in range(run):
+            out_ref[place, :, pl.ds(y * LANES, LANES)] = acc[y]
+
+
+def sum_kernel(parts_ref, out_ref):
+    out_ref[...] = functools.reduce(jnp.add, [parts_ref[place] for place in range(parts_ref.shape[0])])
 
 
 def shards(nb, ng, orbitals, region, potential_table, counts, ritz):
@@ -160,7 +159,6 @@
     per_row = LANES // width
     ritz_rows = -(-columns // per_row)
     rows = -(-(run + ritz_rows) // SUBLANES) * SUBLANES
-    tiles = nb * ng
     vmem = pl.BlockSpec(memory_space=pltpu.VMEM)
     hbm = pl.BlockSpec(memory_space=pltpu.HBM)
     inputs = [
@@ -169,10 +167,10 @@
             jnp.transpose(orbitals[0], (1, 0, 2)), jnp.transpose(region, (1, 0, 2)), ritz.T, potential_table, counts
         )
     ]
-    packed_bytes = 4 * tiles * rows * LANES
+    packed_bytes = 4 * ng * rows * LANES
     packed = pl.pallas_call(
-        functools.partial(filter_kernel, ng, nb, rows, run, width),
-        out_shape=jax.ShapeDtypeStruct((tiles * rows, LANES), jnp.float32),
+        functools.partial(filter_kernel, ng, rows, run, width),
+        out_shape=jax.ShapeDtypeStruct((ng * rows, LANES), jnp.float32),
         in_specs=[hbm] * 5,
         out_specs=vmem,
         scratch_shapes=[
@@ -184,35 +182,44 @@
             pltpu.SemaphoreType.DMA((5,)),
             pltpu.VMEM((ng * rows, LANES), jnp.float32),
         ],
-        compiler_params=pltpu.CompilerParams(vmem_limit_bytes=packed_bytes + 32 * cells + 2**20),
+        compiler_params=pltpu.CompilerParams(vmem_limit_bytes=2 * packed_bytes + 64 * cells + 2**20),
         name="chebyshev_filter",
     )(*inputs)
     got = lax.all_to_all(
-        packed.reshape(tiles, rows, LANES), ("band", "grid"), split_axis=0, concat_axis=0, tiled=True,
-        axis_index_groups=[list(range(tiles))[::-1]],
+        packed.reshape(ng, rows, LANES), "grid", split_axis=0, concat_axis=0, tiled=True,
+        axis_index_groups=[list(range(ng))[::-1]],
     )
-    if columns * width <= LANES and tiles <= 64 and panel == ng and panel <= 16:
-        sum_shape = jax.ShapeDtypeStruct((panel, run * LANES), jnp.float32)
-        limit = pltpu.CompilerParams(vmem_limit_bytes=packed_bytes + 2**20)
-        return pl.pallas_call(
-            functools.partial(rotate_kernel, nb, ng, run, width, columns),
-            out_shape=sum_shape,
+    order = sorted(range(nb), key=lambda band: (-(band // 2), band % 2))
+    parts_shape = (nb, panel, run * LANES)
+    if columns * width <= LANES and panel == ng and panel <= 16 and nb <= 8:
+        parts = pl.pallas_call(
+            functools.partial(partial_kernel, order, ng, run, width, columns),
+            out_shape=jax.ShapeDtypeStruct(parts_shape, jnp.float32),
             in_specs=[vmem],
             out_specs=vmem,
-            compiler_params=limit,
-            name="ritz_rotation",
+            compiler_params=pltpu.CompilerParams(vmem_limit_bytes=2**21),
+            name="ritz_partial_sums",
         )(got)
-    holders = panel // columns
-    by_source = got[::-1].reshape(nb, ng, rows, LANES)
-    blocks = by_source[:, :, run : run + ritz_rows].reshape(nb, ng, ritz_rows * per_row, width)
-    mine = lax.dynamic_slice_in_dim(blocks, lax.axis_index("band") * holders, holders, axis=1)
-    return lax.dot_general(
-        jnp.transpose(mine[:, :, :columns, :panel], (0, 3, 1, 2)).reshape(tiles, panel),
-        by_source[:, :, :run].reshape(tiles, run * LANES),
-        (((0,), (0,)), ((), ())),
-        precision=lax.Precision.HIGHEST,
-        preferred_element_type=jnp.float32,
-    )
+    else:
+        by_source = got[::-1]
+        lines = by_source[:, run : run + ritz_rows].reshape(ng, ritz_rows * per_row, width)[:, :columns, :panel]
+        weights = jnp.transpose(lines, (2, 0, 1)).reshape(panel, nb, panel)
+        parts = lax.dot_general(
+            weights[:, jnp.array(order)].reshape(panel, nb * panel),
+            by_source[:, :run].reshape(ng, run * LANES),
+            (((0,), (0,)), ((), ())),
+            precision=lax.Precision.HIGHEST,
+            preferred_element_type=jnp.float32,
+        ).reshape(parts_shape)
+    parts = lax.all_to_all(parts, "band", split_axis=0, concat_axis=0, tiled=True, axis_index_groups=[order])
+    return pl.pallas_call(
+        sum_kernel,
+        out_shape=jax.ShapeDtypeStruct(parts_shape[1:], jnp.float32),
+        in_specs=[vmem],
+        out_specs=vmem,
+        compiler_params=pltpu.CompilerParams(vmem_limit_bytes=4 * (nb + 1) * panel * run * LANES + 2**20),
+        name="band_sum",
+    )(parts)
 
 
 def solution(mesh):

time: 17.8 us -> 19.9 us (1.12)
  blocking collectives: 15.5 us -> 17.5 us
    all_to_all x1 -> x2, blocking collectives: 15.5 us -> 17.5 us  [the longest x1 11 us: shards(): lax.all_to_all(packed.reshape(ng, rows, LANES), 'grid', split_axis=0, con...]
    pallas_call x2 -> x3, Pallas kernels: 2.16 us -> 2.16 us  [the longest x1 1.35 us: shards(): pl.pallas_call(functools.partial(filter_kernel, ng, rows, run, width), ou...]
where the time goes in v8:
time: 19.9 us; the launch traced here: 19.7 us
  blocking collectives  17.5 us (88%)
  Pallas kernels  2.16 us (11%)
    all_to_all x1, blocking collectives, shards(): lax.all_to_all(packed.reshape(ng, rows, LANES), 'grid', split_axis=0, con...  11 us
    all_to_all x1, blocking collectives, shards(): lax.all_to_all(parts, 'band', split_axis=0, concat_axis=0, tiled=True, ax...  6.51 us
    pallas_call x1, Pallas kernels, shards(): pl.pallas_call(functools.partial(filter_kernel, ng, rows, run, width), ou...  1.35 us
    pallas_call x1, Pallas kernels, shards(): pl.pallas_call(sum_kernel, out_shape=jax.ShapeDtypeStruct(parts_shape[1:]...  0.62 us

profile of v8, /device:TPU:0, one launch (start us, length us, event | category | flops | bytes accessed | tf_op | source)
XLA Modules:
  0.0 19.7 jit_solution(16123146628658400240)
XLA Ops:
  0.0 1.3 %chebyshev_filter.1 = f32[64,128]{1,0:T(8,128)S(1)} custom-call(f32[6,8,128]{2,1,0:T(8,128)} %bitcast.7, s32[6,8,128]{2,1,0:T(8,128)} %bitcast.8, f32[4,8]{1,0:T(4,128)} %bitcast.9, f32[16]{0:T(128)} %refs_3_.1, s32[4]{0:T(128)} %refs_4_.1), custom_call_target="tpu_custom_call" | custom-call | tf_op jit(solution)/shard_map/chebyshev_filter/pallas_call | solution.py:171
  1.4 11.0 %all_to_all.10.got_ref = f32[8,8,128]{2,1,0:T(8,128)S(1)} all-to-all(f32[8,8,128]{2,1,0:T(8,128)S(1)} %bitcast.6), channel_id=1, replica_groups={{7,6,5,4,3,2,1,0},{15,14,13,12,11,10,9,8},{23,22,21,20,19,18,17,16},{31..., dimensions={0} | all-to-all | bytes 65536 | tf_op jit(solution)/shard_map/all_to_all | solution.py:188
  12.3 0.2 %ritz_partial_sums.1 = f32[4,8,768]{2,1,0:T(8,128)S(1)} custom-call(f32[8,8,128]{2,1,0:T(8,128)S(1)} %all_to_all.10.got_ref), custom_call_target="tpu_custom_call" | custom-call | tf_op jit(solution)/shard_map/ritz_partial_sums/pallas_call | solution.py:195
  12.6 6.5 %all_to_all.11.parts_ref = f32[4,8,768]{2,1,0:T(8,128)S(1)} all-to-all(f32[4,8,768]{2,1,0:T(8,128)S(1)} %ritz_partial_sums.1), channel_id=1, replica_groups={{16,24,0,8},{17,25,1,9},{18,26,2,10},{19,27,3,11},{20,28,4,12},{21,29,5..., dimensions={0} | all-to-all | bytes 196608 | tf_op jit(solution)/shard_map/all_to_all | solution.py:214
  19.1 0.6 %band_sum.1 = f32[8,768]{1,0:T(8,128)} custom-call(f32[4,8,768]{2,1,0:T(8,128)S(1)} %all_to_all.11.parts_ref), custom_call_target="tpu_custom_call" | custom-call | tf_op jit(solution)/shard_map/band_sum/pallas_call | solution.py:215

commit v9 on v7

--- a/solution.py
+++ b/solution.py
@@ -67,7 +67,7 @@
     return results
 
 
-def filter_kernel(ng, copies, rows, run, width, cores, *refs):
+def filter_kernel(ng, copies, rows, run, width, cores, order, *refs):
     sources, out_ref, held, sems, natural_ref = refs[:5], refs[5], refs[6:11], refs[11], refs[12]
     orb_ref, region_ref, ritz_ref, table_ref, counts_ref = held
     transfers = [
@@ -119,13 +119,15 @@
         natural_ref[pl.ds(run + row, ng, stride=rows), :] = jnp.broadcast_to(line, (ng, LANES))
     for copy in range(copies):
         for tile in range(ng):
-            place = (copies - 1 - copy) * ng + ng - 1 - tile
+            place = order.index(copy * ng + tile)
             out_ref[pl.ds(place * rows, rows), :] = natural_ref[pl.ds(tile * rows, rows), :]
 
 
-def partial_kernel(nrow, ng, run, width, columns, cores, got_ref, *outs):
+def partial_kernel(nrow, ng, run, width, columns, cores, order, got_ref, *refs):
+    outs, ritz_ref = refs[:-1], refs[-1]
+    for place, source in enumerate(order):
+        ritz_ref[source] = got_ref[place, pl.ds(run, 1), :]
     wanted = outs[0].shape[0]
-    last = nrow * ng - 1
     holders = wanted // columns
     sublane = lax.broadcasted_iota(jnp.int32, (wanted, LANES), 0)
     lane = lax.broadcasted_iota(jnp.int32, (wanted, LANES), 1)
@@ -137,7 +139,7 @@
         for row in range(nrow):
             lines = jnp.zeros((wanted, LANES), jnp.float32)
             for k in range(holders):
-                line = got_ref[last - row * ng - block * holders - k, pl.ds(run, 1), :]
+                line = ritz_ref[row * ng + block * holders + k]
                 lines = jnp.where(sublane // columns == k, jnp.broadcast_to(line, (wanted, LANES)), lines)
             lines = jnp.where(own, lines, 0.0)
             total = lines
@@ -151,7 +153,7 @@
             for r in range(ng):
                 weight = jnp.broadcast_to(weights[distance][row][:, r : r + 1], (wanted, LANES))
                 for y in range(run):
-                    acc[y] = acc[y] + weight * got_ref[last - row * ng - r, pl.ds(y, 1), :]
+                    acc[y] = acc[y] + weight * got_ref[order.index(row * ng + r), pl.ds(y, 1), :]
         for y in range(run):
             out_ref[:, pl.ds(y * LANES, LANES)] = acc[y]
 
@@ -180,9 +182,11 @@
             jnp.transpose(orbitals[0], (1, 0, 2)), jnp.transpose(region, (1, 0, 2)), ritz.T, potential_table, counts
         )
     ]
+    late = sorted(range(tiles), key=lambda place: (place % ng // (ng // 2), place // ng, place % ng), reverse=True)
+    order = [place for pair in zip(late, late[::-1]) for place in pair][:tiles]
     packed_bytes = 4 * tiles * rows * LANES
     packed = pl.pallas_call(
-        functools.partial(filter_kernel, ng, nrow, rows, run, width, cores),
+        functools.partial(filter_kernel, ng, nrow, rows, run, width, cores, order),
         out_shape=jax.ShapeDtypeStruct((tiles * rows, LANES), jnp.float32),
         in_specs=[hbm] * 5,
         out_specs=vmem,
@@ -195,26 +199,27 @@
             pltpu.SemaphoreType.DMA((5,)),
             pltpu.VMEM((ng * rows, LANES), jnp.float32),
         ],
-        compiler_params=pltpu.CompilerParams(vmem_limit_bytes=packed_bytes + 32 * cells + 2**20),
+        compiler_params=pltpu.CompilerParams(vmem_limit_bytes=2 * packed_bytes + 64 * cells + 2**20),
         name="chebyshev_filter",
     )(*inputs)
     got = lax.all_to_all(
         packed.reshape(tiles, rows, LANES), ("row", "grid"), split_axis=0, concat_axis=0, tiled=True,
-        axis_index_groups=[list(range(tiles))[::-1]],
+        axis_index_groups=[order],
     )
     sum_shape = jax.ShapeDtypeStruct((panel, run * LANES), jnp.float32)
     if columns * width <= LANES and tiles <= 64 and panel == ng and panel <= 16:
         sums = pl.pallas_call(
-            functools.partial(partial_kernel, nrow, ng, run, width, columns, cores),
+            functools.partial(partial_kernel, nrow, ng, run, width, columns, cores, order),
             out_shape=[sum_shape] * cores,
             in_specs=[vmem],
             out_specs=[vmem] * cores,
+            scratch_shapes=[pltpu.VMEM((tiles, 1, LANES), jnp.float32)],
             compiler_params=pltpu.CompilerParams(vmem_limit_bytes=packed_bytes + 2**20),
             name="ritz_partial_sums",
         )(got)
     else:
         holders = panel // columns
-        by_source = got[::-1].reshape(nrow, ng, rows, LANES)
+        by_source = got[jnp.argsort(jnp.array(order))].reshape(nrow, ng, rows, LANES)
         fields = by_source[:, :, :run].reshape(tiles, run * LANES)
         blocks = by_source[:, :, run : run + ritz_rows].reshape(nrow, ng, ritz_rows * per_row, width)
         sums = []

time: 15.9 us -> 15.9 us (level)
  no operation moved by 1% of the time
where the time goes in v9:
time: 15.9 us; the launch traced here: 15.7 us
  blocking collectives  12.3 us (77%)
  Pallas kernels  2.17 us (14%)
  waiting for transfers between devices  1.18 us (7%)
    all_to_all x1, blocking collectives, shards(): lax.all_to_all(packed.reshape(tiles, rows, LANES), ('row', 'grid'), split...  12.3 us
    pallas_call x1, Pallas kernels, shards(): pl.pallas_call(functools.partial(filter_kernel, ng, nrow, rows, run, widt...  1.35 us
    ppermute x1, waiting for transfers between devices, shards(): terms.append(lax.ppermute(sums[distance], 'core', pairs))  1.18 us
    pallas_call x1, Pallas kernels, shards(): pl.pallas_call(sum_kernel, out_shape=sum_shape, in_specs=[vmem] * cores,...  0.61 us
  transfers between devices with their start and end apart: 1, of which 1 were waited for; matrix products, arithmetic and copies ran while one was open for 0% of the time, Pallas kernels for 0%

profile of v9, /device:TPU:0, one launch (start us, length us, event | category | flops | bytes accessed | tf_op | source)
XLA Modules:
  0.0 15.7 jit_solution(6079238854750900183)
XLA Ops:
  0.0 1.4 %chebyshev_filter.1 = f32[128,128]{1,0:T(8,128)S(1)} custom-call(f32[6,8,128]{2,1,0:T(8,128)} %bitcast.7, s32[6,8,128]{2,1,0:T(8,128)} %bitcast.8, f32[4,8]{1,0:T(4,128)} %bitcast.9, f32[16]{0:T(128)} %refs_3_.1, s32[4]{0:T(128)} %refs_4_.1), custom_call_target="tpu_custom_call" | custom-call | tf_op jit(solution)/shard_map/chebyshev_filter/pallas_call | solution.py:188
  1.4 12.3 %all_to_all.5.got_ref = f32[16,8,128]{2,1,0:T(8,128)S(1)} all-to-all(f32[16,8,128]{2,1,0:T(8,128)S(1)} %bitcast.6), channel_id=1, replica_groups={{23,0,22,1,21,2,20,3,7,16,6,17,5,18,4,19},{31,8,30,9,29,10,28,11,15,24,..., dimensions={0} | all-to-all | bytes 131072 | tf_op jit(solution)/shard_map/all_to_all | solution.py:205
  13.6 0.2 %ritz_partial_sums.1 = (f32[8,768]{1,0:T(8,128)S(1)}, f32[8,768]{1,0:T(8,128)S(1)}) custom-call(f32[16,8,128]{2,1,0:T(8,128)S(1)} %all_to_all.5.got_ref), custom_call_target="tpu_custom_call" | custom-call | tf_op jit(solution)/shard_map/ritz_partial_sums/pallas_call | solution.py:211
  13.9 0.1 collective-permute-start
  13.9 1.2 %collective-permute-done.refs_1_ = f32[8,768]{1,0:T(8,128)S(1)} collective-permute-done((f32[8,768]{1,0:T(8,128)S(1)}, f32[8,768]{1,0:T(8,128)S(1)}, u32[]{:S(2)}, u32[]{:S(2)}) %collective-permute-start) | collective-permute-done | bytes 24608 | tf_op jit(solution)/shard_map/ppermute | solution.py:242
  15.1 0.6 %core_sum.1 = f32[8,768]{1,0:T(8,128)} custom-call(f32[8,768]{1,0:T(8,128)S(1)} %get-tuple-element.7.refs_0_, f32[8,768]{1,0:T(8,128)S(1)} %collective-permute-done.refs_1_), custom_call_target="tpu_custom_call" | custom-call | tf_op jit(solution)/shard_map/core_sum/pallas_call | solution.py:243
Async XLA Ops:
  13.9 1.3 %collective-permute-start = (f32[8,768]{1,0:T(8,128)S(1)}, f32[8,768]{1,0:T(8,128)S(1)}, u32[]{:S(2)}, u32[]{:S(2)}) collective-permute-start(f32[8,768]{1,0:T(8,128)S(1)} %get-tuple-element.8), channel_id=1, source_target_pairs={{0,8},{8,0},{1,9},{9,1},{2,10},{10,2},{3,11},{11,3},{4,12},{12,4},... | collective-permute-start | bytes 73736 | tf_op jit(solution)/shard_map/ppermute | solution.py:242

commit v10 on v6

--- a/solution.py
+++ b/solution.py
@@ -123,14 +123,18 @@
             out_ref[pl.ds(place * rows, rows), :] = natural_ref[pl.ds(tile * rows, rows), :]
 
 
-def rotate_kernel(nb, ng, run, width, columns, got_ref, out_ref):
+def start_kernel(packed_ref, out_ref):
+    out_ref[...] = jnp.zeros_like(out_ref)
+
+
+def rotate_kernel(nb, ng, run, width, columns, got_ref, start_ref, out_ref):
     wanted = out_ref.shape[0]
     holders = wanted // columns
     sublane = lax.broadcasted_iota(jnp.int32, (wanted, LANES), 0)
     lane = lax.broadcasted_iota(jnp.int32, (wanted, LANES), 1)
     own = lane // width == sublane % columns
     block = lax.axis_index("band")
-    acc = [jnp.zeros((wanted, LANES), jnp.float32) for _ in range(run)]
+    acc = [start_ref[:, pl.ds(y * LANES, LANES)] for y in range(run)]
     last = nb * ng - 1
     for b in range(nb):
         lines = jnp.zeros((wanted, LANES), jnp.float32)
@@ -194,14 +198,22 @@
     if columns * width <= LANES and tiles <= 64 and panel == ng and panel <= 16:
         sum_shape = jax.ShapeDtypeStruct((panel, run * LANES), jnp.float32)
         limit = pltpu.CompilerParams(vmem_limit_bytes=packed_bytes + 2**20)
+        start = pl.pallas_call(
+            start_kernel,
+            out_shape=sum_shape,
+            in_specs=[pl.BlockSpec(memory_space=pl.ANY)],
+            out_specs=vmem,
+            compiler_params=limit,
+            name="sums_start",
+        )(packed)
         return pl.pallas_call(
             functools.partial(rotate_kernel, nb, ng, run, width, columns),
             out_shape=sum_shape,
-            in_specs=[vmem],
+            in_specs=[vmem] * 2,
             out_specs=vmem,
             compiler_params=limit,
             name="ritz_rotation",
-        )(got)
+        )(got, start)
     holders = panel // columns
     by_source = got[::-1].reshape(nb, ng, rows, LANES)
     blocks = by_source[:, :, run : run + ritz_rows].reshape(nb, ng, ritz_rows * per_row, width)

time: 17.8 us -> 18.7 us (1.051)
  blocking collectives: 15.5 us -> 0 us
  waiting for transfers between devices: 0 us -> 8.35 us
  starting transfers between devices: 0 us -> 7.3 us
  Pallas kernels: 2.16 us -> 2.8 us
    all_to_all x1 -> x0, blocking collectives: 15.5 us -> none  [shards(): lax.all_to_all(packed.reshape(tiles, rows, LANES), ('band', 'grid'), spli...]
    all_to_all x0 -> x1, waiting for transfers between devices: none -> 8.35 us  [shards(): lax.all_to_all(packed.reshape(tiles, rows, LANES), ('band', 'grid'), spli...]
    all_to_all x0 -> x1, starting transfers between devices: none -> 7.3 us  [shards(): lax.all_to_all(packed.reshape(tiles, rows, LANES), ('band', 'grid'), spli...]
    pallas_call x1, Pallas kernels: 1.35 us -> 1.99 us  [shards(): pl.pallas_call(functools.partial(filter_kernel, ng, nb, rows, run, width)...]
  transfers between devices with their start and end apart: 0 -> 1, of which waited for: 0 -> 1; matrix products, arithmetic and copies ran while one was open for 0% -> 0% of each run, Pallas kernels for 0% -> 0%
where the time goes in v10:
time: 18.7 us; the launch traced here: 18.5 us
  waiting for transfers between devices  8.35 us (45%)
  starting transfers between devices  7.3 us (39%)
  Pallas kernels  2.8 us (15%)
    all_to_all x1, waiting for transfers between devices, shards(): lax.all_to_all(packed.reshape(tiles, rows, LANES), ('band', 'grid'), spli...  8.35 us
    all_to_all x1, starting transfers between devices, shards(): lax.all_to_all(packed.reshape(tiles, rows, LANES), ('band', 'grid'), spli...  7.3 us
    pallas_call x1, Pallas kernels, shards(): pl.pallas_call(functools.partial(filter_kernel, ng, nb, rows, run, width)...  1.99 us
    pallas_call x1, Pallas kernels, shards(): pl.pallas_call(functools.partial(rotate_kernel, nb, ng, run, width, colum...  0.81 us
  transfers between devices with their start and end apart: 1, of which 1 were waited for; matrix products, arithmetic and copies ran while one was open for 0% of the time, Pallas kernels for 0%

profile of v10, /device:TPU:0, one launch (start us, length us, event | category | flops | bytes accessed | tf_op | source)
XLA Modules:
  0.0 18.5 jit_solution(4514341297114966031)
XLA Ops:
  0.0 2.0 %chebyshev_filter.1.packed_ref = f32[256,128]{1,0:T(8,128)} custom-call(f32[6,8,128]{2,1,0:T(8,128)} %bitcast.6, s32[6,8,128]{2,1,0:T(8,128)} %bitcast.7, f32[4,8]{1,0:T(4,128)} %bitcast.8, f32[16]{0:T(128)} %refs_3_.1, s32[4]{0:T(128)} %refs_4_.1), custom_call_target="tpu_custom_call" | custom-call | tf_op jit(solution)/shard_map/chebyshev_filter/pallas_call | solution.py:177
  2.0 7.3 %all-to-all-start = ((f32[32,8,128]{2,1,0:T(8,128)}), f32[32,8,128]{2,1,0:T(8,128)S(1)}, u32[]{:S(2)}, u32[]{:S(2)}) async-start(f32[32,8,128]{2,1,0:T(8,128)} %bitcast.4), calls=%async_computation | async-start | bytes 262144 | tf_op jit(solution)/shard_map/all_to_all | solution.py:194
  9.3 8.3 %all-to-all-done.got_ref = f32[32,8,128]{2,1,0:T(8,128)S(1)} async-done(((f32[32,8,128]{2,1,0:T(8,128)}), f32[32,8,128]{2,1,0:T(8,128)S(1)}, u32[]{:S(2)}, u32[]{:S(2)}) %all-to-all-start) | async-done | bytes 131104 | tf_op jit(solution)/shard_map/all_to_all | solution.py:194
  17.7 0.8 %ritz_rotation.1 = f32[8,768]{1,0:T(8,128)} custom-call(f32[32,8,128]{2,1,0:T(8,128)S(1)} %all-to-all-done.got_ref, f32[8,768]{1,0:T(8,128)S(1)} %sums_start.1.start_ref), custom_call_target="tpu_custom_call" | custom-call | tf_op jit(solution)/shard_map/ritz_rotation/pallas_call | solution.py:209
  (1 shorter events, 0.0 us)
Async XLA Ops:
  2.0 15.7 %all-to-all-start = ((f32[32,8,128]{2,1,0:T(8,128)}), f32[32,8,128]{2,1,0:T(8,128)S(1)}, u32[]{:S(2)}, u32[]{:S(2)}) async-start(f32[32,8,128]{2,1,0:T(8,128)} %bitcast.4), calls=%async_computation | async-start | bytes 262144 | tf_op jit(solution)/shard_map/all_to_all | solution.py:194

commit v11 on v4

v11 whole, which is shorter than its diff:
```python
import functools

import jax
import jax.numpy as jnp
from jax import lax
from jax.experimental import pallas as pl
from jax.experimental.pallas import tpu as pltpu
from jax.sharding import PartitionSpec as P

DEGREE = 4

COEFFICIENTS = (
    -5369.0 / 1800.0,
    12.0 / 7.0,
    -15.0 / 56.0,
    10.0 / 189.0,
    -1.0 / 112.0,
    2.0 / 1925.0,
    -1.0 / 16632.0,
)
SPACING = 0.5
LOWER = 6.0
UPPER = 46.0
HALF = (UPPER - LOWER) / 2.0
CENTRE = (UPPER + LOWER) / 2.0
LANES = 128
SUBLANES = 8


def ring_weights(length):
    weights = [0.0] * length
    for offset in range(1, 7):
        weights[offset % length] += COEFFICIENTS[offset]
        weights[-offset % length] += COEFFICIENTS[offset]
    return weights


def pair_weights(length):
    weights = ring_weights(length)
    pairs = []
    for distance in range(1, length // 2 + 1):
        if weights[distance] != 0.0:
            pairs.append((sorted({distance, length - distance}), weights[distance]))
    return weights[0], pairs


def off_diagonal(field, planes, xs):
    ys = len(field)
    _, x_pairs = pair_weights(xs)
    _, y_pairs = pair_weights(ys)
    _, p_pairs = pair_weights(planes)
    results = []
    for y in range(ys):
        tile = field[y]
        total = None
        terms = []
        for shifts, weight in x_pairs:
            terms.append((weight, [pltpu.roll(tile, shift, 1) for shift in shifts]))
        for shifts, weight in p_pairs:
            terms.append((weight, [pltpu.roll(tile, shift, 0) for shift in shifts]))
        for shifts, weight in y_pairs:
            terms.append((weight, [field[(y - shift) % ys] for shift in shifts]))
        for weight, parts in terms:
            value = weight * functools.reduce(jnp.add, parts)
            total = value if total is None else total + value
        results.append(total)
    return results


def filter_kernel(ng, copies, rows, run, width, cores, *refs):
    sources, out_ref, held, sems = refs[:5], refs[5], refs[6:11], refs[11]
    orb_ref, region_ref, table_ref, counts_ref, ritz_ref = held
    transfers = [
        pltpu.make_async_copy(source, target, sems.at[index])
        for index, (source, target) in enumerate(zip(sources, held))
    ]
    for transfer in transfers:
        transfer.start()
    ys, planes, xs = orb_ref.shape
    centre_weight = 3.0 * COEFFICIENTS[0] + sum(pair_weights(n)[0] for n in (planes, ys, xs))
    scale = 2.0 / HALF
    hop = -0.5 / (SPACING * SPACING) * scale

    def doubled(field, away):
        return [diagonal[y] * field[y] + hop * away[y] for y in range(ys)]

    transfers[0].wait()
    previous = [orb_ref[y] for y in range(ys)]
    away = off_diagonal(previous, planes, xs)
    transfers[1].wait()
    transfers[2].wait()
    diagonal = []
    for y in range(ys):
        region = region_ref[y]
        potential = jnp.zeros((planes, xs), jnp.float32)
        for index in range(table_ref.shape[0]):
            potential = jnp.where(region == index, table_ref[index], potential)
        diagonal.append(scale * potential + (hop * centre_weight - scale * CENTRE))
    current = [0.5 * value for value in doubled(previous, away)]
    for _ in range(DEGREE - 1):
        away = off_diagonal(current, planes, xs)
        following = [value - before for value, before in zip(doubled(current, away), previous)]
        previous, current = current, following
    transfers[3].wait()
    transfers[4].wait()
    band_pos = lax.axis_index("row") * cores + lax.axis_index("core")
    live = (lax.axis_index("grid") < counts_ref[band_pos]).astype(jnp.float32)

    blocks = ys // run
    for y in range(ys):
        masked = current[y] * live
        for copy in range(copies):
            first = copy * ng + y // run + 1
            count = planes if copy < copies - 1 or y // run < blocks - 1 else planes - 1
            out_ref[pl.ds(first * rows + y % run, count, stride=blocks * rows), :] = masked[:count]
            if count < planes:
                out_ref[pl.ds(y % run, 1), :] = masked[count:]

    columns, panel = ritz_ref.shape
    per_row = LANES // width
    for row in range(-(-columns // per_row)):
        line = jnp.zeros((1, LANES), jnp.float32)
        for slot in range(min(per_row, columns - row * per_row)):
            piece = jnp.concatenate(
                [ritz_ref[pl.ds(row * per_row + slot, 1), :], jnp.zeros((1, LANES - panel), jnp.float32)], axis=1
            )
            line = line + (pltpu.roll(piece, slot * width, 1) if slot else piece)
        out_ref[pl.ds(run + row, copies * ng, stride=rows), :] = jnp.broadcast_to(line, (copies * ng, LANES))


def partial_kernel(nrow, ng, run, width, columns, cores, order, distance, got_ref, out_ref, ritz_ref):
    for place, source in enumerate(order):
        ritz_ref[source] = got_ref[place, pl.ds(run, 1), :]
    wanted = out_ref.shape[0]
    holders = wanted // columns
    sublane = lax.broadcasted_iota(jnp.int32, (wanted, LANES), 0)
    lane = lax.broadcasted_iota(jnp.int32, (wanted, LANES), 1)
    own = lane // width == sublane % columns
    block = lax.axis_index("row") * cores + lax.rem(lax.axis_index("core") + distance, cores)
    acc = [jnp.zeros((wanted, LANES), jnp.float32) for _ in range(run)]
    for row in range(nrow):
        lines = jnp.zeros((wanted, LANES), jnp.float32)
        for k in range(holders):
            line = ritz_ref[row * ng + block * holders + k]
            lines = jnp.where(sublane // columns == k, jnp.broadcast_to(line, (wanted, LANES)), lines)
        lines = jnp.where(own, lines, 0.0)
        weights = lines
        for slot in range(1, columns):
            weights = weights + pltpu.roll(lines, LANES - slot * width, 1)
        for r in range(ng):
            weight = jnp.broadcast_to(weights[:, r : r + 1], (wanted, LANES))
            for y in range(run):
                acc[y] = acc[y] + weight * got_ref[order.index(row * ng + r), pl.ds(y, 1), :]
    for y in range(run):
        out_ref[:, pl.ds(y * LANES, LANES)] = acc[y]


def sum_kernel(*refs):
    refs[-1][...] = functools.reduce(jnp.add, [ref[...] for ref in refs[:-1]])


def shards(nrow, cores, ng, orbitals, region, potential_table, counts, ritz):
    _, planes, ys, xs = orbitals.shape
    cells = planes * ys * xs
    panel, columns = ritz.shape
    run = cells // ng // xs
    width = 1
    while width < panel:
        width *= 2
    per_row = LANES // width
    ritz_rows = -(-columns // per_row)
    rows = -(-(run + ritz_rows) // SUBLANES) * SUBLANES
    tiles = nrow * ng
    vmem = pl.BlockSpec(memory_space=pltpu.VMEM)
    hbm = pl.BlockSpec(memory_space=pltpu.HBM)
    inputs = [
        pltpu.with_memory_space_constraint(value, pltpu.HBM)
        for value in (
            jnp.transpose(orbitals[0], (1, 0, 2)), jnp.transpose(region, (1, 0, 2)), potential_table, counts, ritz.T
        )
    ]
    order = [tiles - 1] + list(range(tiles - 1))
    packed_bytes = 4 * tiles * rows * LANES
    packed = pl.pallas_call(
        functools.partial(filter_kernel, ng, nrow, rows, run, width, cores),
        out_shape=jax.ShapeDtypeStruct((tiles * rows, LANES), jnp.float32),
        in_specs=[hbm] * 5,
        out_specs=vmem,
        scratch_shapes=[
            pltpu.VMEM((ys, planes, xs), jnp.float32),
            pltpu.VMEM((ys, planes, xs), jnp.int32),
            pltpu.SMEM(potential_table.shape, jnp.float32),
            pltpu.SMEM(counts.shape, jnp.int32),
            pltpu.VMEM((columns, panel), jnp.float32),
            pltpu.SemaphoreType.DMA((5,)),
        ],
        compiler_params=pltpu.CompilerParams(vmem_limit_bytes=2 * packed_bytes + 64 * cells + 2**20),
        name="chebyshev_filter",
    )(*inputs)
    got = lax.all_to_all(
        packed.reshape(tiles, rows, LANES), ("row", "grid"), split_axis=0, concat_axis=0, tiled=True,
        axis_index_groups=[order],
    )
    sum_shape = jax.ShapeDtypeStruct((panel, run * LANES), jnp.float32)
    if columns * width <= LANES and tiles <= 64 and panel == ng and panel <= 16:
        def partial_sums(distance):
            return pl.pallas_call(
                functools.partial(partial_kernel, nrow, ng, run, width, columns, cores, order, distance),
                out_shape=sum_shape,
                in_specs=[vmem],
                out_specs=vmem,
                scratch_shapes=[pltpu.VMEM((tiles, 1, LANES), jnp.float32)],
                compiler_params=pltpu.CompilerParams(vmem_limit_bytes=packed_bytes + 2**20),
                name="ritz_partial_sums",
            )(got)

    else:
        holders = panel // columns
        by_source = got[jnp.argsort(jnp.array(order))].reshape(nrow, ng, rows, LANES)
        fields = by_source[:, :, :run].reshape(tiles, run * LANES)
        blocks = by_source[:, :, run : run + ritz_rows].reshape(nrow, ng, ritz_rows * per_row, width)

        def partial_sums(distance):
            block = lax.axis_index("row") * cores + lax.rem(lax.axis_index("core") + distance, cores)
            mine = lax.dynamic_slice_in_dim(blocks, block * holders, holders, axis=1)
            return lax.dot_general(
                jnp.transpose(mine[:, :, :columns, :panel], (0, 3, 1, 2)).reshape(tiles, panel),
                fields,
                (((0,), (0,)), ((), ())),
                precision=lax.Precision.HIGHEST,
                preferred_element_type=jnp.float32,
            )

    terms = []
    for distance in range(1, cores):
        pairs = [(core, (core + distance) % cores) for core in range(cores)]
        terms.append(lax.ppermute(partial_sums(distance), "core", pairs))
    terms.append(partial_sums(0))
    return pl.pallas_call(
        sum_kernel,
        out_shape=sum_shape,
        in_specs=[vmem] * cores,
        out_specs=vmem,
        compiler_params=pltpu.CompilerParams(vmem_limit_bytes=4 * (cores + 1) * panel * run * LANES + 2**20),
        name="core_sum",
    )(*terms)


def solution(mesh):
    bands, ng = mesh.shape["band"], mesh.shape["grid"]
    cores = 2 if bands % 2 == 0 else 1
    nrow = bands // cores
    split = jax.sharding.Mesh(mesh.devices.reshape(nrow, cores, ng), ("row", "core", "grid"))
    return jax.shard_map(
        functools.partial(shards, nrow, cores, ng),
        mesh=split,
        in_specs=(P(("row", "core", "grid"), None, None, None), P(), P(), P(), P(("row", "core"), "grid")),
        out_specs=P(("row", "core"), "grid"),
        check_vma=False,
    )
```

time: 19.3 us -> 16 us (0.83)
  blocking collectives: 15.6 us -> 12.3 us
  Pallas kernels: 2.15 us -> 2.39 us
    all_to_all x1, blocking collectives: 15.6 us -> 12.3 us  [shards(): lax.all_to_all(packed.reshape(tiles, rows, LANES), ('row', 'grid'), split...]
  transfers between devices with their start and end apart: 1 -> 1, of which waited for: 1 -> 1; matrix products, arithmetic and copies ran while one was open for 0% -> 0% of each run, Pallas kernels for 0% -> 1%
where the time goes in v11:
time: 16 us; the launch traced here: 15.8 us
  blocking collectives  12.3 us (77%)
  Pallas kernels  2.39 us (15%)
  waiting for transfers between devices  0.99 us (6%)
    all_to_all x1, blocking collectives, shards(): lax.all_to_all(packed.reshape(tiles, rows, LANES), ('row', 'grid'), split...  12.3 us
    pallas_call x1, Pallas kernels, shards(): pl.pallas_call(functools.partial(filter_kernel, ng, nrow, rows, run, widt...  1.42 us
    ppermute x1, waiting for transfers between devices, shards(): terms.append(lax.ppermute(partial_sums(distance), 'core', pairs))  0.99 us
    pallas_call x1, Pallas kernels, shards(): pl.pallas_call(sum_kernel, out_shape=sum_shape, in_specs=[vmem] * cores,...  0.61 us
    pallas_call x2, Pallas kernels, partial_sums(): pl.pallas_call(functools.partial(partial_kernel, nrow, ng, run, width, co...  0.36 us
  transfers between devices with their start and end apart: 1, of which 1 were waited for; matrix products, arithmetic and copies ran while one was open for 0% of the time, Pallas kernels for 1%

profile of v11, /device:TPU:0, one launch (start us, length us, event | category | flops | bytes accessed | tf_op | source)
XLA Modules:
  0.0 15.8 jit_solution(16028347321168217113)
XLA Ops:
  0.0 1.4 %chebyshev_filter.1 = f32[128,128]{1,0:T(8,128)S(1)} custom-call(f32[6,8,128]{2,1,0:T(8,128)} %bitcast.7, s32[6,8,128]{2,1,0:T(8,128)} %bitcast.8, f32[16]{0:T(128)} %refs_2_.1, s32[4]{0:T(128)} %refs_3_.1, f32[4,8]{1,0:T(4,128)} %bitcast.9), custom_call_target="tpu_custom_call" | custom-call | tf_op jit(solution)/shard_map/chebyshev_filter/pallas_call | solution.py:184
  1.4 12.3 %all_to_all.5.got_ref = f32[16,8,128]{2,1,0:T(8,128)S(1)} all-to-all(f32[16,8,128]{2,1,0:T(8,128)S(1)} %bitcast.6), channel_id=1, replica_groups={{23,0,1,2,3,4,5,6,7,16,17,18,19,20,21,22},{31,8,9,10,11,12,13,14,15,24,..., dimensions={0} | all-to-all | bytes 131072 | tf_op jit(solution)/shard_map/all_to_all | solution.py:200
  13.8 0.2 %ritz_partial_sums.2 = f32[8,768]{1,0:T(8,128)S(1)} custom-call(f32[16,8,128]{2,1,0:T(8,128)S(1)} %all_to_all.5.got_ref), custom_call_target="tpu_custom_call" | custom-call | tf_op jit(solution)/shard_map/ritz_partial_sums/pallas_call | solution.py:207
  13.9 0.1 collective-permute-start
  14.0 0.2 %ritz_partial_sums.3.refs_1_ = f32[8,768]{1,0:T(8,128)S(1)} custom-call(f32[16,8,128]{2,1,0:T(8,128)S(1)} %all_to_all.5.got_ref), custom_call_target="tpu_custom_call" | custom-call | tf_op jit(solution)/shard_map/ritz_partial_sums/pallas_call | solution.py:207
  14.2 1.0 %collective-permute-done.refs_0_ = f32[8,768]{1,0:T(8,128)S(1)} collective-permute-done((f32[8,768]{1,0:T(8,128)S(1)}, f32[8,768]{1,0:T(8,128)S(1)}, u32[]{:S(2)}, u32[]{:S(2)}) %collective-permute-start) | collective-permute-done | bytes 24608 | tf_op jit(solution)/shard_map/ppermute | solution.py:237
  15.2 0.6 %core_sum.1 = f32[8,768]{1,0:T(8,128)} custom-call(f32[8,768]{1,0:T(8,128)S(1)} %collective-permute-done.refs_0_, f32[8,768]{1,0:T(8,128)S(1)} %ritz_partial_sums.3.refs_1_), custom_call_target="tpu_custom_call" | custom-call | tf_op jit(solution)/shard_map/core_sum/pallas_call | solution.py:239
Async XLA Ops:
  13.9 1.3 %collective-permute-start = (f32[8,768]{1,0:T(8,128)S(1)}, f32[8,768]{1,0:T(8,128)S(1)}, u32[]{:S(2)}, u32[]{:S(2)}) collective-permute-start(f32[8,768]{1,0:T(8,128)S(1)} %ritz_partial_sums.2), channel_id=1, source_target_pairs={{0,8},{8,0},{1,9},{9,1},{2,10},{10,2},{3,11},{11,3},{4,12},{12,4},... | collective-permute-start | bytes 73736 | tf_op jit(solution)/shard_map/ppermute | solution.py:237

commit v12 on v11

--- a/solution.py
+++ b/solution.py
@@ -67,28 +67,24 @@
     return results
 
 
-def filter_kernel(ng, copies, rows, run, width, cores, *refs):
-    sources, out_ref, held, sems = refs[:5], refs[5], refs[6:11], refs[11]
-    orb_ref, region_ref, table_ref, counts_ref, ritz_ref = held
+def filter_kernel(ng, copies, rows, run, width, cores, order, *refs):
+    sources, out_ref, held, sems, natural_ref = refs[:5], refs[5], refs[6:11], refs[11], refs[12]
+    orb_ref, region_ref, ritz_ref, table_ref, counts_ref = held
     transfers = [
         pltpu.make_async_copy(source, target, sems.at[index])
         for index, (source, target) in enumerate(zip(sources, held))
     ]
     for transfer in transfers:
         transfer.start()
+    for transfer in transfers:
+        transfer.wait()
     ys, planes, xs = orb_ref.shape
+    band_pos = lax.axis_index("row") * cores + lax.axis_index("core")
+    live = (lax.axis_index("grid") < counts_ref[band_pos]).astype(jnp.float32)
+
     centre_weight = 3.0 * COEFFICIENTS[0] + sum(pair_weights(n)[0] for n in (planes, ys, xs))
     scale = 2.0 / HALF
     hop = -0.5 / (SPACING * SPACING) * scale
-
-    def doubled(field, away):
-        return [diagonal[y] * field[y] + hop * away[y] for y in range(ys)]
-
-    transfers[0].wait()
-    previous = [orb_ref[y] for y in range(ys)]
-    away = off_diagonal(previous, planes, xs)
-    transfers[1].wait()
-    transfers[2].wait()
     diagonal = []
     for y in range(ys):
         region = region_ref[y]
@@ -96,25 +92,20 @@
         for index in range(table_ref.shape[0]):
             potential = jnp.where(region == index, table_ref[index], potential)
         diagonal.append(scale * potential + (hop * centre_weight - scale * CENTRE))
-    current = [0.5 * value for value in doubled(previous, away)]
+
+    def doubled(field):
+        away = off_diagonal(field, planes, xs)
+        return [diagonal[y] * field[y] + hop * away[y] for y in range(ys)]
+
+    previous = [orb_ref[y] * live for y in range(ys)]
+    current = [0.5 * value for value in doubled(previous)]
     for _ in range(DEGREE - 1):
-        away = off_diagonal(current, planes, xs)
-        following = [value - before for value, before in zip(doubled(current, away), previous)]
+        following = [value - before for value, before in zip(doubled(current), previous)]
         previous, current = current, following
-    transfers[3].wait()
-    transfers[4].wait()
-    band_pos = lax.axis_index("row") * cores + lax.axis_index("core")
-    live = (lax.axis_index("grid") < counts_ref[band_pos]).astype(jnp.float32)
 
     blocks = ys // run
     for y in range(ys):
-        masked = current[y] * live
-        for copy in range(copies):
-            first = copy * ng + y // run + 1
-            count = planes if copy < copies - 1 or y // run < blocks - 1 else planes - 1
-            out_ref[pl.ds(first * rows + y % run, count, stride=blocks * rows), :] = masked[:count]
-            if count < planes:
-                out_ref[pl.ds(y % run, 1), :] = masked[count:]
+        natural_ref[pl.ds((y // run) * rows + y % run, planes, stride=blocks * rows), :] = current[y]
 
     columns, panel = ritz_ref.shape
     per_row = LANES // width
@@ -125,7 +116,11 @@
                 [ritz_ref[pl.ds(row * per_row + slot, 1), :], jnp.zeros((1, LANES - panel), jnp.float32)], axis=1
             )
             line = line + (pltpu.roll(piece, slot * width, 1) if slot else piece)
-        out_ref[pl.ds(run + row, copies * ng, stride=rows), :] = jnp.broadcast_to(line, (copies * ng, LANES))
+        natural_ref[pl.ds(run + row, ng, stride=rows), :] = jnp.broadcast_to(line, (ng, LANES))
+    for copy in range(copies):
+        for tile in range(ng):
+            place = order.index(copy * ng + tile)
+            out_ref[pl.ds(place * rows, rows), :] = natural_ref[pl.ds(tile * rows, rows), :]
 
 
 def partial_kernel(nrow, ng, run, width, columns, cores, order, distance, got_ref, out_ref, ritz_ref):
@@ -176,30 +171,35 @@
     inputs = [
         pltpu.with_memory_space_constraint(value, pltpu.HBM)
         for value in (
-            jnp.transpose(orbitals[0], (1, 0, 2)), jnp.transpose(region, (1, 0, 2)), potential_table, counts, ritz.T
+            jnp.transpose(orbitals[0], (1, 0, 2)), jnp.transpose(region, (1, 0, 2)), ritz.T, potential_table, counts
         )
     ]
-    order = [tiles - 1] + list(range(tiles - 1))
+    others = sorted(range(1, tiles - 1), key=lambda chip: (chip % ng // 2, chip), reverse=True)
+    order = [tiles - 1, 0] + others
+    groups = [
+        [(chip // ng * cores + (group + chip // ng) % cores) * ng + chip % ng for chip in order] for group in range(cores)
+    ]
     packed_bytes = 4 * tiles * rows * LANES
     packed = pl.pallas_call(
-        functools.partial(filter_kernel, ng, nrow, rows, run, width, cores),
+        functools.partial(filter_kernel, ng, nrow, rows, run, width, cores, order),
         out_shape=jax.ShapeDtypeStruct((tiles * rows, LANES), jnp.float32),
         in_specs=[hbm] * 5,
         out_specs=vmem,
         scratch_shapes=[
             pltpu.VMEM((ys, planes, xs), jnp.float32),
             pltpu.VMEM((ys, planes, xs), jnp.int32),
+            pltpu.VMEM((columns, panel), jnp.float32),
             pltpu.SMEM(potential_table.shape, jnp.float32),
             pltpu.SMEM(counts.shape, jnp.int32),
-            pltpu.VMEM((columns, panel), jnp.float32),
             pltpu.SemaphoreType.DMA((5,)),
+            pltpu.VMEM((ng * rows, LANES), jnp.float32),
         ],
         compiler_params=pltpu.CompilerParams(vmem_limit_bytes=2 * packed_bytes + 64 * cells + 2**20),
         name="chebyshev_filter",
     )(*inputs)
     got = lax.all_to_all(
-        packed.reshape(tiles, rows, LANES), ("row", "grid"), split_axis=0, concat_axis=0, tiled=True,
-        axis_index_groups=[order],
+        packed.reshape(tiles, rows, LANES), ("row", "core", "grid"), split_axis=0, concat_axis=0, tiled=True,
+        axis_index_groups=groups,
     )
     sum_shape = jax.ShapeDtypeStruct((panel, run * LANES), jnp.float32)
     if columns * width <= LANES and tiles <= 64 and panel == ng and panel <= 16:

time: 16 us -> 16.1 us (level)
  no operation moved by 1% of the time
where the time goes in v12:
time: 16.1 us; the launch traced here: 15.9 us
  blocking collectives  12.4 us (77%)
  Pallas kernels  2.32 us (14%)
  waiting for transfers between devices  0.92 us (6%)
    all_to_all x1, blocking collectives, shards(): lax.all_to_all(packed.reshape(tiles, rows, LANES), ('row', 'core', 'grid'...  12.4 us
    pallas_call x1, Pallas kernels, shards(): pl.pallas_call(functools.partial(filter_kernel, ng, nrow, rows, run, widt...  1.35 us
    ppermute x1, waiting for transfers between devices, shards(): terms.append(lax.ppermute(partial_sums(distance), 'core', pairs))  0.92 us
    pallas_call x1, Pallas kernels, shards(): pl.pallas_call(sum_kernel, out_shape=sum_shape, in_specs=[vmem] * cores,...  0.61 us
    pallas_call x2, Pallas kernels, partial_sums(): pl.pallas_call(functools.partial(partial_kernel, nrow, ng, run, width, co...  0.36 us
  transfers between devices with their start and end apart: 1, of which 1 were waited for; matrix products, arithmetic and copies ran while one was open for 0% of the time, Pallas kernels for 1%

profile of v12, /device:TPU:0, one launch (start us, length us, event | category | flops | bytes accessed | tf_op | source)
XLA Modules:
  0.0 15.9 jit_solution(1257992522288333618)
XLA Ops:
  0.0 1.4 %chebyshev_filter.1 = f32[128,128]{1,0:T(8,128)S(1)} custom-call(f32[6,8,128]{2,1,0:T(8,128)} %bitcast.7, s32[6,8,128]{2,1,0:T(8,128)} %bitcast.8, f32[4,8]{1,0:T(4,128)} %bitcast.9, f32[16]{0:T(128)} %refs_3_.1, s32[4]{0:T(128)} %refs_4_.1), custom_call_target="tpu_custom_call" | custom-call | tf_op jit(solution)/shard_map/chebyshev_filter/pallas_call | solution.py:183
  1.4 12.4 %all_to_all.5.got_ref = f32[16,8,128]{2,1,0:T(8,128)S(1)} all-to-all(f32[16,8,128]{2,1,0:T(8,128)S(1)} %bitcast.6), channel_id=1, replica_groups={{31,0,30,7,6,29,28,5,4,27,26,3,2,25,24,1},{23,8,22,15,14,21,20,13,12,19..., dimensions={0} | all-to-all | bytes 131072 | tf_op jit(solution)/shard_map/all_to_all | solution.py:200
  13.8 0.2 %ritz_partial_sums.2 = f32[8,768]{1,0:T(8,128)S(1)} custom-call(f32[16,8,128]{2,1,0:T(8,128)S(1)} %all_to_all.5.got_ref), custom_call_target="tpu_custom_call" | custom-call | tf_op jit(solution)/shard_map/ritz_partial_sums/pallas_call | solution.py:207
  14.0 0.2 collective-permute-start
  14.1 0.2 %ritz_partial_sums.3.refs_1_ = f32[8,768]{1,0:T(8,128)S(1)} custom-call(f32[16,8,128]{2,1,0:T(8,128)S(1)} %all_to_all.5.got_ref), custom_call_target="tpu_custom_call" | custom-call | tf_op jit(solution)/shard_map/ritz_partial_sums/pallas_call | solution.py:207
  14.3 0.9 %collective-permute-done.refs_0_ = f32[8,768]{1,0:T(8,128)S(1)} collective-permute-done((f32[8,768]{1,0:T(8,128)S(1)}, f32[8,768]{1,0:T(8,128)S(1)}, u32[]{:S(2)}, u32[]{:S(2)}) %collective-permute-start) | collective-permute-done | bytes 24608 | tf_op jit(solution)/shard_map/ppermute | solution.py:237
  15.2 0.6 %core_sum.1 = f32[8,768]{1,0:T(8,128)} custom-call(f32[8,768]{1,0:T(8,128)S(1)} %collective-permute-done.refs_0_, f32[8,768]{1,0:T(8,128)S(1)} %ritz_partial_sums.3.refs_1_), custom_call_target="tpu_custom_call" | custom-call | tf_op jit(solution)/shard_map/core_sum/pallas_call | solution.py:239
Async XLA Ops:
  14.0 1.3 %collective-permute-start = (f32[8,768]{1,0:T(8,128)S(1)}, f32[8,768]{1,0:T(8,128)S(1)}, u32[]{:S(2)}, u32[]{:S(2)}) collective-permute-start(f32[8,768]{1,0:T(8,128)S(1)} %ritz_partial_sums.2), channel_id=1, source_target_pairs={{0,8},{8,0},{1,9},{9,1},{2,10},{10,2},{3,11},{11,3},{4,12},{12,4},... | collective-permute-start | bytes 73736 | tf_op jit(solution)/shard_map/ppermute | solution.py:237

commit v13 on v12

--- a/solution.py
+++ b/solution.py
@@ -44,25 +44,33 @@
     return weights[0], pairs
 
 
-def off_diagonal(field, planes, xs):
+def along_x(tile):
+    length = tile.shape[1]
+    near = {-1: pltpu.roll(tile, length - 1, 1), 0: tile, 1: pltpu.roll(tile, 1, 1)}
+    total = COEFFICIENTS[1] * (near[-1] + near[1])
+    for m in (-2, -1, 1, 2):
+        parts = [COEFFICIENTS[abs(3 * m + r)] * near[r] for r in (-1, 0, 1) if abs(3 * m + r) <= 6]
+        total = total + pltpu.roll(functools.reduce(jnp.add, parts), (3 * m) % length, 1)
+    return total
+
+
+def along_planes(tile):
+    _, pairs = pair_weights(tile.shape[0])
+    one, two, three, four = [weight for _, weight in pairs]
+    opposite = pltpu.roll(tile, 4, 0)
+    odd = one * tile + three * opposite
+    even = two * (tile + opposite)
+    return four * opposite + pltpu.roll(odd, 1, 0) + pltpu.roll(odd, 7, 0) + pltpu.roll(even, 2, 0)
+
+
+def off_diagonal(field):
     ys = len(field)
-    _, x_pairs = pair_weights(xs)
     _, y_pairs = pair_weights(ys)
-    _, p_pairs = pair_weights(planes)
     results = []
     for y in range(ys):
-        tile = field[y]
-        total = None
-        terms = []
-        for shifts, weight in x_pairs:
-            terms.append((weight, [pltpu.roll(tile, shift, 1) for shift in shifts]))
-        for shifts, weight in p_pairs:
-            terms.append((weight, [pltpu.roll(tile, shift, 0) for shift in shifts]))
+        total = along_x(field[y]) + along_planes(field[y])
         for shifts, weight in y_pairs:
-            terms.append((weight, [field[(y - shift) % ys] for shift in shifts]))
-        for weight, parts in terms:
-            value = weight * functools.reduce(jnp.add, parts)
-            total = value if total is None else total + value
+            total = total + weight * functools.reduce(jnp.add, [field[(y - shift) % ys] for shift in shifts])
         results.append(total)
     return results
 
@@ -94,7 +102,7 @@
         diagonal.append(scale * potential + (hop * centre_weight - scale * CENTRE))
 
     def doubled(field):
-        away = off_diagonal(field, planes, xs)
+        away = off_diagonal(field)
         return [diagonal[y] * field[y] + hop * away[y] for y in range(ys)]
 
     previous = [orb_ref[y] * live for y in range(ys)]
@@ -174,11 +182,8 @@
             jnp.transpose(orbitals[0], (1, 0, 2)), jnp.transpose(region, (1, 0, 2)), ritz.T, potential_table, counts
         )
     ]
-    others = sorted(range(1, tiles - 1), key=lambda chip: (chip % ng // 2, chip), reverse=True)
-    order = [tiles - 1, 0] + others
-    groups = [
-        [(chip // ng * cores + (group + chip // ng) % cores) * ng + chip % ng for chip in order] for group in range(cores)
-    ]
+    late = sorted(range(tiles), key=lambda place: (place % ng // (ng // 2), place // ng, place % ng), reverse=True)
+    order = [place for pair in zip(late, late[::-1]) for place in pair][:tiles]
     packed_bytes = 4 * tiles * rows * LANES
     packed = pl.pallas_call(
         functools.partial(filter_kernel, ng, nrow, rows, run, width, cores, order),
@@ -198,8 +203,8 @@
         name="chebyshev_filter",
     )(*inputs)
     got = lax.all_to_all(
-        packed.reshape(tiles, rows, LANES), ("row", "core", "grid"), split_axis=0, concat_axis=0, tiled=True,
-        axis_index_groups=groups,
+        packed.reshape(tiles, rows, LANES), ("row", "grid"), split_axis=0, concat_axis=0, tiled=True,
+        axis_index_groups=[order],
     )
     sum_shape = jax.ShapeDtypeStruct((panel, run * LANES), jnp.float32)
     if columns * width <= LANES and tiles <= 64 and panel == ng and panel <= 16:

time: 16.1 us -> 16.1 us (level)
  Pallas kernels: 2.32 us -> 2.53 us
    pallas_call x1, Pallas kernels: 1.35 us -> 1.55 us  [shards(): pl.pallas_call(functools.partial(filter_kernel, ng, nrow, rows, run, widt...]
where the time goes in v13:
time: 16.1 us; the launch traced here: 15.9 us
  blocking collectives  12.3 us (76%)
  Pallas kernels  2.53 us (16%)
  waiting for transfers between devices  0.99 us (6%)
    all_to_all x1, blocking collectives, shards(): lax.all_to_all(packed.reshape(tiles, rows, LANES), ('row', 'grid'), split...  12.3 us
    pallas_call x1, Pallas kernels, shards(): pl.pallas_call(functools.partial(filter_kernel, ng, nrow, rows, run, widt...  1.55 us
    ppermute x1, waiting for transfers between devices, shards(): terms.append(lax.ppermute(partial_sums(distance), 'core', pairs))  0.99 us
    pallas_call x1, Pallas kernels, shards(): pl.pallas_call(sum_kernel, out_shape=sum_shape, in_specs=[vmem] * cores,...  0.61 us
    pallas_call x2, Pallas kernels, partial_sums(): pl.pallas_call(functools.partial(partial_kernel, nrow, ng, run, width, co...  0.36 us
  transfers between devices with their start and end apart: 1, of which 1 were waited for; matrix products, arithmetic and copies ran while one was open for 0% of the time, Pallas kernels for 1%

profile of v13, /device:TPU:0, one launch (start us, length us, event | category | flops | bytes accessed | tf_op | source)
XLA Modules:
  0.0 15.9 jit_solution(17933584211001153336)
XLA Ops:
  0.0 1.6 %chebyshev_filter.1 = f32[128,128]{1,0:T(8,128)S(1)} custom-call(f32[6,8,128]{2,1,0:T(8,128)} %bitcast.7, s32[6,8,128]{2,1,0:T(8,128)} %bitcast.8, f32[4,8]{1,0:T(4,128)} %bitcast.9, f32[16]{0:T(128)} %refs_3_.1, s32[4]{0:T(128)} %refs_4_.1), custom_call_target="tpu_custom_call" | custom-call | tf_op jit(solution)/shard_map/chebyshev_filter/pallas_call | solution.py:188
  1.6 12.3 %all_to_all.5.got_ref = f32[16,8,128]{2,1,0:T(8,128)S(1)} all-to-all(f32[16,8,128]{2,1,0:T(8,128)S(1)} %bitcast.6), channel_id=1, replica_groups={{23,0,22,1,21,2,20,3,7,16,6,17,5,18,4,19},{31,8,30,9,29,10,28,11,15,24,..., dimensions={0} | all-to-all | bytes 131072 | tf_op jit(solution)/shard_map/all_to_all | solution.py:205
  13.9 0.2 %ritz_partial_sums.2 = f32[8,768]{1,0:T(8,128)S(1)} custom-call(f32[16,8,128]{2,1,0:T(8,128)S(1)} %all_to_all.5.got_ref), custom_call_target="tpu_custom_call" | custom-call | tf_op jit(solution)/shard_map/ritz_partial_sums/pallas_call | solution.py:212
  14.0 0.1 collective-permute-start
  14.1 0.2 %ritz_partial_sums.3.refs_1_ = f32[8,768]{1,0:T(8,128)S(1)} custom-call(f32[16,8,128]{2,1,0:T(8,128)S(1)} %all_to_all.5.got_ref), custom_call_target="tpu_custom_call" | custom-call | tf_op jit(solution)/shard_map/ritz_partial_sums/pallas_call | solution.py:212
  14.3 1.0 %collective-permute-done.refs_0_ = f32[8,768]{1,0:T(8,128)S(1)} collective-permute-done((f32[8,768]{1,0:T(8,128)S(1)}, f32[8,768]{1,0:T(8,128)S(1)}, u32[]{:S(2)}, u32[]{:S(2)}) %collective-permute-start) | collective-permute-done | bytes 24608 | tf_op jit(solution)/shard_map/ppermute | solution.py:242
  15.3 0.6 %core_sum.1 = f32[8,768]{1,0:T(8,128)} custom-call(f32[8,768]{1,0:T(8,128)S(1)} %collective-permute-done.refs_0_, f32[8,768]{1,0:T(8,128)S(1)} %ritz_partial_sums.3.refs_1_), custom_call_target="tpu_custom_call" | custom-call | tf_op jit(solution)/shard_map/core_sum/pallas_call | solution.py:244
Async XLA Ops:
  14.0 1.3 %collective-permute-start = (f32[8,768]{1,0:T(8,128)S(1)}, f32[8,768]{1,0:T(8,128)S(1)}, u32[]{:S(2)}, u32[]{:S(2)}) collective-permute-start(f32[8,768]{1,0:T(8,128)S(1)} %ritz_partial_sums.2), channel_id=1, source_target_pairs={{0,8},{8,0},{1,9},{9,1},{2,10},{10,2},{3,11},{11,3},{4,12},{12,4},... | collective-permute-start | bytes 73736 | tf_op jit(solution)/shard_map/ppermute | solution.py:242

commit v14 on v12

--- a/solution.py
+++ b/solution.py
@@ -176,9 +176,6 @@
     ]
     others = sorted(range(1, tiles - 1), key=lambda chip: (chip % ng // 2, chip), reverse=True)
     order = [tiles - 1, 0] + others
-    groups = [
-        [(chip // ng * cores + (group + chip // ng) % cores) * ng + chip % ng for chip in order] for group in range(cores)
-    ]
     packed_bytes = 4 * tiles * rows * LANES
     packed = pl.pallas_call(
         functools.partial(filter_kernel, ng, nrow, rows, run, width, cores, order),
@@ -198,8 +195,8 @@
         name="chebyshev_filter",
     )(*inputs)
     got = lax.all_to_all(
-        packed.reshape(tiles, rows, LANES), ("row", "core", "grid"), split_axis=0, concat_axis=0, tiled=True,
-        axis_index_groups=groups,
+        packed.reshape(tiles, rows, LANES), ("row", "grid"), split_axis=0, concat_axis=0, tiled=True,
+        axis_index_groups=[order],
     )
     sum_shape = jax.ShapeDtypeStruct((panel, run * LANES), jnp.float32)
     if columns * width <= LANES and tiles <= 64 and panel == ng and panel <= 16:

time: 16.1 us -> 16 us (level)
  no operation moved by 1% of the time
where the time goes in v14:
time: 16 us; the launch traced here: 15.8 us
  blocking collectives  12.4 us (78%)
  Pallas kernels  2.32 us (14%)
  waiting for transfers between devices  0.99 us (6%)
    all_to_all x1, blocking collectives, shards(): lax.all_to_all(packed.reshape(tiles, rows, LANES), ('row', 'grid'), split...  12.4 us
    pallas_call x1, Pallas kernels, shards(): pl.pallas_call(functools.partial(filter_kernel, ng, nrow, rows, run, widt...  1.35 us
    ppermute x1, waiting for transfers between devices, shards(): terms.append(lax.ppermute(partial_sums(distance), 'core', pairs))  0.99 us
    pallas_call x1, Pallas kernels, shards(): pl.pallas_call(sum_kernel, out_shape=sum_shape, in_specs=[vmem] * cores,...  0.61 us
    pallas_call x2, Pallas kernels, partial_sums(): pl.pallas_call(functools.partial(partial_kernel, nrow, ng, run, width, co...  0.36 us
  transfers between devices with their start and end apart: 1, of which 1 were waited for; matrix products, arithmetic and copies ran while one was open for 0% of the time, Pallas kernels for 1%

profile of v14, /device:TPU:0, one launch (start us, length us, event | category | flops | bytes accessed | tf_op | source)
XLA Modules:
  0.0 15.8 jit_solution(14187470461099540588)
XLA Ops:
  0.0 1.4 %chebyshev_filter.1 = f32[128,128]{1,0:T(8,128)S(1)} custom-call(f32[6,8,128]{2,1,0:T(8,128)} %bitcast.7, s32[6,8,128]{2,1,0:T(8,128)} %bitcast.8, f32[4,8]{1,0:T(4,128)} %bitcast.9, f32[16]{0:T(128)} %refs_3_.1, s32[4]{0:T(128)} %refs_4_.1), custom_call_target="tpu_custom_call" | custom-call | tf_op jit(solution)/shard_map/chebyshev_filter/pallas_call | solution.py:180
  1.4 12.4 %all_to_all.5.got_ref = f32[16,8,128]{2,1,0:T(8,128)S(1)} all-to-all(f32[16,8,128]{2,1,0:T(8,128)S(1)} %bitcast.6), channel_id=1, replica_groups={{23,0,22,7,6,21,20,5,4,19,18,3,2,17,16,1},{31,8,30,15,14,29,28,13,12,27..., dimensions={0} | all-to-all | bytes 131072 | tf_op jit(solution)/shard_map/all_to_all | solution.py:197
  13.7 0.2 %ritz_partial_sums.2 = f32[8,768]{1,0:T(8,128)S(1)} custom-call(f32[16,8,128]{2,1,0:T(8,128)S(1)} %all_to_all.5.got_ref), custom_call_target="tpu_custom_call" | custom-call | tf_op jit(solution)/shard_map/ritz_partial_sums/pallas_call | solution.py:204
  13.9 0.1 collective-permute-start
  14.0 0.2 %ritz_partial_sums.3.refs_1_ = f32[8,768]{1,0:T(8,128)S(1)} custom-call(f32[16,8,128]{2,1,0:T(8,128)S(1)} %all_to_all.5.got_ref), custom_call_target="tpu_custom_call" | custom-call | tf_op jit(solution)/shard_map/ritz_partial_sums/pallas_call | solution.py:204
  14.2 1.0 %collective-permute-done.refs_0_ = f32[8,768]{1,0:T(8,128)S(1)} collective-permute-done((f32[8,768]{1,0:T(8,128)S(1)}, f32[8,768]{1,0:T(8,128)S(1)}, u32[]{:S(2)}, u32[]{:S(2)}) %collective-permute-start) | collective-permute-done | bytes 24608 | tf_op jit(solution)/shard_map/ppermute | solution.py:234
  15.2 0.6 %core_sum.1 = f32[8,768]{1,0:T(8,128)} custom-call(f32[8,768]{1,0:T(8,128)S(1)} %collective-permute-done.refs_0_, f32[8,768]{1,0:T(8,128)S(1)} %ritz_partial_sums.3.refs_1_), custom_call_target="tpu_custom_call" | custom-call | tf_op jit(solution)/shard_map/core_sum/pallas_call | solution.py:236
Async XLA Ops:
  13.9 1.3 %collective-permute-start = (f32[8,768]{1,0:T(8,128)S(1)}, f32[8,768]{1,0:T(8,128)S(1)}, u32[]{:S(2)}, u32[]{:S(2)}) collective-permute-start(f32[8,768]{1,0:T(8,128)S(1)} %ritz_partial_sums.2), channel_id=1, source_target_pairs={{0,8},{8,0},{1,9},{9,1},{2,10},{10,2},{3,11},{11,3},{4,12},{12,4},... | collective-permute-start | bytes 73736 | tf_op jit(solution)/shard_map/ppermute | solution.py:234

commit v15 on v14

--- a/solution.py
+++ b/solution.py
@@ -44,32 +44,30 @@
     return weights[0], pairs
 
 
-def off_diagonal(field, planes, xs):
+def apply(field, diagonal, hop, before):
     ys = len(field)
-    _, x_pairs = pair_weights(xs)
-    _, y_pairs = pair_weights(ys)
-    _, p_pairs = pair_weights(planes)
+    planes, xs = field[0].shape
+    along_y, along_planes, along_x = [pair_weights(length)[1] for length in (ys, planes, xs)]
     results = []
     for y in range(ys):
         tile = field[y]
-        total = None
-        terms = []
-        for shifts, weight in x_pairs:
-            terms.append((weight, [pltpu.roll(tile, shift, 1) for shift in shifts]))
-        for shifts, weight in p_pairs:
-            terms.append((weight, [pltpu.roll(tile, shift, 0) for shift in shifts]))
-        for shifts, weight in y_pairs:
-            terms.append((weight, [field[(y - shift) % ys] for shift in shifts]))
-        for weight, parts in terms:
-            value = weight * functools.reduce(jnp.add, parts)
-            total = value if total is None else total + value
+        total = diagonal[y] * tile
+        if before is not None:
+            total = total - before[y]
+        for shifts, weight in along_y:
+            total = total + (hop * weight) * functools.reduce(jnp.add, [field[(y - shift) % ys] for shift in shifts])
+        for pairs, axis in ((along_planes, 0), (along_x, 1)):
+            for shifts, weight in pairs:
+                total = total + (hop * weight) * functools.reduce(
+                    jnp.add, [pltpu.roll(tile, shift, axis) for shift in shifts]
+                )
         results.append(total)
     return results
 
 
 def filter_kernel(ng, copies, rows, run, width, cores, order, *refs):
     sources, out_ref, held, sems, natural_ref = refs[:5], refs[5], refs[6:11], refs[11], refs[12]
-    orb_ref, region_ref, ritz_ref, table_ref, counts_ref = held
+    orb_ref, region_ref, table_ref, counts_ref, ritz_ref = held
     transfers = [
         pltpu.make_async_copy(source, target, sems.at[index])
         for index, (source, target) in enumerate(zip(sources, held))
@@ -79,8 +77,16 @@
     for transfer in transfers:
         transfer.wait()
     ys, planes, xs = orb_ref.shape
-    band_pos = lax.axis_index("row") * cores + lax.axis_index("core")
-    live = (lax.axis_index("grid") < counts_ref[band_pos]).astype(jnp.float32)
+    columns, panel = ritz_ref.shape
+    per_row = LANES // width
+    for row in range(-(-columns // per_row)):
+        line = jnp.zeros((1, LANES), jnp.float32)
+        for slot in range(min(per_row, columns - row * per_row)):
+            piece = jnp.concatenate(
+                [ritz_ref[pl.ds(row * per_row + slot, 1), :], jnp.zeros((1, LANES - panel), jnp.float32)], axis=1
+            )
+            line = line + (pltpu.roll(piece, slot * width, 1) if slot else piece)
+        natural_ref[pl.ds(run + row, ng, stride=rows), :] = jnp.broadcast_to(line, (ng, LANES))
 
     centre_weight = 3.0 * COEFFICIENTS[0] + sum(pair_weights(n)[0] for n in (planes, ys, xs))
     scale = 2.0 / HALF
@@ -92,31 +98,16 @@
         for index in range(table_ref.shape[0]):
             potential = jnp.where(region == index, table_ref[index], potential)
         diagonal.append(scale * potential + (hop * centre_weight - scale * CENTRE))
-
-    def doubled(field):
-        away = off_diagonal(field, planes, xs)
-        return [diagonal[y] * field[y] + hop * away[y] for y in range(ys)]
-
-    previous = [orb_ref[y] * live for y in range(ys)]
-    current = [0.5 * value for value in doubled(previous)]
+    band_pos = lax.axis_index("row") * cores + lax.axis_index("core")
+    live = (lax.axis_index("grid") < counts_ref[band_pos]).astype(jnp.float32)
+    previous = [live * orb_ref[y] for y in range(ys)]
+    current = apply(previous, [0.5 * value for value in diagonal], 0.5 * hop, None)
     for _ in range(DEGREE - 1):
-        following = [value - before for value, before in zip(doubled(current), previous)]
-        previous, current = current, following
+        previous, current = current, apply(current, diagonal, hop, previous)
 
     blocks = ys // run
     for y in range(ys):
         natural_ref[pl.ds((y // run) * rows + y % run, planes, stride=blocks * rows), :] = current[y]
-
-    columns, panel = ritz_ref.shape
-    per_row = LANES // width
-    for row in range(-(-columns // per_row)):
-        line = jnp.zeros((1, LANES), jnp.float32)
-        for slot in range(min(per_row, columns - row * per_row)):
-            piece = jnp.concatenate(
-                [ritz_ref[pl.ds(row * per_row + slot, 1), :], jnp.zeros((1, LANES - panel), jnp.float32)], axis=1
-            )
-            line = line + (pltpu.roll(piece, slot * width, 1) if slot else piece)
-        natural_ref[pl.ds(run + row, ng, stride=rows), :] = jnp.broadcast_to(line, (ng, LANES))
     for copy in range(copies):
         for tile in range(ng):
             place = order.index(copy * ng + tile)
@@ -129,8 +120,6 @@
     wanted = out_ref.shape[0]
     holders = wanted // columns
     sublane = lax.broadcasted_iota(jnp.int32, (wanted, LANES), 0)
-    lane = lax.broadcasted_iota(jnp.int32, (wanted, LANES), 1)
-    own = lane // width == sublane % columns
     block = lax.axis_index("row") * cores + lax.rem(lax.axis_index("core") + distance, cores)
     acc = [jnp.zeros((wanted, LANES), jnp.float32) for _ in range(run)]
     for row in range(nrow):
@@ -138,12 +127,8 @@
         for k in range(holders):
             line = ritz_ref[row * ng + block * holders + k]
             lines = jnp.where(sublane // columns == k, jnp.broadcast_to(line, (wanted, LANES)), lines)
-        lines = jnp.where(own, lines, 0.0)
-        weights = lines
-        for slot in range(1, columns):
-            weights = weights + pltpu.roll(lines, LANES - slot * width, 1)
         for r in range(ng):
-            weight = jnp.broadcast_to(weights[:, r : r + 1], (wanted, LANES))
+            weight = jnp.take_along_axis(lines, sublane % columns * width + r, axis=1)
             for y in range(run):
                 acc[y] = acc[y] + weight * got_ref[order.index(row * ng + r), pl.ds(y, 1), :]
     for y in range(run):
@@ -171,11 +156,11 @@
     inputs = [
         pltpu.with_memory_space_constraint(value, pltpu.HBM)
         for value in (
-            jnp.transpose(orbitals[0], (1, 0, 2)), jnp.transpose(region, (1, 0, 2)), ritz.T, potential_table, counts
+            jnp.transpose(orbitals[0], (1, 0, 2)), jnp.transpose(region, (1, 0, 2)), potential_table, counts, ritz.T
         )
     ]
-    others = sorted(range(1, tiles - 1), key=lambda chip: (chip % ng // 2, chip), reverse=True)
-    order = [tiles - 1, 0] + others
+    late = sorted(range(tiles), key=lambda place: (place % ng // (ng // 2), place // ng, place % ng), reverse=True)
+    order = [place for pair in zip(late, late[::-1]) for place in pair][:tiles]
     packed_bytes = 4 * tiles * rows * LANES
     packed = pl.pallas_call(
         functools.partial(filter_kernel, ng, nrow, rows, run, width, cores, order),
@@ -185,9 +170,9 @@
         scratch_shapes=[
             pltpu.VMEM((ys, planes, xs), jnp.float32),
             pltpu.VMEM((ys, planes, xs), jnp.int32),
-            pltpu.VMEM((columns, panel), jnp.float32),
             pltpu.SMEM(potential_table.shape, jnp.float32),
             pltpu.SMEM(counts.shape, jnp.int32),
+            pltpu.VMEM((columns, panel), jnp.float32),
             pltpu.SemaphoreType.DMA((5,)),
             pltpu.VMEM((ng * rows, LANES), jnp.float32),
         ],

time: 16 us -> 15.8 us (0.988)
  Pallas kernels: 2.32 us -> 2.15 us
where the time goes in v15:
time: 15.8 us; the launch traced here: 15.6 us
  blocking collectives  12.3 us (78%)
  Pallas kernels  2.15 us (14%)
  waiting for transfers between devices  1.05 us (7%)
    all_to_all x1, blocking collectives, shards(): lax.all_to_all(packed.reshape(tiles, rows, LANES), ('row', 'grid'), split...  12.3 us
    pallas_call x1, Pallas kernels, shards(): pl.pallas_call(functools.partial(filter_kernel, ng, nrow, rows, run, widt...  1.3 us
    ppermute x1, waiting for transfers between devices, shards(): terms.append(lax.ppermute(partial_sums(distance), 'core', pairs))  1.05 us
    pallas_call x1, Pallas kernels, shards(): pl.pallas_call(sum_kernel, out_shape=sum_shape, in_specs=[vmem] * cores,...  0.61 us
  transfers between devices with their start and end apart: 1, of which 1 were waited for; matrix products, arithmetic and copies ran while one was open for 0% of the time, Pallas kernels for 1%

profile of v15, /device:TPU:0, one launch (start us, length us, event | category | flops | bytes accessed | tf_op | source)
XLA Modules:
  0.0 15.6 jit_solution(13831608489453338923)
XLA Ops:
  0.0 1.3 %chebyshev_filter.1 = f32[128,128]{1,0:T(8,128)S(1)} custom-call(f32[6,8,128]{2,1,0:T(8,128)} %bitcast.7, s32[6,8,128]{2,1,0:T(8,128)} %bitcast.8, f32[16]{0:T(128)} %refs_2_.1, s32[4]{0:T(128)} %refs_3_.1, f32[4,8]{1,0:T(4,128)} %bitcast.9), custom_call_target="tpu_custom_call" | custom-call | tf_op jit(solution)/shard_map/chebyshev_filter/pallas_call | solution.py:165
  1.3 12.3 %all_to_all.5.got_ref = f32[16,8,128]{2,1,0:T(8,128)S(1)} all-to-all(f32[16,8,128]{2,1,0:T(8,128)S(1)} %bitcast.6), channel_id=1, replica_groups={{23,0,22,1,21,2,20,3,7,16,6,17,5,18,4,19},{31,8,30,9,29,10,28,11,15,24,..., dimensions={0} | all-to-all | bytes 131072 | tf_op jit(solution)/shard_map/all_to_all | solution.py:182
  13.6 0.1 ritz_partial_sums.2
  13.7 0.1 collective-permute-start
  13.8 0.1 ritz_partial_sums.3.refs_1_
  13.9 1.1 %collective-permute-done.refs_0_ = f32[8,768]{1,0:T(8,128)S(1)} collective-permute-done((f32[8,768]{1,0:T(8,128)S(1)}, f32[8,768]{1,0:T(8,128)S(1)}, u32[]{:S(2)}, u32[]{:S(2)}) %collective-permute-start) | collective-permute-done | bytes 24608 | tf_op jit(solution)/shard_map/ppermute | solution.py:219
  15.0 0.6 %core_sum.1 = f32[8,768]{1,0:T(8,128)} custom-call(f32[8,768]{1,0:T(8,128)S(1)} %collective-permute-done.refs_0_, f32[8,768]{1,0:T(8,128)S(1)} %ritz_partial_sums.3.refs_1_), custom_call_target="tpu_custom_call" | custom-call | tf_op jit(solution)/shard_map/core_sum/pallas_call | solution.py:221
Async XLA Ops:
  13.7 1.3 %collective-permute-start = (f32[8,768]{1,0:T(8,128)S(1)}, f32[8,768]{1,0:T(8,128)S(1)}, u32[]{:S(2)}, u32[]{:S(2)}) collective-permute-start(f32[8,768]{1,0:T(8,128)S(1)} %ritz_partial_sums.2), channel_id=1, source_target_pairs={{0,8},{8,0},{1,9},{9,1},{2,10},{10,2},{3,11},{11,3},{4,12},{12,4},... | collective-permute-start | bytes 73736 | tf_op jit(solution)/shard_map/ppermute | solution.py:219

commit v16 on v15

v16 whole, which is shorter than its diff:
```python
import functools

import jax
import jax.numpy as jnp
from jax import lax
from jax.experimental import pallas as pl
from jax.experimental.pallas import tpu as pltpu
from jax.sharding import PartitionSpec as P

DEGREE = 4

COEFFICIENTS = (
    -5369.0 / 1800.0,
    12.0 / 7.0,
    -15.0 / 56.0,
    10.0 / 189.0,
    -1.0 / 112.0,
    2.0 / 1925.0,
    -1.0 / 16632.0,
)
SPACING = 0.5
LOWER = 6.0
UPPER = 46.0
HALF = (UPPER - LOWER) / 2.0
CENTRE = (UPPER + LOWER) / 2.0
LANES = 128
SUBLANES = 8


def ring_weights(length):
    weights = [0.0] * length
    for offset in range(1, 7):
        weights[offset % length] += COEFFICIENTS[offset]
        weights[-offset % length] += COEFFICIENTS[offset]
    return weights


def pair_weights(length):
    weights = ring_weights(length)
    pairs = []
    for distance in range(1, length // 2 + 1):
        if weights[distance] != 0.0:
            pairs.append((sorted({distance, length - distance}), weights[distance]))
    return weights[0], pairs


def apply(field, diagonal, hop, before):
    ys = len(field)
    planes, xs = field[0].shape
    along_y, along_planes, along_x = [pair_weights(length)[1] for length in (ys, planes, xs)]
    results = []
    for y in range(ys):
        tile = field[y]
        total = diagonal[y] * tile
        if before is not None:
            total = total - before[y]
        for shifts, weight in along_y:
            total = total + (hop * weight) * functools.reduce(jnp.add, [field[(y - shift) % ys] for shift in shifts])
        for pairs, axis in ((along_planes, 0), (along_x, 1)):
            for shifts, weight in pairs:
                total = total + (hop * weight) * functools.reduce(
                    jnp.add, [pltpu.roll(tile, shift, axis) for shift in shifts]
                )
        results.append(total)
    return results


def filtered_tiles(rows, run, width, sources, held, sems, natural_ref):
    orb_ref, region_ref, table_ref, counts_ref, ritz_ref = held
    transfers = [
        pltpu.make_async_copy(source, target, sems.at[index])
        for index, (source, target) in enumerate(zip(sources, held))
    ]
    for transfer in transfers:
        transfer.start()
    for transfer in transfers:
        transfer.wait()
    ys, planes, xs = orb_ref.shape
    columns, panel = ritz_ref.shape
    ng = natural_ref.shape[0] // rows
    per_row = LANES // width
    for row in range(-(-columns // per_row)):
        line = jnp.zeros((1, LANES), jnp.float32)
        for slot in range(min(per_row, columns - row * per_row)):
            piece = jnp.concatenate(
                [ritz_ref[pl.ds(row * per_row + slot, 1), :], jnp.zeros((1, LANES - panel), jnp.float32)], axis=1
            )
            line = line + (pltpu.roll(piece, slot * width, 1) if slot else piece)
        natural_ref[pl.ds(run + row, ng, stride=rows), :] = jnp.broadcast_to(line, (ng, LANES))

    centre_weight = 3.0 * COEFFICIENTS[0] + sum(pair_weights(n)[0] for n in (planes, ys, xs))
    scale = 2.0 / HALF
    hop = -0.5 / (SPACING * SPACING) * scale
    diagonal = []
    for y in range(ys):
        region = region_ref[y]
        potential = jnp.zeros((planes, xs), jnp.float32)
        for index in range(table_ref.shape[0]):
            potential = jnp.where(region == index, table_ref[index], potential)
        diagonal.append(scale * potential + (hop * centre_weight - scale * CENTRE))
    live = (lax.axis_index("grid") < counts_ref[lax.axis_index("band")]).astype(jnp.float32)
    previous = [live * orb_ref[y] for y in range(ys)]
    current = apply(previous, [0.5 * value for value in diagonal], 0.5 * hop, None)
    for _ in range(DEGREE - 1):
        previous, current = current, apply(current, diagonal, hop, previous)

    blocks = ys // run
    for y in range(ys):
        natural_ref[pl.ds((y // run) * rows + y % run, planes, stride=blocks * rows), :] = current[y]


def filter_to_all(rows, run, width, order, *refs):
    sources, out_ref, held, sems, natural_ref = refs[:5], refs[5], refs[6:11], refs[11], refs[12]
    filtered_tiles(rows, run, width, sources, held, sems, natural_ref)
    ng = natural_ref.shape[0] // rows
    for place, chip in enumerate(order):
        out_ref[pl.ds(place * rows, rows), :] = natural_ref[pl.ds(chip % ng * rows, rows), :]


def filter_to_lines(rows, run, width, distances, *refs):
    sources, outs, held, sems, natural_ref = refs[:5], refs[5:-7], refs[-7:-2], refs[-2], refs[-1]
    filtered_tiles(rows, run, width, sources, held, sems, natural_ref)
    here = lax.axis_index("grid")
    for distance, out_ref in zip(distances, outs):
        for dx in (0, 1):
            start = pl.multiple_of((here ^ (2 * distance + dx)) * rows, rows)
            out_ref[dx] = natural_ref[pl.ds(start, rows), :]


def turn_kernel(kept_ref, *refs):
    count = len(refs) - 7
    from_late, from_early, outs = refs[: count // 2], refs[count // 2 : count][::-1], refs[count:]
    here = lax.axis_index("grid") // 2
    pairs = [kept_ref[...]]
    for distance, (late_ref, early_ref) in enumerate(zip(from_late, from_early), 1):
        pairs.append(jnp.where((here ^ distance) > here, late_ref[...], early_ref[...]))
    for out_ref, dx in zip(outs, (0, 1, 0, 1, 1, 0, 1)):
        for distance, pair in enumerate(pairs):
            out_ref[distance] = pair[dx]


def gather_sums(run, width, columns, distance, own_ref, x_late, y_late, xy_late, xy_early, y_early, x_early, *refs):
    out_ref, tiles_ref = refs
    depth = own_ref.shape[0]
    band, here = lax.axis_index("band"), lax.axis_index("grid")
    row, z, x = band // 2, here // 2, here % 2
    tiles_ref[0, 0] = own_ref[...]
    tiles_ref[0, 1] = jnp.where(x == 0, x_late[...], x_early[...])
    tiles_ref[1, 0] = jnp.where(row == 0, y_late[...], y_early[...])
    tiles_ref[1, 1] = jnp.where(row == 0, xy_late[...], xy_early[...])
    wanted = out_ref.shape[0]
    holders = wanted // columns
    sublane = lax.broadcasted_iota(jnp.int32, (wanted, LANES), 0)
    block = band ^ distance
    acc = [jnp.zeros((wanted, LANES), jnp.float32) for _ in range(run)]
    for dy in (0, 1):
        lines = jnp.zeros((wanted, LANES), jnp.float32)
        for k in range(holders):
            holder = block * holders + k
            line = tiles_ref[dy, x ^ (holder % 2), z ^ (holder // 2), pl.ds(run, 1), :]
            lines = jnp.where(sublane // columns == k, jnp.broadcast_to(line, (wanted, LANES)), lines)
        for dx in (0, 1):
            for dz in range(depth):
                weight = jnp.take_along_axis(lines, sublane % columns * width + (here ^ (2 * dz + dx)), axis=1)
                for y in range(run):
                    acc[y] = acc[y] + weight * tiles_ref[dy, dx, dz, pl.ds(y, 1), :]
    for y in range(run):
        out_ref[:, pl.ds(y * LANES, LANES)] = acc[y]


def sum_kernel(*refs):
    refs[-1][...] = functools.reduce(jnp.add, [ref[...] for ref in refs[:-1]])


def send(value, axis, size, distance, late):
    pairs = [(place, place ^ distance) for place in range(size)]
    return lax.ppermute(value, axis, [(source, target) for source, target in pairs if (source > target) == late])


def shards(nb, ng, orbitals, region, potential_table, counts, ritz):
    _, planes, ys, xs = orbitals.shape
    cells = planes * ys * xs
    panel, columns = ritz.shape
    run = cells // ng // xs
    width = 1
    while width < panel:
        width *= 2
    per_row = LANES // width
    ritz_rows = -(-columns // per_row)
    rows = -(-(run + ritz_rows) // SUBLANES) * SUBLANES
    cores = 2 if nb % 2 == 0 else 1
    chips = nb // cores * ng
    vmem = pl.BlockSpec(memory_space=pltpu.VMEM)
    hbm = pl.BlockSpec(memory_space=pltpu.HBM)
    inputs = [
        pltpu.with_memory_space_constraint(value, pltpu.HBM)
        for value in (
            jnp.transpose(orbitals[0], (1, 0, 2)), jnp.transpose(region, (1, 0, 2)), potential_table, counts, ritz.T
        )
    ]
    scratch = [
        pltpu.VMEM((ys, planes, xs), jnp.float32),
        pltpu.VMEM((ys, planes, xs), jnp.int32),
        pltpu.SMEM(potential_table.shape, jnp.float32),
        pltpu.SMEM(counts.shape, jnp.int32),
        pltpu.VMEM((columns, panel), jnp.float32),
        pltpu.SemaphoreType.DMA((5,)),
        pltpu.VMEM((ng * rows, LANES), jnp.float32),
    ]
    limit = pltpu.CompilerParams(vmem_limit_bytes=8 * chips * rows * LANES + 64 * cells + 2**20)
    small = pltpu.CompilerParams(vmem_limit_bytes=2**21)
    sum_shape = jax.ShapeDtypeStruct((panel, run * LANES), jnp.float32)
    terms = []

    if (nb, ng, panel) == (4, 8, 8) and columns * width <= LANES and rows == SUBLANES:
        depth = ng // 2
        distances = [0, 1, 2, 3, 3, 2, 1]
        lines = pl.pallas_call(
            functools.partial(filter_to_lines, rows, run, width, distances),
            out_shape=[jax.ShapeDtypeStruct((2, rows, LANES), jnp.float32)] * 7,
            in_specs=[hbm] * 5,
            out_specs=[vmem] * 7,
            scratch_shapes=scratch,
            compiler_params=limit,
            name="chebyshev_filter",
        )(*inputs)
        sent = [
            send(lines[place], "grid", ng, 2 * distances[place], late=place <= 3) for place in range(1, 7)
        ]
        planes_of = pl.pallas_call(
            turn_kernel,
            out_shape=[jax.ShapeDtypeStruct((depth, rows, LANES), jnp.float32)] * 7,
            in_specs=[vmem] * 7,
            out_specs=[vmem] * 7,
            compiler_params=small,
            name="turn",
        )(lines[0], *sent)
        along_x, along_y, across = ("grid", ng, 1), ("band", nb, 2), (("band", "grid"), nb * ng, 2 * ng + 1)
        ways = [along_x, along_y, across, across, along_y, along_x]
        sent = [send(planes_of[place], *ways[place - 1], late=place <= 3) for place in range(1, 7)]

        def partial_sums(distance):
            return pl.pallas_call(
                functools.partial(gather_sums, run, width, columns, distance),
                out_shape=sum_shape,
                in_specs=[vmem] * 7,
                out_specs=vmem,
                scratch_shapes=[pltpu.VMEM((2, 2, depth, rows, LANES), jnp.float32)],
                compiler_params=small,
                name="ritz_partial_sums",
            )(planes_of[0], *sent)
    else:
        order = list(range(chips))[::-1]
        groups = [[(chip // ng * cores + core) * ng + chip % ng for chip in order] for core in range(cores)]
        packed = pl.pallas_call(
            functools.partial(filter_to_all, rows, run, width, order),
            out_shape=jax.ShapeDtypeStruct((chips * rows, LANES), jnp.float32),
            in_specs=[hbm] * 5,
            out_specs=vmem,
            scratch_shapes=scratch,
            compiler_params=limit,
            name="chebyshev_filter",
        )(*inputs)
        got = lax.all_to_all(
            packed.reshape(chips, rows, LANES), ("band", "grid"), split_axis=0, concat_axis=0, tiled=True,
            axis_index_groups=groups,
        )
        by_source = got[::-1].reshape(nb // cores, ng, rows, LANES)
        fields = by_source[:, :, :run].reshape(chips, run * LANES)
        blocks = by_source[:, :, run : run + ritz_rows].reshape(nb // cores, ng, ritz_rows * per_row, width)

        def partial_sums(distance):
            holders = panel // columns
            mine = lax.dynamic_slice_in_dim(blocks, (lax.axis_index("band") ^ distance) * holders, holders, axis=1)
            return lax.dot_general(
                jnp.transpose(mine[:, :, :columns, :panel], (0, 3, 1, 2)).reshape(chips, panel),
                fields,
                (((0,), (0,)), ((), ())),
                precision=lax.Precision.HIGHEST,
                preferred_element_type=jnp.float32,
            )

    if cores == 2:
        terms.append(lax.ppermute(partial_sums(1), "band", [(band, band ^ 1) for band in range(nb)]))
    terms.append(partial_sums(0))
    return pl.pallas_call(
        sum_kernel,
        out_shape=sum_shape,
        in_specs=[vmem] * cores,
        out_specs=vmem,
        compiler_params=pltpu.CompilerParams(vmem_limit_bytes=4 * (cores + 1) * panel * run * LANES + 2**20),
        name="core_sum",
    )(*terms)


def solution(mesh):
    return jax.shard_map(
        functools.partial(shards, mesh.shape["band"], mesh.shape["grid"]),
        mesh=mesh,
        in_specs=(P(("band", "grid"), None, None, None), P(), P(), P(), P("band", "grid")),
        out_specs=P("band", "grid"),
        check_vma=False,
    )
```

time: 15.8 us -> 37.8 us (2.39)
  the two profiles are of different devices: /device:TPU:0 before, /device:TPU:11 now
where the time goes in v16:
time: 37.8 us; the launch traced here: 37.4 us
  starting transfers between devices  28.1 us (74%)
  waiting for transfers between devices  6.93 us (18%)
  Pallas kernels  2.19 us (6%)
    ppermute x12, starting transfers between devices, send(): lax.ppermute(value, axis, [(source, target) for source, target in pairs i...  23.7 us
    ppermute x12, waiting for transfers between devices, send(): lax.ppermute(value, axis, [(source, target) for source, target in pairs i...  6.22 us
    ppermute x1, starting transfers between devices, shards(): lax.ppermute(partial_sums(1), 'band', [(band, band ^ 1) for band in range...  4.44 us
    pallas_call x1, Pallas kernels, shards(): pl.pallas_call(functools.partial(filter_to_lines, rows, run, width, dista...  1.29 us
  transfers between devices with their start and end apart: 13, of which 3 were waited for; matrix products, arithmetic and copies ran while one was open for 0% of the time, Pallas kernels for 0%

profile of v16, /device:TPU:11, one launch (start us, length us, event | category | flops | bytes accessed | tf_op | source)
XLA Modules:
  0.0 37.4 jit_solution(6908184068866459430)
XLA Ops:
  0.0 1.3 %chebyshev_filter.1 = (f32[2,8,128]{2,1,0:T(8,128)S(1)}, f32[2,8,128]{2,1,0:T(8,128)S(1)}, f32[2,8,128]{2,1,0:T(8,128)S(1)}, f32[2,8,128]{2,1,0:T(8,128)S(1)}, f...) custom-call(f32[6,8,128]{2,1,0:T(8,128)} %bitcast.5, s32[6,8,128]{2,1,0:T(8,128)} %bitcast.6, ...), custom_call_target="tpu_custom_call" | custom-call | tf_op jit(solution)/shard_map/chebyshev_filter/pallas_call | solution.py:218
  1.3 2.1 %collective-permute-start = (f32[2,8,128]{2,1,0:T(8,128)S(1)}, f32[2,8,128]{2,1,0:T(8,128)S(1)}, u32[]{:S(2)}, u32[]{:S(2)}) collective-permute-start(f32[2,8,128]{2,1,0:T(8,128)S(1)} %get-tuple-element.20), channel_id=1, source_target_pairs={{2,0},{3,1},{6,4},{7,5},{10,8},{11,9},{14,12},{15,13},{18,16},{19,... | collective-permute-start | bytes 24584 | tf_op jit(solution)/shard_map/ppermute | solution.py:177
  3.4 1.3 %collective-permute-start.1 = (f32[2,8,128]{2,1,0:T(8,128)S(1)}, f32[2,8,128]{2,1,0:T(8,128)S(1)}, u32[]{:S(2)}, u32[]{:S(2)}) collective-permute-start(f32[2,8,128]{2,1,0:T(8,128)S(1)} %get-tuple-element.21), channel_id=1, source_target_pairs={{4,0},{5,1},{6,2},{7,3},{12,8},{13,9},{14,10},{15,11},{20,16},{21,... | collective-permute-start | bytes 24584 | tf_op jit(solution)/shard_map/ppermute | solution.py:177
  4.7 1.3 %collective-permute-start.2 = (f32[2,8,128]{2,1,0:T(8,128)S(1)}, f32[2,8,128]{2,1,0:T(8,128)S(1)}, u32[]{:S(2)}, u32[]{:S(2)}) collective-permute-start(f32[2,8,128]{2,1,0:T(8,128)S(1)} %get-tuple-element.22), channel_id=1, source_target_pairs={{4,2},{5,3},{6,0},{7,1},{12,10},{13,11},{14,8},{15,9},{20,18},{21,... | collective-permute-start | bytes 24584 | tf_op jit(solution)/shard_map/ppermute | solution.py:177
  6.0 4.0 %collective-permute-start.3 = (f32[2,8,128]{2,1,0:T(8,128)S(1)}, f32[2,8,128]{2,1,0:T(8,128)S(1)}, u32[]{:S(2)}, u32[]{:S(2)}) collective-permute-start(f32[2,8,128]{2,1,0:T(8,128)S(1)} %get-tuple-element.23), channel_id=1, source_target_pairs={{0,6},{1,7},{2,4},{3,5},{8,14},{9,15},{10,12},{11,13},{16,22},{17,... | collective-permute-start | bytes 24584 | tf_op jit(solution)/shard_map/ppermute | solution.py:177
  10.0 2.2 %collective-permute-start.4 = (f32[2,8,128]{2,1,0:T(8,128)S(1)}, f32[2,8,128]{2,1,0:T(8,128)S(1)}, u32[]{:S(2)}, u32[]{:S(2)}) collective-permute-start(f32[2,8,128]{2,1,0:T(8,128)S(1)} %get-tuple-element.24), channel_id=1, source_target_pairs={{0,4},{1,5},{2,6},{3,7},{8,12},{9,13},{10,14},{11,15},{16,20},{17,... | collective-permute-start | bytes 24584 | tf_op jit(solution)/shard_map/ppermute | solution.py:177
  12.2 1.3 %collective-permute-start.5 = (f32[2,8,128]{2,1,0:T(8,128)S(1)}, f32[2,8,128]{2,1,0:T(8,128)S(1)}, u32[]{:S(2)}, u32[]{:S(2)}) collective-permute-start(f32[2,8,128]{2,1,0:T(8,128)S(1)} %get-tuple-element.25), channel_id=1, source_target_pairs={{0,2},{1,3},{4,6},{5,7},{8,10},{9,11},{12,14},{13,15},{16,18},{17,... | collective-permute-start | bytes 24584 | tf_op jit(solution)/shard_map/ppermute | solution.py:177
  13.5 0.0 collective-permute-done.2.refs_2_
  13.5 0.0 collective-permute-done.3.refs_3_
  13.5 3.1 %collective-permute-done.5.refs_5_ = f32[2,8,128]{2,1,0:T(8,128)S(1)} collective-permute-done((f32[2,8,128]{2,1,0:T(8,128)S(1)}, f32[2,8,128]{2,1,0:T(8,128)S(1)}, u32[]{:S(2)}, u32[]{:S(2)}) %collective-permute-start.5) | collective-permute-done | bytes 8224 | tf_op jit(solution)/shard_map/ppermute | solution.py:177
  16.6 1.5 %collective-permute-start.6 = (f32[4,8,128]{2,1,0:T(8,128)S(1)}, f32[4,8,128]{2,1,0:T(8,128)S(1)}, u32[]{:S(2)}, u32[]{:S(2)}) collective-permute-start(f32[4,8,128]{2,1,0:T(8,128)S(1)} %get-tuple-element.27), channel_id=1, source_target_pairs={{1,0},{3,2},{5,4},{7,6},{9,8},{11,10},{13,12},{15,14},{17,16},{19,... | collective-permute-start | bytes 49160 | tf_op jit(solution)/shard_map/ppermute | solution.py:177
  18.1 1.3 %collective-permute-start.7 = (f32[4,8,128]{2,1,0:T(8,128)S(1)}, f32[4,8,128]{2,1,0:T(8,128)S(1)}, u32[]{:S(2)}, u32[]{:S(2)}) collective-permute-start(f32[4,8,128]{2,1,0:T(8,128)S(1)} %get-tuple-element.28), channel_id=1, source_target_pairs={{16,0},{24,8},{17,1},{25,9},{18,2},{26,10},{19,3},{27,11},{20,4},{... | collective-permute-start | bytes 49160 | tf_op jit(solution)/shard_map/ppermute | solution.py:177
  19.4 1.3 %collective-permute-start.8 = (f32[4,8,128]{2,1,0:T(8,128)S(1)}, f32[4,8,128]{2,1,0:T(8,128)S(1)}, u32[]{:S(2)}, u32[]{:S(2)}) collective-permute-start(f32[4,8,128]{2,1,0:T(8,128)S(1)} %get-tuple-element.29), channel_id=1, source_target_pairs={{16,1},{17,0},{18,3},{19,2},{20,5},{21,4},{22,7},{23,6},{24,9},{25... | collective-permute-start | bytes 49160 | tf_op jit(solution)/shard_map/ppermute | solution.py:177
  20.7 4.9 %collective-permute-start.9 = (f32[4,8,128]{2,1,0:T(8,128)S(1)}, f32[4,8,128]{2,1,0:T(8,128)S(1)}, u32[]{:S(2)}, u32[]{:S(2)}) collective-permute-start(f32[4,8,128]{2,1,0:T(8,128)S(1)} %get-tuple-element.30), channel_id=1, source_target_pairs={{0,17},{1,16},{2,19},{3,18},{4,21},{5,20},{6,23},{7,22},{8,25},{9,... | collective-permute-start | bytes 49160 | tf_op jit(solution)/shard_map/ppermute | solution.py:177
  25.6 1.3 %collective-permute-start.10 = (f32[4,8,128]{2,1,0:T(8,128)S(1)}, f32[4,8,128]{2,1,0:T(8,128)S(1)}, u32[]{:S(2)}, u32[]{:S(2)}) collective-permute-start(f32[4,8,128]{2,1,0:T(8,128)S(1)} %get-tuple-element.31), channel_id=1, source_target_pairs={{0,16},{8,24},{1,17},{9,25},{2,18},{10,26},{3,19},{11,27},{4,20},{... | collective-permute-start | bytes 49160 | tf_op jit(solution)/shard_map/ppermute | solution.py:177
  26.9 0.0 collective-permute-done.6.x_late
  26.9 1.3 %collective-permute-start.11 = (f32[4,8,128]{2,1,0:T(8,128)S(1)}, f32[4,8,128]{2,1,0:T(8,128)S(1)}, u32[]{:S(2)}, u32[]{:S(2)}) collective-permute-start(f32[4,8,128]{2,1,0:T(8,128)S(1)} %get-tuple-element.32), channel_id=1, source_target_pairs={{0,1},{2,3},{4,5},{6,7},{8,9},{10,11},{12,13},{14,15},{16,17},{18,... | collective-permute-start | bytes 49160 | tf_op jit(solution)/shard_map/ppermute | solution.py:177
  28.2 0.0 collective-permute-done.9.xy_early
  28.2 3.1 %collective-permute-done.11.x_early = f32[4,8,128]{2,1,0:T(8,128)S(1)} collective-permute-done((f32[4,8,128]{2,1,0:T(8,128)S(1)}, f32[4,8,128]{2,1,0:T(8,128)S(1)}, u32[]{:S(2)}, u32[]{:S(2)}) %collective-permute-start.11) | collective-permute-done | bytes 16416 | tf_op jit(solution)/shard_map/ppermute | solution.py:177
  31.4 0.1 ritz_partial_sums.2
  31.5 4.4 %collective-permute-start.12 = (f32[8,768]{1,0:T(8,128)S(1)}, f32[8,768]{1,0:T(8,128)S(1)}, u32[]{:S(2)}, u32[]{:S(2)}) collective-permute-start(f32[8,768]{1,0:T(8,128)S(1)} %ritz_partial_sums.2), channel_id=1, source_target_pairs={{0,8},{8,0},{16,24},{24,16},{1,9},{9,1},{17,25},{25,17},{2,10},{10... | collective-permute-start | bytes 73736 | tf_op jit(solution)/shard_map/ppermute | solution.py:284
  36.0 0.1 ritz_partial_sums.3.refs_1_
  36.1 0.7 %collective-permute-done.12.refs_0_ = f32[8,768]{1,0:T(8,128)S(1)} collective-permute-done((f32[8,768]{1,0:T(8,128)S(1)}, f32[8,768]{1,0:T(8,128)S(1)}, u32[]{:S(2)}, u32[]{:S(2)}) %collective-permute-start.12) | collective-permute-done | bytes 24608 | tf_op jit(solution)/shard_map/ppermute | solution.py:284
  36.8 0.6 %core_sum.1 = f32[8,768]{1,0:T(8,128)} custom-call(f32[8,768]{1,0:T(8,128)S(1)} %collective-permute-done.12.refs_0_, f32[8,768]{1,0:T(8,128)S(1)} %ritz_partial_sums.3.refs_1_), custom_call_target="tpu_custom_call" | custom-call | tf_op jit(solution)/shard_map/core_sum/pallas_call | solution.py:286
  (7 shorter events, 0.0 us)
Async XLA Ops:
  1.3 10.9 %collective-permute-start = (f32[2,8,128]{2,1,0:T(8,128)S(1)}, f32[2,8,128]{2,1,0:T(8,128)S(1)}, u32[]{:S(2)}, u32[]{:S(2)}) collective-permute-start(f32[2,8,128]{2,1,0:T(8,128)S(1)} %get-tuple-element.20), channel_id=1, source_target_pairs={{2,0},{3,1},{6,4},{7,5},{10,8},{11,9},{14,12},{15,13},{18,16},{19,... | collective-permute-start | bytes 24584 | tf_op jit(solution)/shard_map/ppermute | solution.py:177
  3.4 10.1 %collective-permute-start.1 = (f32[2,8,128]{2,1,0:T(8,128)S(1)}, f32[2,8,128]{2,1,0:T(8,128)S(1)}, u32[]{:S(2)}, u32[]{:S(2)}) collective-permute-start(f32[2,8,128]{2,1,0:T(8,128)S(1)} %get-tuple-element.21), channel_id=1, source_target_pairs={{4,0},{5,1},{6,2},{7,3},{12,8},{13,9},{14,10},{15,11},{20,16},{21,... | collective-permute-start | bytes 24584 | tf_op jit(solution)/shard_map/ppermute | solution.py:177
  4.7 8.8 %collective-permute-start.2 = (f32[2,8,128]{2,1,0:T(8,128)S(1)}, f32[2,8,128]{2,1,0:T(8,128)S(1)}, u32[]{:S(2)}, u32[]{:S(2)}) collective-permute-start(f32[2,8,128]{2,1,0:T(8,128)S(1)} %get-tuple-element.22), channel_id=1, source_target_pairs={{4,2},{5,3},{6,0},{7,1},{12,10},{13,11},{14,8},{15,9},{20,18},{21,... | collective-permute-start | bytes 24584 | tf_op jit(solution)/shard_map/ppermute | solution.py:177
  6.0 7.5 %collective-permute-start.3 = (f32[2,8,128]{2,1,0:T(8,128)S(1)}, f32[2,8,128]{2,1,0:T(8,128)S(1)}, u32[]{:S(2)}, u32[]{:S(2)}) collective-permute-start(f32[2,8,128]{2,1,0:T(8,128)S(1)} %get-tuple-element.23), channel_id=1, source_target_pairs={{0,6},{1,7},{2,4},{3,5},{8,14},{9,15},{10,12},{11,13},{16,22},{17,... | collective-permute-start | bytes 24584 | tf_op jit(solution)/shard_map/ppermute | solution.py:177
  10.0 3.5 %collective-permute-start.4 = (f32[2,8,128]{2,1,0:T(8,128)S(1)}, f32[2,8,128]{2,1,0:T(8,128)S(1)}, u32[]{:S(2)}, u32[]{:S(2)}) collective-permute-start(f32[2,8,128]{2,1,0:T(8,128)S(1)} %get-tuple-element.24), channel_id=1, source_target_pairs={{0,4},{1,5},{2,6},{3,7},{8,12},{9,13},{10,14},{11,15},{16,20},{17,... | collective-permute-start | bytes 24584 | tf_op jit(solution)/shard_map/ppermute | solution.py:177
  12.2 4.4 %collective-permute-start.5 = (f32[2,8,128]{2,1,0:T(8,128)S(1)}, f32[2,8,128]{2,1,0:T(8,128)S(1)}, u32[]{:S(2)}, u32[]{:S(2)}) collective-permute-start(f32[2,8,128]{2,1,0:T(8,128)S(1)} %get-tuple-element.25), channel_id=1, source_target_pairs={{0,2},{1,3},{4,6},{5,7},{8,10},{9,11},{12,14},{13,15},{16,18},{17,... | collective-permute-start | bytes 24584 | tf_op jit(solution)/shard_map/ppermute | solution.py:177
  16.6 10.3 %collective-permute-start.6 = (f32[4,8,128]{2,1,0:T(8,128)S(1)}, f32[4,8,128]{2,1,0:T(8,128)S(1)}, u32[]{:S(2)}, u32[]{:S(2)}) collective-permute-start(f32[4,8,128]{2,1,0:T(8,128)S(1)} %get-tuple-element.27), channel_id=1, source_target_pairs={{1,0},{3,2},{5,4},{7,6},{9,8},{11,10},{13,12},{15,14},{17,16},{19,... | collective-permute-start | bytes 49160 | tf_op jit(solution)/shard_map/ppermute | solution.py:177
  18.1 10.1 %collective-permute-start.7 = (f32[4,8,128]{2,1,0:T(8,128)S(1)}, f32[4,8,128]{2,1,0:T(8,128)S(1)}, u32[]{:S(2)}, u32[]{:S(2)}) collective-permute-start(f32[4,8,128]{2,1,0:T(8,128)S(1)} %get-tuple-element.28), channel_id=1, source_target_pairs={{16,0},{24,8},{17,1},{25,9},{18,2},{26,10},{19,3},{27,11},{20,4},{... | collective-permute-start | bytes 49160 | tf_op jit(solution)/shard_map/ppermute | solution.py:177
  19.4 8.8 %collective-permute-start.8 = (f32[4,8,128]{2,1,0:T(8,128)S(1)}, f32[4,8,128]{2,1,0:T(8,128)S(1)}, u32[]{:S(2)}, u32[]{:S(2)}) collective-permute-start(f32[4,8,128]{2,1,0:T(8,128)S(1)} %get-tuple-element.29), channel_id=1, source_target_pairs={{16,1},{17,0},{18,3},{19,2},{20,5},{21,4},{22,7},{23,6},{24,9},{25... | collective-permute-start | bytes 49160 | tf_op jit(solution)/shard_map/ppermute | solution.py:177
  20.7 7.5 %collective-permute-start.9 = (f32[4,8,128]{2,1,0:T(8,128)S(1)}, f32[4,8,128]{2,1,0:T(8,128)S(1)}, u32[]{:S(2)}, u32[]{:S(2)}) collective-permute-start(f32[4,8,128]{2,1,0:T(8,128)S(1)} %get-tuple-element.30), channel_id=1, source_target_pairs={{0,17},{1,16},{2,19},{3,18},{4,21},{5,20},{6,23},{7,22},{8,25},{9,... | collective-permute-start | bytes 49160 | tf_op jit(solution)/shard_map/ppermute | solution.py:177
  25.6 2.6 %collective-permute-start.10 = (f32[4,8,128]{2,1,0:T(8,128)S(1)}, f32[4,8,128]{2,1,0:T(8,128)S(1)}, u32[]{:S(2)}, u32[]{:S(2)}) collective-permute-start(f32[4,8,128]{2,1,0:T(8,128)S(1)} %get-tuple-element.31), channel_id=1, source_target_pairs={{0,16},{8,24},{1,17},{9,25},{2,18},{10,26},{3,19},{11,27},{4,20},{... | collective-permute-start | bytes 49160 | tf_op jit(solution)/shard_map/ppermute | solution.py:177
  26.9 4.5 %collective-permute-start.11 = (f32[4,8,128]{2,1,0:T(8,128)S(1)}, f32[4,8,128]{2,1,0:T(8,128)S(1)}, u32[]{:S(2)}, u32[]{:S(2)}) collective-permute-start(f32[4,8,128]{2,1,0:T(8,128)S(1)} %get-tuple-element.32), channel_id=1, source_target_pairs={{0,1},{2,3},{4,5},{6,7},{8,9},{10,11},{12,13},{14,15},{16,17},{18,... | collective-permute-start | bytes 49160 | tf_op jit(solution)/shard_map/ppermute | solution.py:177
  31.5 5.3 %collective-permute-start.12 = (f32[8,768]{1,0:T(8,128)S(1)}, f32[8,768]{1,0:T(8,128)S(1)}, u32[]{:S(2)}, u32[]{:S(2)}) collective-permute-start(f32[8,768]{1,0:T(8,128)S(1)} %ritz_partial_sums.2), channel_id=1, source_target_pairs={{0,8},{8,0},{16,24},{24,16},{1,9},{9,1},{17,25},{25,17},{2,10},{10... | collective-permute-start | bytes 73736 | tf_op jit(solution)/shard_map/ppermute | solution.py:284

commit v17 on v16

--- a/solution.py
+++ b/solution.py
@@ -117,37 +117,39 @@
         out_ref[pl.ds(place * rows, rows), :] = natural_ref[pl.ds(chip % ng * rows, rows), :]
 
 
-def filter_to_lines(rows, run, width, distances, *refs):
-    sources, outs, held, sems, natural_ref = refs[:5], refs[5:-7], refs[-7:-2], refs[-2], refs[-1]
+def filter_to_lines(rows, run, width, *refs):
+    sources, outs, held, sems, natural_ref = refs[:5], refs[5:7], refs[7:12], refs[12], refs[13]
     filtered_tiles(rows, run, width, sources, held, sems, natural_ref)
     here = lax.axis_index("grid")
-    for distance, out_ref in zip(distances, outs):
-        for dx in (0, 1):
-            start = pl.multiple_of((here ^ (2 * distance + dx)) * rows, rows)
-            out_ref[dx] = natural_ref[pl.ds(start, rows), :]
-
-
-def turn_kernel(kept_ref, *refs):
-    count = len(refs) - 7
-    from_late, from_early, outs = refs[: count // 2], refs[count // 2 : count][::-1], refs[count:]
-    here = lax.axis_index("grid") // 2
-    pairs = [kept_ref[...]]
-    for distance, (late_ref, early_ref) in enumerate(zip(from_late, from_early), 1):
-        pairs.append(jnp.where((here ^ distance) > here, late_ref[...], early_ref[...]))
-    for out_ref, dx in zip(outs, (0, 1, 0, 1, 1, 0, 1)):
-        for distance, pair in enumerate(pairs):
-            out_ref[distance] = pair[dx]
-
-
-def gather_sums(run, width, columns, distance, own_ref, x_late, y_late, xy_late, xy_early, y_early, x_early, *refs):
+    for far, out_ref in enumerate(outs):
+        for tile in range(4):
+            start = pl.multiple_of((here ^ (4 * far + tile)) * rows, rows)
+            out_ref[tile] = natural_ref[pl.ds(start, rows), :]
+
+
+def turn_kernel(kept_ref, came_ref, first_ref, second_ref):
+    count = first_ref.shape[0] // 2
+    for half, ref in enumerate((kept_ref, came_ref)):
+        first_ref[pl.ds(half * count, count)] = ref[pl.ds(0, count)]
+        second_ref[pl.ds(half * count, count)] = ref[pl.ds(count, count)]
+
+
+def split_kernel(kept_ref, came_ref, own_ref, other_ref):
+    for half, ref in enumerate((kept_ref, came_ref)):
+        for orbital in (0, 1):
+            own_ref[2 * orbital + half] = ref[2 * orbital]
+            other_ref[2 * orbital + half] = ref[2 * orbital + 1]
+
+
+def gather_sums(run, width, columns, distance, own_ref, x_ref, xy_ref, y_ref, *refs):
     out_ref, tiles_ref = refs
     depth = own_ref.shape[0]
     band, here = lax.axis_index("band"), lax.axis_index("grid")
-    row, z, x = band // 2, here // 2, here % 2
+    z, x = here // 2, here % 2
     tiles_ref[0, 0] = own_ref[...]
-    tiles_ref[0, 1] = jnp.where(x == 0, x_late[...], x_early[...])
-    tiles_ref[1, 0] = jnp.where(row == 0, y_late[...], y_early[...])
-    tiles_ref[1, 1] = jnp.where(row == 0, xy_late[...], xy_early[...])
+    tiles_ref[0, 1] = x_ref[...]
+    tiles_ref[1, 0] = y_ref[...]
+    tiles_ref[1, 1] = xy_ref[...]
     wanted = out_ref.shape[0]
     holders = wanted // columns
     sublane = lax.broadcasted_iota(jnp.int32, (wanted, LANES), 0)
@@ -172,9 +174,8 @@
     refs[-1][...] = functools.reduce(jnp.add, [ref[...] for ref in refs[:-1]])
 
 
-def send(value, axis, size, distance, late):
-    pairs = [(place, place ^ distance) for place in range(size)]
-    return lax.ppermute(value, axis, [(source, target) for source, target in pairs if (source > target) == late])
+def swap(value, axis, size, distance):
+    return lax.ppermute(value, axis, [(place, place ^ distance) for place in range(size)])
 
 
 def shards(nb, ng, orbitals, region, potential_table, counts, ritz):
@@ -214,41 +215,41 @@
 
     if (nb, ng, panel) == (4, 8, 8) and columns * width <= LANES and rows == SUBLANES:
         depth = ng // 2
-        distances = [0, 1, 2, 3, 3, 2, 1]
-        lines = pl.pallas_call(
-            functools.partial(filter_to_lines, rows, run, width, distances),
-            out_shape=[jax.ShapeDtypeStruct((2, rows, LANES), jnp.float32)] * 7,
+        four = [jax.ShapeDtypeStruct((depth, rows, LANES), jnp.float32)] * 2
+        near, far = pl.pallas_call(
+            functools.partial(filter_to_lines, rows, run, width),
+            out_shape=four,
             in_specs=[hbm] * 5,
-            out_specs=[vmem] * 7,
+            out_specs=[vmem] * 2,
             scratch_shapes=scratch,
             compiler_params=limit,
             name="chebyshev_filter",
         )(*inputs)
-        sent = [
-            send(lines[place], "grid", ng, 2 * distances[place], late=place <= 3) for place in range(1, 7)
+
+        def repack(kernel, kept, came):
+            return pl.pallas_call(
+                kernel, out_shape=four, in_specs=[vmem] * 2, out_specs=[vmem] * 2, compiler_params=small, name="repack"
+            )(kept, came)
+
+        near, far = repack(turn_kernel, near, swap(far, "grid", ng, 4))
+        own, other = repack(split_kernel, near, swap(far, "grid", ng, 2))
+        tiles = [
+            own,
+            swap(other, "grid", ng, 1),
+            swap(other, ("band", "grid"), nb * ng, 2 * ng + 1),
+            swap(own, "band", nb, 2),
         ]
-        planes_of = pl.pallas_call(
-            turn_kernel,
-            out_shape=[jax.ShapeDtypeStruct((depth, rows, LANES), jnp.float32)] * 7,
-            in_specs=[vmem] * 7,
-            out_specs=[vmem] * 7,
-            compiler_params=small,
-            name="turn",
-        )(lines[0], *sent)
-        along_x, along_y, across = ("grid", ng, 1), ("band", nb, 2), (("band", "grid"), nb * ng, 2 * ng + 1)
-        ways = [along_x, along_y, across, across, along_y, along_x]
-        sent = [send(planes_of[place], *ways[place - 1], late=place <= 3) for place in range(1, 7)]
 
         def partial_sums(distance):
             return pl.pallas_call(
                 functools.partial(gather_sums, run, width, columns, distance),
                 out_shape=sum_shape,
-                in_specs=[vmem] * 7,
+                in_specs=[vmem] * 4,
                 out_specs=vmem,
                 scratch_shapes=[pltpu.VMEM((2, 2, depth, rows, LANES), jnp.float32)],
                 compiler_params=small,
                 name="ritz_partial_sums",
-            )(planes_of[0], *sent)
+            )(*tiles)
     else:
         order = list(range(chips))[::-1]
         groups = [[(chip // ng * cores + core) * ng + chip % ng for chip in order] for core in range(cores)]

time: 37.8 us -> 20.2 us (0.53)
  the two profiles are of different devices: /device:TPU:11 before, /device:TPU:0 now
where the time goes in v17:
time: 20.2 us; the launch traced here: 20 us
  starting transfers between devices  9.57 us (47%)
  waiting for transfers between devices  8.2 us (41%)
  Pallas kernels  2.18 us (11%)
    ppermute x5, starting transfers between devices, swap(): lax.ppermute(value, axis, [(place, place ^ distance) for place in range(s...  9.5 us
    ppermute x5, waiting for transfers between devices, swap(): lax.ppermute(value, axis, [(place, place ^ distance) for place in range(s...  7.16 us
    pallas_call x1, Pallas kernels, shards(): pl.pallas_call(functools.partial(filter_to_lines, rows, run, width), out_...  1.29 us
    ppermute x1, waiting for transfers between devices, shards(): lax.ppermute(partial_sums(1), 'band', [(band, band ^ 1) for band in range...  1.04 us
    pallas_call x1, Pallas kernels, shards(): pl.pallas_call(sum_kernel, out_shape=sum_shape, in_specs=[vmem] * cores,...  0.61 us
  transfers between devices with their start and end apart: 6, of which 6 were waited for; matrix products, arithmetic and copies ran while one was open for 0% of the time, Pallas kernels for 1%

profile of v17, /device:TPU:0, one launch (start us, length us, event | category | flops | bytes accessed | tf_op | source)
XLA Modules:
  0.0 20.0 jit_solution(5839965866410296320)
XLA Ops:
  0.0 1.3 %chebyshev_filter.1 = (f32[4,8,128]{2,1,0:T(8,128)S(1)}, f32[4,8,128]{2,1,0:T(8,128)S(1)}) custom-call(f32[6,8,128]{2,1,0:T(8,128)} %bitcast.5, s32[6,8,128]{2,1,0:T(8,128)} %bitcast.6, f32[16]{0:T(128)} %refs_2_.1, s32[4]{0:T(128)} %refs_3_.1, f32[4,8]{1,0:T(4,128)} %bitcast.7), custom_call_target="tpu_custom_call" | custom-call | tf_op jit(solution)/shard_map/chebyshev_filter/pallas_call | solution.py:219
  1.3 4.1 %collective-permute-start = (f32[4,8,128]{2,1,0:T(8,128)S(1)}, f32[4,8,128]{2,1,0:T(8,128)S(1)}, u32[]{:S(2)}, u32[]{:S(2)}) collective-permute-start(f32[4,8,128]{2,1,0:T(8,128)S(1)} %get-tuple-element.12), channel_id=1, source_target_pairs={{0,4},{1,5},{2,6},{3,7},{4,0},{5,1},{6,2},{7,3},{8,12},{9,13},{10,... | collective-permute-start | bytes 49160 | tf_op jit(solution)/shard_map/ppermute | solution.py:178
  5.4 1.7 %collective-permute-done.came_ref = f32[4,8,128]{2,1,0:T(8,128)S(1)} collective-permute-done((f32[4,8,128]{2,1,0:T(8,128)S(1)}, f32[4,8,128]{2,1,0:T(8,128)S(1)}, u32[]{:S(2)}, u32[]{:S(2)}) %collective-permute-start) | collective-permute-done | bytes 16416 | tf_op jit(solution)/shard_map/ppermute | solution.py:178
  7.1 1.9 %collective-permute-start.1 = (f32[4,8,128]{2,1,0:T(8,128)S(1)}, f32[4,8,128]{2,1,0:T(8,128)S(1)}, u32[]{:S(2)}, u32[]{:S(2)}) collective-permute-start(f32[4,8,128]{2,1,0:T(8,128)S(1)} %get-tuple-element.14), channel_id=1, source_target_pairs={{0,2},{1,3},{2,0},{3,1},{4,6},{5,7},{6,4},{7,5},{8,10},{9,11},{10,... | collective-permute-start | bytes 49160 | tf_op jit(solution)/shard_map/ppermute | solution.py:178
  9.0 1.8 %collective-permute-done.1.came_ref = f32[4,8,128]{2,1,0:T(8,128)S(1)} collective-permute-done((f32[4,8,128]{2,1,0:T(8,128)S(1)}, f32[4,8,128]{2,1,0:T(8,128)S(1)}, u32[]{:S(2)}, u32[]{:S(2)}) %collective-permute-start.1) | collective-permute-done | bytes 16416 | tf_op jit(solution)/shard_map/ppermute | solution.py:178
  10.9 2.8 %collective-permute-start.3 = (f32[4,8,128]{2,1,0:T(8,128)S(1)}, f32[4,8,128]{2,1,0:T(8,128)S(1)}, u32[]{:S(2)}, u32[]{:S(2)}) collective-permute-start(f32[4,8,128]{2,1,0:T(8,128)S(1)} %get-tuple-element.16), channel_id=1, source_target_pairs={{0,17},{1,16},{2,19},{3,18},{4,21},{5,20},{6,23},{7,22},{8,25},{9,... | collective-permute-start | bytes 49160 | tf_op jit(solution)/shard_map/ppermute | solution.py:178
  13.7 0.5 %collective-permute-start.2 = (f32[4,8,128]{2,1,0:T(8,128)S(1)}, f32[4,8,128]{2,1,0:T(8,128)S(1)}, u32[]{:S(2)}, u32[]{:S(2)}) collective-permute-start(f32[4,8,128]{2,1,0:T(8,128)S(1)} %get-tuple-element.16), channel_id=1, source_target_pairs={{0,1},{1,0},{2,3},{3,2},{4,5},{5,4},{6,7},{7,6},{8,9},{9,8},{10,11... | collective-permute-start | bytes 49160 | tf_op jit(solution)/shard_map/ppermute | solution.py:178
  14.2 0.1 collective-permute-start.4
  14.4 1.1 %collective-permute-done.3.xy_ref = f32[4,8,128]{2,1,0:T(8,128)S(1)} collective-permute-done((f32[4,8,128]{2,1,0:T(8,128)S(1)}, f32[4,8,128]{2,1,0:T(8,128)S(1)}, u32[]{:S(2)}, u32[]{:S(2)}) %collective-permute-start.3) | collective-permute-done | bytes 16416 | tf_op jit(solution)/shard_map/ppermute | solution.py:178
  15.5 1.9 %collective-permute-done.2.x_ref = f32[4,8,128]{2,1,0:T(8,128)S(1)} collective-permute-done((f32[4,8,128]{2,1,0:T(8,128)S(1)}, f32[4,8,128]{2,1,0:T(8,128)S(1)}, u32[]{:S(2)}, u32[]{:S(2)}) %collective-permute-start.2) | collective-permute-done | bytes 16416 | tf_op jit(solution)/shard_map/ppermute | solution.py:178
  17.4 0.5 %collective-permute-done.4.y_ref = f32[4,8,128]{2,1,0:T(8,128)S(1)} collective-permute-done((f32[4,8,128]{2,1,0:T(8,128)S(1)}, f32[4,8,128]{2,1,0:T(8,128)S(1)}, u32[]{:S(2)}, u32[]{:S(2)}) %collective-permute-start.4) | collective-permute-done | bytes 16416 | tf_op jit(solution)/shard_map/ppermute | solution.py:178
  18.0 0.1 ritz_partial_sums.2
  18.1 0.1 collective-permute-start.5
  18.2 0.1 ritz_partial_sums.3.refs_1_
  18.3 1.0 %collective-permute-done.5.refs_0_ = f32[8,768]{1,0:T(8,128)S(1)} collective-permute-done((f32[8,768]{1,0:T(8,128)S(1)}, f32[8,768]{1,0:T(8,128)S(1)}, u32[]{:S(2)}, u32[]{:S(2)}) %collective-permute-start.5) | collective-permute-done | bytes 24608 | tf_op jit(solution)/shard_map/ppermute | solution.py:285
  19.4 0.6 %core_sum.1 = f32[8,768]{1,0:T(8,128)} custom-call(f32[8,768]{1,0:T(8,128)S(1)} %collective-permute-done.5.refs_0_, f32[8,768]{1,0:T(8,128)S(1)} %ritz_partial_sums.3.refs_1_), custom_call_target="tpu_custom_call" | custom-call | tf_op jit(solution)/shard_map/core_sum/pallas_call | solution.py:287
  (2 shorter events, 0.0 us)
Async XLA Ops:
  1.3 5.8 %collective-permute-start = (f32[4,8,128]{2,1,0:T(8,128)S(1)}, f32[4,8,128]{2,1,0:T(8,128)S(1)}, u32[]{:S(2)}, u32[]{:S(2)}) collective-permute-start(f32[4,8,128]{2,1,0:T(8,128)S(1)} %get-tuple-element.12), channel_id=1, source_target_pairs={{0,4},{1,5},{2,6},{3,7},{4,0},{5,1},{6,2},{7,3},{8,12},{9,13},{10,... | collective-permute-start | bytes 49160 | tf_op jit(solution)/shard_map/ppermute | solution.py:178
  7.1 3.7 %collective-permute-start.1 = (f32[4,8,128]{2,1,0:T(8,128)S(1)}, f32[4,8,128]{2,1,0:T(8,128)S(1)}, u32[]{:S(2)}, u32[]{:S(2)}) collective-permute-start(f32[4,8,128]{2,1,0:T(8,128)S(1)} %get-tuple-element.14), channel_id=1, source_target_pairs={{0,2},{1,3},{2,0},{3,1},{4,6},{5,7},{6,4},{7,5},{8,10},{9,11},{10,... | collective-permute-start | bytes 49160 | tf_op jit(solution)/shard_map/ppermute | solution.py:178
  10.9 4.6 %collective-permute-start.3 = (f32[4,8,128]{2,1,0:T(8,128)S(1)}, f32[4,8,128]{2,1,0:T(8,128)S(1)}, u32[]{:S(2)}, u32[]{:S(2)}) collective-permute-start(f32[4,8,128]{2,1,0:T(8,128)S(1)} %get-tuple-element.16), channel_id=1, source_target_pairs={{0,17},{1,16},{2,19},{3,18},{4,21},{5,20},{6,23},{7,22},{8,25},{9,... | collective-permute-start | bytes 49160 | tf_op jit(solution)/shard_map/ppermute | solution.py:178
  13.7 3.7 %collective-permute-start.2 = (f32[4,8,128]{2,1,0:T(8,128)S(1)}, f32[4,8,128]{2,1,0:T(8,128)S(1)}, u32[]{:S(2)}, u32[]{:S(2)}) collective-permute-start(f32[4,8,128]{2,1,0:T(8,128)S(1)} %get-tuple-element.16), channel_id=1, source_target_pairs={{0,1},{1,0},{2,3},{3,2},{4,5},{5,4},{6,7},{7,6},{8,9},{9,8},{10,11... | collective-permute-start | bytes 49160 | tf_op jit(solution)/shard_map/ppermute | solution.py:178
  14.2 3.7 %collective-permute-start.4 = (f32[4,8,128]{2,1,0:T(8,128)S(1)}, f32[4,8,128]{2,1,0:T(8,128)S(1)}, u32[]{:S(2)}, u32[]{:S(2)}) collective-permute-start(f32[4,8,128]{2,1,0:T(8,128)S(1)} %get-tuple-element.15.own_ref), channel_id=1, source_target_pairs={{0,16},{8,24},{16,0},{24,8},{1,17},{9,25},{17,1},{25,9},{2,18},{10... | collective-permute-start | bytes 49160 | tf_op jit(solution)/shard_map/ppermute | solution.py:178
  18.1 1.3 %collective-permute-start.5 = (f32[8,768]{1,0:T(8,128)S(1)}, f32[8,768]{1,0:T(8,128)S(1)}, u32[]{:S(2)}, u32[]{:S(2)}) collective-permute-start(f32[8,768]{1,0:T(8,128)S(1)} %ritz_partial_sums.2), channel_id=1, source_target_pairs={{0,8},{8,0},{16,24},{24,16},{1,9},{9,1},{17,25},{25,17},{2,10},{10... | collective-permute-start | bytes 73736 | tf_op jit(solution)/shard_map/ppermute | solution.py:285

commit v18 on v15

--- a/solution.py
+++ b/solution.py
@@ -133,10 +133,6 @@
                 acc[y] = acc[y] + weight * got_ref[order.index(row * ng + r), pl.ds(y, 1), :]
     for y in range(run):
         out_ref[:, pl.ds(y * LANES, LANES)] = acc[y]
-
-
-def sum_kernel(*refs):
-    refs[-1][...] = functools.reduce(jnp.add, [ref[...] for ref in refs[:-1]])
 
 
 def shards(nrow, cores, ng, orbitals, region, potential_table, counts, ritz):
@@ -218,14 +214,7 @@
         pairs = [(core, (core + distance) % cores) for core in range(cores)]
         terms.append(lax.ppermute(partial_sums(distance), "core", pairs))
     terms.append(partial_sums(0))
-    return pl.pallas_call(
-        sum_kernel,
-        out_shape=sum_shape,
-        in_specs=[vmem] * cores,
-        out_specs=vmem,
-        compiler_params=pltpu.CompilerParams(vmem_limit_bytes=4 * (cores + 1) * panel * run * LANES + 2**20),
-        name="core_sum",
-    )(*terms)
+    return functools.reduce(jnp.add, terms)
 
 
 def solution(mesh):

time: 15.8 us -> 15.8 us (level)
  other arithmetic: 0 us -> 0.61 us
  Pallas kernels: 2.15 us -> 1.54 us
    add x0 -> x1, other arithmetic: none -> 0.61 us  [shards(): return functools.reduce(jnp.add, terms)]
    pallas_call x1 -> x0, Pallas kernels: 0.61 us -> none  [shards(): pl.pallas_call(sum_kernel, out_shape=sum_shape, in_specs=[vmem] * cores,...]
where the time goes in v18:
time: 15.8 us; the launch traced here: 15.6 us
  blocking collectives  12.3 us (78%)
  Pallas kernels  1.54 us (10%)
  waiting for transfers between devices  1.05 us (7%)
  other arithmetic  0.61 us (4%)
    all_to_all x1, blocking collectives, shards(): lax.all_to_all(packed.reshape(tiles, rows, LANES), ('row', 'grid'), split...  12.3 us
    pallas_call x1, Pallas kernels, shards(): pl.pallas_call(functools.partial(filter_kernel, ng, nrow, rows, run, widt...  1.3 us
    ppermute x1, waiting for transfers between devices, shards(): terms.append(lax.ppermute(partial_sums(distance), 'core', pairs))  1.05 us
    add x1, other arithmetic, shards(): return functools.reduce(jnp.add, terms)  0.61 us
  transfers between devices with their start and end apart: 1, of which 1 were waited for; matrix products, arithmetic and copies ran while one was open for 0% of the time, Pallas kernels for 1%

profile of v18, /device:TPU:0, one launch (start us, length us, event | category | flops | bytes accessed | tf_op | source)
XLA Modules:
  0.0 15.6 jit_solution(5795597555304139470)
XLA Ops:
  0.0 1.3 %chebyshev_filter.1 = f32[128,128]{1,0:T(8,128)S(1)} custom-call(f32[6,8,128]{2,1,0:T(8,128)} %bitcast.7, s32[6,8,128]{2,1,0:T(8,128)} %bitcast.8, f32[16]{0:T(128)} %refs_2_.1, s32[4]{0:T(128)} %refs_3_.1, f32[4,8]{1,0:T(4,128)} %bitcast.9), custom_call_target="tpu_custom_call" | custom-call | tf_op jit(solution)/shard_map/chebyshev_filter/pallas_call | solution.py:161
  1.3 12.3 %all_to_all.5.got_ref = f32[16,8,128]{2,1,0:T(8,128)S(1)} all-to-all(f32[16,8,128]{2,1,0:T(8,128)S(1)} %bitcast.6), channel_id=1, replica_groups={{23,0,22,1,21,2,20,3,7,16,6,17,5,18,4,19},{31,8,30,9,29,10,28,11,15,24,..., dimensions={0} | all-to-all | bytes 131072 | tf_op jit(solution)/shard_map/all_to_all | solution.py:178
  13.6 0.1 ritz_partial_sums.2
  13.7 0.1 collective-permute-start
  13.8 0.1 ritz_partial_sums.3
  13.9 1.1 %collective-permute-done = f32[8,768]{1,0:T(8,128)S(1)} collective-permute-done((f32[8,768]{1,0:T(8,128)S(1)}, f32[8,768]{1,0:T(8,128)S(1)}, u32[]{:S(2)}, u32[]{:S(2)}) %collective-permute-start) | collective-permute-done | bytes 24608 | tf_op jit(solution)/shard_map/ppermute | solution.py:215
  15.0 0.6 %add.3 = f32[8,768]{1,0:T(8,128)} add(f32[8,768]{1,0:T(8,128)S(1)} %collective-permute-done, f32[8,768]{1,0:T(8,128)S(1)} %ritz_partial_sums.3) | non-fusion elementwise | flops 6144 | bytes 73728 | tf_op jit(solution)/shard_map/add | solution.py:217
Async XLA Ops:
  13.7 1.3 %collective-permute-start = (f32[8,768]{1,0:T(8,128)S(1)}, f32[8,768]{1,0:T(8,128)S(1)}, u32[]{:S(2)}, u32[]{:S(2)}) collective-permute-start(f32[8,768]{1,0:T(8,128)S(1)} %ritz_partial_sums.2), channel_id=1, source_target_pairs={{0,8},{8,0},{1,9},{9,1},{2,10},{10,2},{3,11},{11,3},{4,12},{12,4},... | collective-permute-start | bytes 73736 | tf_op jit(solution)/shard_map/ppermute | solution.py:215

commit v19 on v18

--- a/solution.py
+++ b/solution.py
@@ -63,6 +63,13 @@
                 )
         results.append(total)
     return results
+
+
+def place_of(chip, order):
+    place = order.index(chip)
+    if place == 0:
+        return place
+    return jnp.where(lax.axis_index("core") == 0, place, len(order) - place)
 
 
 def filter_kernel(ng, copies, rows, run, width, cores, order, *refs):
@@ -110,13 +117,14 @@
         natural_ref[pl.ds((y // run) * rows + y % run, planes, stride=blocks * rows), :] = current[y]
     for copy in range(copies):
         for tile in range(ng):
-            place = order.index(copy * ng + tile)
-            out_ref[pl.ds(place * rows, rows), :] = natural_ref[pl.ds(tile * rows, rows), :]
+            start = pl.multiple_of(place_of(copy * ng + tile, order) * rows, rows)
+            out_ref[pl.ds(start, rows), :] = natural_ref[pl.ds(tile * rows, rows), :]
 
 
 def partial_kernel(nrow, ng, run, width, columns, cores, order, distance, got_ref, out_ref, ritz_ref):
-    for place, source in enumerate(order):
-        ritz_ref[source] = got_ref[place, pl.ds(run, 1), :]
+    places = [place_of(chip, order) for chip in range(nrow * ng)]
+    for chip, place in enumerate(places):
+        ritz_ref[chip] = got_ref[place, pl.ds(run, 1), :]
     wanted = out_ref.shape[0]
     holders = wanted // columns
     sublane = lax.broadcasted_iota(jnp.int32, (wanted, LANES), 0)
@@ -130,7 +138,7 @@
         for r in range(ng):
             weight = jnp.take_along_axis(lines, sublane % columns * width + r, axis=1)
             for y in range(run):
-                acc[y] = acc[y] + weight * got_ref[order.index(row * ng + r), pl.ds(y, 1), :]
+                acc[y] = acc[y] + weight * got_ref[places[row * ng + r], pl.ds(y, 1), :]
     for y in range(run):
         out_ref[:, pl.ds(y * LANES, LANES)] = acc[y]
 
@@ -176,8 +184,11 @@
         name="chebyshev_filter",
     )(*inputs)
     got = lax.all_to_all(
-        packed.reshape(tiles, rows, LANES), ("row", "grid"), split_axis=0, concat_axis=0, tiled=True,
-        axis_index_groups=[order],
+        packed.reshape(tiles, rows, LANES), ("row", "core", "grid"), split_axis=0, concat_axis=0, tiled=True,
+        axis_index_groups=[
+            [(chip // ng * cores + core) * ng + chip % ng for chip in (order[:1] + order[:0:-1] if core else order)]
+            for core in range(cores)
+        ],
     )
     sum_shape = jax.ShapeDtypeStruct((panel, run * LANES), jnp.float32)
     if columns * width <= LANES and tiles <= 64 and panel == ng and panel <= 16:
@@ -194,7 +205,7 @@
 
     else:
         holders = panel // columns
-        by_source = got[jnp.argsort(jnp.array(order))].reshape(nrow, ng, rows, LANES)
+        by_source = got[jnp.stack([place_of(chip, order) for chip in range(tiles)])].reshape(nrow, ng, rows, LANES)
         fields = by_source[:, :, :run].reshape(tiles, run * LANES)
         blocks = by_source[:, :, run : run + ritz_rows].reshape(nrow, ng, ritz_rows * per_row, width)
 

time: 15.8 us -> 15.8 us (level)
  no operation moved by 1% of the time
where the time goes in v19:
time: 15.8 us; the launch traced here: 15.6 us
  blocking collectives  12.3 us (78%)
  Pallas kernels  1.56 us (10%)
  waiting for transfers between devices  1.05 us (7%)
  other arithmetic  0.61 us (4%)
    all_to_all x1, blocking collectives, shards(): lax.all_to_all(packed.reshape(tiles, rows, LANES), ('row', 'core', 'grid'...  12.3 us
    pallas_call x1, Pallas kernels, shards(): pl.pallas_call(functools.partial(filter_kernel, ng, nrow, rows, run, widt...  1.3 us
    ppermute x1, waiting for transfers between devices, shards(): terms.append(lax.ppermute(partial_sums(distance), 'core', pairs))  1.05 us
    add x1, other arithmetic, shards(): return functools.reduce(jnp.add, terms)  0.61 us
  transfers between devices with their start and end apart: 1, of which 1 were waited for; matrix products, arithmetic and copies ran while one was open for 0% of the time, Pallas kernels for 1%

profile of v19, /device:TPU:0, one launch (start us, length us, event | category | flops | bytes accessed | tf_op | source)
XLA Modules:
  0.0 15.6 jit_solution(5220289129704201372)
XLA Ops:
  0.0 1.3 %chebyshev_filter.1 = f32[128,128]{1,0:T(8,128)S(1)} custom-call(f32[6,8,128]{2,1,0:T(8,128)} %bitcast.7, s32[6,8,128]{2,1,0:T(8,128)} %bitcast.8, f32[16]{0:T(128)} %refs_2_.1, s32[4]{0:T(128)} %refs_3_.1, f32[4,8]{1,0:T(4,128)} %bitcast.9), custom_call_target="tpu_custom_call" | custom-call | tf_op jit(solution)/shard_map/chebyshev_filter/pallas_call | solution.py:169
  1.3 12.3 %all_to_all.5.got_ref = f32[16,8,128]{2,1,0:T(8,128)S(1)} all-to-all(f32[16,8,128]{2,1,0:T(8,128)S(1)} %bitcast.6), channel_id=1, replica_groups={{23,0,22,1,21,2,20,3,7,16,6,17,5,18,4,19},{31,27,12,26,13,25,14,24,15,1..., dimensions={0} | all-to-all | bytes 131072 | tf_op jit(solution)/shard_map/all_to_all | solution.py:186
  13.6 0.1 ritz_partial_sums.2
  13.7 0.1 collective-permute-start
  13.8 0.1 ritz_partial_sums.3
  13.9 1.0 %collective-permute-done = f32[8,768]{1,0:T(8,128)S(1)} collective-permute-done((f32[8,768]{1,0:T(8,128)S(1)}, f32[8,768]{1,0:T(8,128)S(1)}, u32[]{:S(2)}, u32[]{:S(2)}) %collective-permute-start) | collective-permute-done | bytes 24608 | tf_op jit(solution)/shard_map/ppermute | solution.py:226
  15.0 0.6 %add.3 = f32[8,768]{1,0:T(8,128)} add(f32[8,768]{1,0:T(8,128)S(1)} %collective-permute-done, f32[8,768]{1,0:T(8,128)S(1)} %ritz_partial_sums.3) | non-fusion elementwise | flops 6144 | bytes 73728 | tf_op jit(solution)/shard_map/add | solution.py:228
Async XLA Ops:
  13.7 1.3 %collective-permute-start = (f32[8,768]{1,0:T(8,128)S(1)}, f32[8,768]{1,0:T(8,128)S(1)}, u32[]{:S(2)}, u32[]{:S(2)}) collective-permute-start(f32[8,768]{1,0:T(8,128)S(1)} %ritz_partial_sums.2), channel_id=1, source_target_pairs={{0,8},{8,0},{1,9},{9,1},{2,10},{10,2},{3,11},{11,3},{4,12},{12,4},... | collective-permute-start | bytes 73736 | tf_op jit(solution)/shard_map/ppermute | solution.py:226

commit v20 on v18

--- a/solution.py
+++ b/solution.py
@@ -155,8 +155,7 @@
             jnp.transpose(orbitals[0], (1, 0, 2)), jnp.transpose(region, (1, 0, 2)), potential_table, counts, ritz.T
         )
     ]
-    late = sorted(range(tiles), key=lambda place: (place % ng // (ng // 2), place // ng, place % ng), reverse=True)
-    order = [place for pair in zip(late, late[::-1]) for place in pair][:tiles]
+    order = [tiles - 1] + sorted(range(tiles - 1), key=lambda chip: (chip % ng // 2, chip))
     packed_bytes = 4 * tiles * rows * LANES
     packed = pl.pallas_call(
         functools.partial(filter_kernel, ng, nrow, rows, run, width, cores, order),

time: 15.8 us -> 15.8 us (level)
  no operation moved by 1% of the time
where the time goes in v20:
time: 15.8 us; the launch traced here: 15.6 us
  blocking collectives  12.3 us (78%)
  Pallas kernels  1.54 us (10%)
  waiting for transfers between devices  1.05 us (7%)
  other arithmetic  0.61 us (4%)
    all_to_all x1, blocking collectives, shards(): lax.all_to_all(packed.reshape(tiles, rows, LANES), ('row', 'grid'), split...  12.3 us
    pallas_call x1, Pallas kernels, shards(): pl.pallas_call(functools.partial(filter_kernel, ng, nrow, rows, run, widt...  1.3 us
    ppermute x1, waiting for transfers between devices, shards(): terms.append(lax.ppermute(partial_sums(distance), 'core', pairs))  1.05 us
    add x1, other arithmetic, shards(): return functools.reduce(jnp.add, terms)  0.61 us
  transfers between devices with their start and end apart: 1, of which 1 were waited for; matrix products, arithmetic and copies ran while one was open for 0% of the time, Pallas kernels for 1%

profile of v20, /device:TPU:0, one launch (start us, length us, event | category | flops | bytes accessed | tf_op | source)
XLA Modules:
  0.0 15.6 jit_solution(8409784564927997561)
XLA Ops:
  0.0 1.3 %chebyshev_filter.1 = f32[128,128]{1,0:T(8,128)S(1)} custom-call(f32[6,8,128]{2,1,0:T(8,128)} %bitcast.7, s32[6,8,128]{2,1,0:T(8,128)} %bitcast.8, f32[16]{0:T(128)} %refs_2_.1, s32[4]{0:T(128)} %refs_3_.1, f32[4,8]{1,0:T(4,128)} %bitcast.9), custom_call_target="tpu_custom_call" | custom-call | tf_op jit(solution)/shard_map/chebyshev_filter/pallas_call | solution.py:160
  1.3 12.3 %all_to_all.5.got_ref = f32[16,8,128]{2,1,0:T(8,128)S(1)} all-to-all(f32[16,8,128]{2,1,0:T(8,128)S(1)} %bitcast.6), channel_id=1, replica_groups={{23,0,1,16,17,2,3,18,19,4,5,20,21,6,7,22},{31,8,9,24,25,10,11,26,27,12,..., dimensions={0} | all-to-all | bytes 131072 | tf_op jit(solution)/shard_map/all_to_all | solution.py:177
  13.6 0.1 ritz_partial_sums.2
  13.7 0.1 collective-permute-start
  13.8 0.1 ritz_partial_sums.3
  13.9 1.1 %collective-permute-done = f32[8,768]{1,0:T(8,128)S(1)} collective-permute-done((f32[8,768]{1,0:T(8,128)S(1)}, f32[8,768]{1,0:T(8,128)S(1)}, u32[]{:S(2)}, u32[]{:S(2)}) %collective-permute-start) | collective-permute-done | bytes 24608 | tf_op jit(solution)/shard_map/ppermute | solution.py:214
  15.0 0.6 %add.3 = f32[8,768]{1,0:T(8,128)} add(f32[8,768]{1,0:T(8,128)S(1)} %collective-permute-done, f32[8,768]{1,0:T(8,128)S(1)} %ritz_partial_sums.3) | non-fusion elementwise | flops 6144 | bytes 73728 | tf_op jit(solution)/shard_map/add | solution.py:216
Async XLA Ops:
  13.7 1.3 %collective-permute-start = (f32[8,768]{1,0:T(8,128)S(1)}, f32[8,768]{1,0:T(8,128)S(1)}, u32[]{:S(2)}, u32[]{:S(2)}) collective-permute-start(f32[8,768]{1,0:T(8,128)S(1)} %ritz_partial_sums.2), channel_id=1, source_target_pairs={{0,8},{8,0},{1,9},{9,1},{2,10},{10,2},{3,11},{11,3},{4,12},{12,4},... | collective-permute-start | bytes 73736 | tf_op jit(solution)/shard_map/ppermute | solution.py:214

commit v21 on v19

--- a/solution.py
+++ b/solution.py
@@ -121,7 +121,11 @@
             out_ref[pl.ds(start, rows), :] = natural_ref[pl.ds(tile * rows, rows), :]
 
 
-def partial_kernel(nrow, ng, run, width, columns, cores, order, distance, got_ref, out_ref, ritz_ref):
+def start_kernel(packed_ref, out_ref):
+    out_ref[...] = jnp.zeros_like(out_ref)
+
+
+def partial_kernel(nrow, ng, run, width, columns, cores, order, distance, got_ref, start_ref, out_ref, ritz_ref):
     places = [place_of(chip, order) for chip in range(nrow * ng)]
     for chip, place in enumerate(places):
         ritz_ref[chip] = got_ref[place, pl.ds(run, 1), :]
@@ -129,7 +133,7 @@
     holders = wanted // columns
     sublane = lax.broadcasted_iota(jnp.int32, (wanted, LANES), 0)
     block = lax.axis_index("row") * cores + lax.rem(lax.axis_index("core") + distance, cores)
-    acc = [jnp.zeros((wanted, LANES), jnp.float32) for _ in range(run)]
+    acc = [start_ref[:, pl.ds(y * LANES, LANES)] for y in range(run)]
     for row in range(nrow):
         lines = jnp.zeros((wanted, LANES), jnp.float32)
         for k in range(holders):
@@ -192,16 +196,25 @@
     )
     sum_shape = jax.ShapeDtypeStruct((panel, run * LANES), jnp.float32)
     if columns * width <= LANES and tiles <= 64 and panel == ng and panel <= 16:
+        start = pl.pallas_call(
+            start_kernel,
+            out_shape=sum_shape,
+            in_specs=[pl.BlockSpec(memory_space=pl.ANY)],
+            out_specs=vmem,
+            compiler_params=pltpu.CompilerParams(vmem_limit_bytes=2**20),
+            name="sums_start",
+        )(packed)
+
         def partial_sums(distance):
             return pl.pallas_call(
                 functools.partial(partial_kernel, nrow, ng, run, width, columns, cores, order, distance),
                 out_shape=sum_shape,
-                in_specs=[vmem],
+                in_specs=[vmem] * 2,
                 out_specs=vmem,
                 scratch_shapes=[pltpu.VMEM((tiles, 1, LANES), jnp.float32)],
                 compiler_params=pltpu.CompilerParams(vmem_limit_bytes=packed_bytes + 2**20),
                 name="ritz_partial_sums",
-            )(got)
+            )(got, start)
 
     else:
         holders = panel // columns

time: 15.8 us -> 17.3 us (1.095)
  blocking collectives: 12.3 us -> 0 us
  starting transfers between devices: 0.07 us -> 10.3 us
  waiting for transfers between devices: 1.05 us -> 4 us
  Pallas kernels: 1.56 us -> 2.17 us
    all_to_all x1 -> x0, blocking collectives: 12.3 us -> none  [shards(): lax.all_to_all(packed.reshape(tiles, rows, LANES), ('row', 'core', 'grid'...]
    all_to_all x0 -> x1, starting transfers between devices: none -> 10.2 us  [shards(): lax.all_to_all(packed.reshape(tiles, rows, LANES), ('row', 'core', 'grid'...]
    all_to_all x0 -> x1, waiting for transfers between devices: none -> 2.95 us  [shards(): lax.all_to_all(packed.reshape(tiles, rows, LANES), ('row', 'core', 'grid'...]
    pallas_call x1, Pallas kernels: 1.3 us -> 1.92 us  [shards(): pl.pallas_call(functools.partial(filter_kernel, ng, nrow, rows, run, widt...]
  transfers between devices with their start and end apart: 1 -> 2, of which waited for: 1 -> 2; matrix products, arithmetic and copies ran while one was open for 0% -> 0% of each run, Pallas kernels for 1% -> 1%
where the time goes in v21:
time: 17.3 us; the launch traced here: 17.1 us
  starting transfers between devices  10.3 us (60%)
  waiting for transfers between devices  4 us (23%)
  Pallas kernels  2.17 us (13%)
  other arithmetic  0.61 us (4%)
    all_to_all x1, starting transfers between devices, shards(): lax.all_to_all(packed.reshape(tiles, rows, LANES), ('row', 'core', 'grid'...  10.2 us
    all_to_all x1, waiting for transfers between devices, shards(): lax.all_to_all(packed.reshape(tiles, rows, LANES), ('row', 'core', 'grid'...  2.95 us
    pallas_call x1, Pallas kernels, shards(): pl.pallas_call(functools.partial(filter_kernel, ng, nrow, rows, run, widt...  1.92 us
    ppermute x1, waiting for transfers between devices, shards(): terms.append(lax.ppermute(partial_sums(distance), 'core', pairs))  1.05 us
    add x1, other arithmetic, shards(): return functools.reduce(jnp.add, terms)  0.61 us
  transfers between devices with their start and end apart: 2, of which 2 were waited for; matrix products, arithmetic and copies ran while one was open for 0% of the time, Pallas kernels for 1%

profile of v21, /device:TPU:0, one launch (start us, length us, event | category | flops | bytes accessed | tf_op | source)
XLA Modules:
  0.0 17.1 jit_solution(11439149589748051028)
XLA Ops:
  0.0 1.9 %chebyshev_filter.1.packed_ref = f32[128,128]{1,0:T(8,128)} custom-call(f32[6,8,128]{2,1,0:T(8,128)} %bitcast.6, s32[6,8,128]{2,1,0:T(8,128)} %bitcast.7, f32[16]{0:T(128)} %refs_2_.1, s32[4]{0:T(128)} %refs_3_.1, f32[4,8]{1,0:T(4,128)} %bitcast.8), custom_call_target="tpu_custom_call" | custom-call | tf_op jit(solution)/shard_map/chebyshev_filter/pallas_call | solution.py:173
  1.9 10.2 %all-to-all-start = ((f32[16,8,128]{2,1,0:T(8,128)}), f32[16,8,128]{2,1,0:T(8,128)S(1)}, u32[]{:S(2)}, u32[]{:S(2)}) async-start(f32[16,8,128]{2,1,0:T(8,128)} %bitcast.4), calls=%async_computation | async-start | bytes 131072 | tf_op jit(solution)/shard_map/all_to_all | solution.py:190
  12.2 3.0 %all-to-all-done.got_ref = f32[16,8,128]{2,1,0:T(8,128)S(1)} async-done(((f32[16,8,128]{2,1,0:T(8,128)}), f32[16,8,128]{2,1,0:T(8,128)S(1)}, u32[]{:S(2)}, u32[]{:S(2)}) %all-to-all-start) | async-done | bytes 65568 | tf_op jit(solution)/shard_map/all_to_all | solution.py:190
  15.1 0.1 ritz_partial_sums.2
  15.2 0.1 collective-permute-start
  15.3 0.1 ritz_partial_sums.3
  15.5 1.0 %collective-permute-done = f32[8,768]{1,0:T(8,128)S(1)} collective-permute-done((f32[8,768]{1,0:T(8,128)S(1)}, f32[8,768]{1,0:T(8,128)S(1)}, u32[]{:S(2)}, u32[]{:S(2)}) %collective-permute-start) | collective-permute-done | bytes 24608 | tf_op jit(solution)/shard_map/ppermute | solution.py:239
  16.5 0.6 %add.3 = f32[8,768]{1,0:T(8,128)} add(f32[8,768]{1,0:T(8,128)S(1)} %collective-permute-done, f32[8,768]{1,0:T(8,128)S(1)} %ritz_partial_sums.3) | non-fusion elementwise | flops 6144 | bytes 73728 | tf_op jit(solution)/shard_map/add | solution.py:241
  (1 shorter events, 0.0 us)
Async XLA Ops:
  1.9 13.2 %all-to-all-start = ((f32[16,8,128]{2,1,0:T(8,128)}), f32[16,8,128]{2,1,0:T(8,128)S(1)}, u32[]{:S(2)}, u32[]{:S(2)}) async-start(f32[16,8,128]{2,1,0:T(8,128)} %bitcast.4), calls=%async_computation | async-start | bytes 131072 | tf_op jit(solution)/shard_map/all_to_all | solution.py:190
  15.2 1.3 %collective-permute-start = (f32[8,768]{1,0:T(8,128)S(1)}, f32[8,768]{1,0:T(8,128)S(1)}, u32[]{:S(2)}, u32[]{:S(2)}) collective-permute-start(f32[8,768]{1,0:T(8,128)S(1)} %ritz_partial_sums.2), channel_id=1, source_target_pairs={{0,8},{8,0},{1,9},{9,1},{2,10},{10,2},{3,11},{11,3},{4,12},{12,4},... | collective-permute-start | bytes 73736 | tf_op jit(solution)/shard_map/ppermute | solution.py:239

commit v22 on v19

--- a/solution.py
+++ b/solution.py
@@ -165,6 +165,8 @@
     ]
     late = sorted(range(tiles), key=lambda place: (place % ng // (ng // 2), place // ng, place % ng), reverse=True)
     order = [place for pair in zip(late, late[::-1]) for place in pair][:tiles]
+    first = ng - ng // 4 - 1
+    order = [first] + [place for place in order if place != first]
     packed_bytes = 4 * tiles * rows * LANES
     packed = pl.pallas_call(
         functools.partial(filter_kernel, ng, nrow, rows, run, width, cores, order),

time: 15.8 us -> 16.7 us (1.057)
  blocking collectives: 12.3 us -> 13.2 us
    all_to_all x1, blocking collectives: 12.3 us -> 13.2 us  [shards(): lax.all_to_all(packed.reshape(tiles, rows, LANES), ('row', 'core', 'grid'...]
where the time goes in v22:
time: 16.7 us; the launch traced here: 16.5 us
  blocking collectives  13.2 us (79%)
  Pallas kernels  1.56 us (9%)
  waiting for transfers between devices  1.05 us (6%)
  other arithmetic  0.61 us (4%)
    all_to_all x1, blocking collectives, shards(): lax.all_to_all(packed.reshape(tiles, rows, LANES), ('row', 'core', 'grid'...  13.2 us
    pallas_call x1, Pallas kernels, shards(): pl.pallas_call(functools.partial(filter_kernel, ng, nrow, rows, run, widt...  1.3 us
    ppermute x1, waiting for transfers between devices, shards(): terms.append(lax.ppermute(partial_sums(distance), 'core', pairs))  1.05 us
    add x1, other arithmetic, shards(): return functools.reduce(jnp.add, terms)  0.61 us
  transfers between devices with their start and end apart: 1, of which 1 were waited for; matrix products, arithmetic and copies ran while one was open for 0% of the time, Pallas kernels for 1%

profile of v22, /device:TPU:0, one launch (start us, length us, event | category | flops | bytes accessed | tf_op | source)
XLA Modules:
  0.0 16.5 jit_solution(14469222058871718602)
XLA Ops:
  0.0 1.3 %chebyshev_filter.1 = f32[128,128]{1,0:T(8,128)S(1)} custom-call(f32[6,8,128]{2,1,0:T(8,128)} %bitcast.7, s32[6,8,128]{2,1,0:T(8,128)} %bitcast.8, f32[16]{0:T(128)} %refs_2_.1, s32[4]{0:T(128)} %refs_3_.1, f32[4,8]{1,0:T(4,128)} %bitcast.9), custom_call_target="tpu_custom_call" | custom-call | tf_op jit(solution)/shard_map/chebyshev_filter/pallas_call | solution.py:171
  1.3 13.2 %all_to_all.5.got_ref = f32[16,8,128]{2,1,0:T(8,128)S(1)} all-to-all(f32[16,8,128]{2,1,0:T(8,128)S(1)} %bitcast.6), channel_id=1, replica_groups={{5,23,0,22,1,21,2,20,3,7,16,6,17,18,4,19},{13,27,12,26,25,14,24,15,11,2..., dimensions={0} | all-to-all | bytes 131072 | tf_op jit(solution)/shard_map/all_to_all | solution.py:188
  14.5 0.1 ritz_partial_sums.2
  14.6 0.1 collective-permute-start
  14.7 0.1 ritz_partial_sums.3
  14.8 1.0 %collective-permute-done = f32[8,768]{1,0:T(8,128)S(1)} collective-permute-done((f32[8,768]{1,0:T(8,128)S(1)}, f32[8,768]{1,0:T(8,128)S(1)}, u32[]{:S(2)}, u32[]{:S(2)}) %collective-permute-start) | collective-permute-done | bytes 24608 | tf_op jit(solution)/shard_map/ppermute | solution.py:228
  15.9 0.6 %add.3 = f32[8,768]{1,0:T(8,128)} add(f32[8,768]{1,0:T(8,128)S(1)} %collective-permute-done, f32[8,768]{1,0:T(8,128)S(1)} %ritz_partial_sums.3) | non-fusion elementwise | flops 6144 | bytes 73728 | tf_op jit(solution)/shard_map/add | solution.py:230
Async XLA Ops:
  14.6 1.3 %collective-permute-start = (f32[8,768]{1,0:T(8,128)S(1)}, f32[8,768]{1,0:T(8,128)S(1)}, u32[]{:S(2)}, u32[]{:S(2)}) collective-permute-start(f32[8,768]{1,0:T(8,128)S(1)} %ritz_partial_sums.2), channel_id=1, source_target_pairs={{0,8},{8,0},{1,9},{9,1},{2,10},{10,2},{3,11},{11,3},{4,12},{12,4},... | collective-permute-start | bytes 73736 | tf_op jit(solution)/shard_map/ppermute | solution.py:228

commit v23 on v18

--- a/solution.py
+++ b/solution.py
@@ -44,10 +44,13 @@
     return weights[0], pairs
 
 
-def apply(field, diagonal, hop, before):
+def apply(field, diagonal, hop, before, twice_ref):
     ys = len(field)
     planes, xs = field[0].shape
     along_y, along_planes, along_x = [pair_weights(length)[1] for length in (ys, planes, xs)]
+    for y in range(ys):
+        twice_ref[y, pl.ds(0, planes), :] = field[y]
+        twice_ref[y, pl.ds(planes, planes), :] = field[y]
     results = []
     for y in range(ys):
         tile = field[y]
@@ -56,17 +59,18 @@
             total = total - before[y]
         for shifts, weight in along_y:
             total = total + (hop * weight) * functools.reduce(jnp.add, [field[(y - shift) % ys] for shift in shifts])
-        for pairs, axis in ((along_planes, 0), (along_x, 1)):
-            for shifts, weight in pairs:
-                total = total + (hop * weight) * functools.reduce(
-                    jnp.add, [pltpu.roll(tile, shift, axis) for shift in shifts]
-                )
+        for shifts, weight in along_planes:
+            total = total + (hop * weight) * functools.reduce(
+                jnp.add, [twice_ref[y, pl.ds(planes - shift, planes), :] for shift in shifts]
+            )
+        for shifts, weight in along_x:
+            total = total + (hop * weight) * functools.reduce(jnp.add, [pltpu.roll(tile, shift, 1) for shift in shifts])
         results.append(total)
     return results
 
 
 def filter_kernel(ng, copies, rows, run, width, cores, order, *refs):
-    sources, out_ref, held, sems, natural_ref = refs[:5], refs[5], refs[6:11], refs[11], refs[12]
+    sources, out_ref, held, sems, natural_ref, twice_ref = refs[:5], refs[5], refs[6:11], *refs[11:]
     orb_ref, region_ref, table_ref, counts_ref, ritz_ref = held
     transfers = [
         pltpu.make_async_copy(source, target, sems.at[index])
@@ -101,9 +105,9 @@
     band_pos = lax.axis_index("row") * cores + lax.axis_index("core")
     live = (lax.axis_index("grid") < counts_ref[band_pos]).astype(jnp.float32)
     previous = [live * orb_ref[y] for y in range(ys)]
-    current = apply(previous, [0.5 * value for value in diagonal], 0.5 * hop, None)
+    current = apply(previous, [0.5 * value for value in diagonal], 0.5 * hop, None, twice_ref)
     for _ in range(DEGREE - 1):
-        previous, current = current, apply(current, diagonal, hop, previous)
+        previous, current = current, apply(current, diagonal, hop, previous, twice_ref)
 
     blocks = ys // run
     for y in range(ys):
@@ -171,6 +175,7 @@
             pltpu.VMEM((columns, panel), jnp.float32),
             pltpu.SemaphoreType.DMA((5,)),
             pltpu.VMEM((ng * rows, LANES), jnp.float32),
+            pltpu.VMEM((ys, 2 * planes, xs), jnp.float32),
         ],
         compiler_params=pltpu.CompilerParams(vmem_limit_bytes=2 * packed_bytes + 64 * cells + 2**20),
         name="chebyshev_filter",

time: 15.8 us -> 15.8 us (level)
  no operation moved by 1% of the time
where the time goes in v23:
time: 15.8 us; the launch traced here: 15.6 us
  blocking collectives  12.3 us (78%)
  Pallas kernels  1.54 us (10%)
  waiting for transfers between devices  1.05 us (7%)
  other arithmetic  0.61 us (4%)
    all_to_all x1, blocking collectives, shards(): lax.all_to_all(packed.reshape(tiles, rows, LANES), ('row', 'grid'), split...  12.3 us
    pallas_call x1, Pallas kernels, shards(): pl.pallas_call(functools.partial(filter_kernel, ng, nrow, rows, run, widt...  1.3 us
    ppermute x1, waiting for transfers between devices, shards(): terms.append(lax.ppermute(partial_sums(distance), 'core', pairs))  1.05 us
    add x1, other arithmetic, shards(): return functools.reduce(jnp.add, terms)  0.61 us
  transfers between devices with their start and end apart: 1, of which 1 were waited for; matrix products, arithmetic and copies ran while one was open for 0% of the time, Pallas kernels for 1%

profile of v23, /device:TPU:0, one launch (start us, length us, event | category | flops | bytes accessed | tf_op | source)
XLA Modules:
  0.0 15.6 jit_solution(18201425475148173530)
XLA Ops:
  0.0 1.3 %chebyshev_filter.1 = f32[128,128]{1,0:T(8,128)S(1)} custom-call(f32[6,8,128]{2,1,0:T(8,128)} %bitcast.7, s32[6,8,128]{2,1,0:T(8,128)} %bitcast.8, f32[16]{0:T(128)} %refs_2_.1, s32[4]{0:T(128)} %refs_3_.1, f32[4,8]{1,0:T(4,128)} %bitcast.9), custom_call_target="tpu_custom_call" | custom-call | tf_op jit(solution)/shard_map/chebyshev_filter/pallas_call | solution.py:165
  1.3 12.3 %all_to_all.5.got_ref = f32[16,8,128]{2,1,0:T(8,128)S(1)} all-to-all(f32[16,8,128]{2,1,0:T(8,128)S(1)} %bitcast.6), channel_id=1, replica_groups={{23,0,22,1,21,2,20,3,7,16,6,17,5,18,4,19},{31,8,30,9,29,10,28,11,15,24,..., dimensions={0} | all-to-all | bytes 131072 | tf_op jit(solution)/shard_map/all_to_all | solution.py:183
  13.6 0.1 ritz_partial_sums.2
  13.7 0.1 collective-permute-start
  13.8 0.1 ritz_partial_sums.3
  13.9 1.1 %collective-permute-done = f32[8,768]{1,0:T(8,128)S(1)} collective-permute-done((f32[8,768]{1,0:T(8,128)S(1)}, f32[8,768]{1,0:T(8,128)S(1)}, u32[]{:S(2)}, u32[]{:S(2)}) %collective-permute-start) | collective-permute-done | bytes 24608 | tf_op jit(solution)/shard_map/ppermute | solution.py:220
  15.0 0.6 %add.3 = f32[8,768]{1,0:T(8,128)} add(f32[8,768]{1,0:T(8,128)S(1)} %collective-permute-done, f32[8,768]{1,0:T(8,128)S(1)} %ritz_partial_sums.3) | non-fusion elementwise | flops 6144 | bytes 73728 | tf_op jit(solution)/shard_map/add | solution.py:222
Async XLA Ops:
  13.7 1.3 %collective-permute-start = (f32[8,768]{1,0:T(8,128)S(1)}, f32[8,768]{1,0:T(8,128)S(1)}, u32[]{:S(2)}, u32[]{:S(2)}) collective-permute-start(f32[8,768]{1,0:T(8,128)S(1)} %ritz_partial_sums.2), channel_id=1, source_target_pairs={{0,8},{8,0},{1,9},{9,1},{2,10},{10,2},{3,11},{11,3},{4,12},{12,4},... | collective-permute-start | bytes 73736 | tf_op jit(solution)/shard_map/ppermute | solution.py:220

commit v24 on v18

v24 whole, which is shorter than its diff:
```python
import functools

import jax
import jax.numpy as jnp
from jax import lax
from jax.experimental import pallas as pl
from jax.experimental.pallas import tpu as pltpu
from jax.sharding import PartitionSpec as P

DEGREE = 4

COEFFICIENTS = (
    -5369.0 / 1800.0,
    12.0 / 7.0,
    -15.0 / 56.0,
    10.0 / 189.0,
    -1.0 / 112.0,
    2.0 / 1925.0,
    -1.0 / 16632.0,
)
SPACING = 0.5
LOWER = 6.0
UPPER = 46.0
HALF = (UPPER - LOWER) / 2.0
CENTRE = (UPPER + LOWER) / 2.0
SCALE = 2.0 / HALF
HOP = -0.5 / (SPACING * SPACING) * SCALE
LANES = 128
SUBLANES = 8


def ring_weights(length):
    weights = [0.0] * length
    for offset in range(1, 7):
        weights[offset % length] += COEFFICIENTS[offset]
        weights[-offset % length] += COEFFICIENTS[offset]
    return weights


def pair_weights(length):
    weights = ring_weights(length)
    pairs = []
    for distance in range(1, length // 2 + 1):
        if weights[distance] != 0.0:
            pairs.append((sorted({distance, length - distance}), weights[distance]))
    return weights[0], pairs


def apply(field, diagonal, hop, before):
    ys = len(field)
    planes, xs = field[0].shape
    along_y, along_planes, along_x = [pair_weights(length)[1] for length in (ys, planes, xs)]
    results = []
    for y in range(ys):
        tile = field[y]
        total = diagonal[y] * tile
        if before is not None:
            total = total - before[y]
        for shifts, weight in along_y:
            total = total + (hop * weight) * functools.reduce(jnp.add, [field[(y - shift) % ys] for shift in shifts])
        for pairs, axis in ((along_planes, 0), (along_x, 1)):
            for shifts, weight in pairs:
                total = total + (hop * weight) * functools.reduce(
                    jnp.add, [pltpu.roll(tile, shift, axis) for shift in shifts]
                )
        results.append(total)
    return results


def pack_ritz(ritz_ref, natural_ref, ng, rows, run, width):
    columns, panel = ritz_ref.shape
    per_row = LANES // width
    for row in range(-(-columns // per_row)):
        line = jnp.zeros((1, LANES), jnp.float32)
        for slot in range(min(per_row, columns - row * per_row)):
            piece = jnp.concatenate(
                [ritz_ref[pl.ds(row * per_row + slot, 1), :], jnp.zeros((1, LANES - panel), jnp.float32)], axis=1
            )
            line = line + (pltpu.roll(piece, slot * width, 1) if slot else piece)
        natural_ref[pl.ds(run + row, ng, stride=rows), :] = jnp.broadcast_to(line, (ng, LANES))


def filter_into(field, diagonal, natural_ref, rows, run):
    ys, planes = len(field), field[0].shape[0]
    previous = field
    current = apply(previous, [0.5 * value for value in diagonal], 0.5 * HOP, None)
    for _ in range(DEGREE - 1):
        previous, current = current, apply(current, diagonal, HOP, previous)
    blocks = ys // run
    for y in range(ys):
        natural_ref[pl.ds((y // run) * rows + y % run, planes, stride=blocks * rows), :] = current[y]


def load_and_filter(ng, rows, run, width, cores, sources, held, sems, natural_ref):
    orb_ref, region_ref, table_ref, counts_ref, ritz_ref = held
    transfers = [
        pltpu.make_async_copy(source, target, sems.at[index])
        for index, (source, target) in enumerate(zip(sources, held))
    ]
    for transfer in transfers:
        transfer.start()
    for transfer in transfers:
        transfer.wait()
    pack_ritz(ritz_ref, natural_ref, ng, rows, run, width)
    ys, planes, xs = orb_ref.shape
    centre_weight = 3.0 * COEFFICIENTS[0] + sum(pair_weights(n)[0] for n in (planes, ys, xs))
    diagonal = []
    for y in range(ys):
        region = region_ref[y]
        potential = jnp.zeros((planes, xs), jnp.float32)
        for index in range(table_ref.shape[0]):
            potential = jnp.where(region == index, table_ref[index], potential)
        diagonal.append(SCALE * potential + (HOP * centre_weight - SCALE * CENTRE))

    def live(core):
        band_pos = lax.axis_index("row") * cores + core
        return (lax.axis_index("grid") < counts_ref[band_pos]).astype(jnp.float32)

    mask = live(lax.axis_index("core"))
    filter_into([mask * orb_ref[y] for y in range(ys)], diagonal, natural_ref, rows, run)
    return diagonal, live


def filter_kernel(ng, rows, run, width, cores, order, *refs):
    sources, out_ref, held, sems, natural_ref = refs[:5], refs[5], refs[6:11], refs[11], refs[12]
    load_and_filter(ng, rows, run, width, cores, sources, held, sems, natural_ref)
    for place, chip in enumerate(order):
        out_ref[pl.ds(place * rows, rows), :] = natural_ref[pl.ds(chip % ng * rows, rows), :]


def own_kernel(ng, rows, run, width, cores, *refs):
    sources, (natural_ref, diagonal_ref, mask_ref), held, sems = refs[:5], refs[5:8], refs[8:13], refs[13]
    diagonal, live = load_and_filter(ng, rows, run, width, cores, sources, held, sems, natural_ref)
    for y, value in enumerate(diagonal):
        diagonal_ref[y] = value
    mask_ref[...] = jnp.broadcast_to(live(1 - lax.axis_index("core")), mask_ref.shape)


def other_kernel(ng, rows, run, width, order, orb_ref, ritz_ref, natural_ref, diagonal_ref, mask_ref, out_ref, held_ref):
    pack_ritz(ritz_ref, held_ref, ng, rows, run, width)
    ys = orb_ref.shape[0]
    filter_into([mask_ref[...] * orb_ref[y] for y in range(ys)], [diagonal_ref[y] for y in range(ys)], held_ref, rows, run)
    for place, chip in enumerate(order):
        tile = pl.ds(chip % ng * rows, rows)
        out_ref[pl.ds(2 * place * rows, rows), :] = natural_ref[tile, :]
        out_ref[pl.ds((2 * place + 1) * rows, rows), :] = held_ref[tile, :]


def rotate_kernel(nrow, ng, rows, run, width, columns, cores, order, got_ref, out_ref, ritz_ref):
    wanted = out_ref.shape[0]
    holders = wanted // columns
    sublane = lax.broadcasted_iota(jnp.int32, (wanted, LANES), 0)
    block = lax.axis_index("row") * cores + lax.axis_index("core")
    for tile in range(2):
        for place, source in enumerate(order):
            ritz_ref[tile, source] = got_ref[place, pl.ds(tile * rows + run, 1), :]
    acc = [jnp.zeros((wanted, LANES), jnp.float32) for _ in range(run)]
    for tile in range(2):
        for row in range(nrow):
            lines = jnp.zeros((wanted, LANES), jnp.float32)
            for k in range(holders):
                line = ritz_ref[tile, row * ng + block * holders + k]
                lines = jnp.where(sublane // columns == k, jnp.broadcast_to(line, (wanted, LANES)), lines)
            for r in range(ng):
                weight = jnp.take_along_axis(lines, sublane % columns * width + r, axis=1)
                for y in range(run):
                    acc[y] = acc[y] + weight * got_ref[order.index(row * ng + r), pl.ds(tile * rows + y, 1), :]
    for y in range(run):
        out_ref[:, pl.ds(y * LANES, LANES)] = acc[y]


def shards(nrow, cores, ng, orbitals, region, potential_table, counts, ritz):
    _, planes, ys, xs = orbitals.shape
    cells = planes * ys * xs
    panel, columns = ritz.shape
    run = cells // ng // xs
    width = 1
    while width < panel:
        width *= 2
    per_row = LANES // width
    ritz_rows = -(-columns // per_row)
    rows = -(-(run + ritz_rows) // SUBLANES) * SUBLANES
    tiles = nrow * ng
    vmem = pl.BlockSpec(memory_space=pltpu.VMEM)
    hbm = pl.BlockSpec(memory_space=pltpu.HBM)
    inputs = [
        pltpu.with_memory_space_constraint(value, pltpu.HBM)
        for value in (
            jnp.transpose(orbitals[0], (1, 0, 2)), jnp.transpose(region, (1, 0, 2)), potential_table, counts, ritz.T
        )
    ]
    late = sorted(range(tiles), key=lambda place: (place % ng // (ng // 2), place // ng, place % ng), reverse=True)
    order = [place for pair in zip(late, late[::-1]) for place in pair][:tiles]
    packed_bytes = 4 * tiles * rows * LANES
    loaded = [
        pltpu.VMEM((ys, planes, xs), jnp.float32),
        pltpu.VMEM((ys, planes, xs), jnp.int32),
        pltpu.SMEM(potential_table.shape, jnp.float32),
        pltpu.SMEM(counts.shape, jnp.int32),
        pltpu.VMEM((columns, panel), jnp.float32),
        pltpu.SemaphoreType.DMA((5,)),
    ]
    limit = pltpu.CompilerParams(vmem_limit_bytes=4 * packed_bytes + 64 * cells + 2**20)
    natural = jax.ShapeDtypeStruct((ng * rows, LANES), jnp.float32)
    across = [(core, cores - 1 - core) for core in range(cores)]

    def exchange(packed, height):
        return lax.all_to_all(
            packed.reshape(tiles, height, LANES), ("row", "grid"), split_axis=0, concat_axis=0, tiled=True,
            axis_index_groups=[order],
        )

    if cores == 2 and columns * width <= LANES and tiles <= 64 and panel == ng and panel <= 16:
        other_orb = jnp.transpose(lax.ppermute(orbitals, "core", across)[0], (1, 0, 2))
        other_ritz = lax.ppermute(ritz, "core", across).T
        own, diagonal, mask = pl.pallas_call(
            functools.partial(own_kernel, ng, rows, run, width, cores),
            out_shape=[
                natural,
                jax.ShapeDtypeStruct((ys, planes, xs), jnp.float32),
                jax.ShapeDtypeStruct((planes, xs), jnp.float32),
            ],
            in_specs=[hbm] * 5,
            out_specs=[vmem] * 3,
            scratch_shapes=loaded,
            compiler_params=limit,
            name="own_filter",
        )(*inputs)
        packed = pl.pallas_call(
            functools.partial(other_kernel, ng, rows, run, width, order),
            out_shape=jax.ShapeDtypeStruct((2 * tiles * rows, LANES), jnp.float32),
            in_specs=[vmem] * 5,
            out_specs=vmem,
            scratch_shapes=[pltpu.VMEM((ng * rows, LANES), jnp.float32)],
            compiler_params=limit,
            name="other_filter",
        )(other_orb, other_ritz, own, diagonal, mask)
        return pl.pallas_call(
            functools.partial(rotate_kernel, nrow, ng, rows, run, width, columns, cores, order),
            out_shape=jax.ShapeDtypeStruct((panel, run * LANES), jnp.float32),
            in_specs=[vmem],
            out_specs=vmem,
            scratch_shapes=[pltpu.VMEM((2, tiles, 1, LANES), jnp.float32)],
            compiler_params=limit,
            name="ritz_rotation",
        )(exchange(packed, 2 * rows))

    packed = pl.pallas_call(
        functools.partial(filter_kernel, ng, rows, run, width, cores, order),
        out_shape=jax.ShapeDtypeStruct((tiles * rows, LANES), jnp.float32),
        in_specs=[hbm] * 5,
        out_specs=vmem,
        scratch_shapes=loaded + [pltpu.VMEM((ng * rows, LANES), jnp.float32)],
        compiler_params=limit,
        name="chebyshev_filter",
    )(*inputs)
    by_source = exchange(packed, rows)[jnp.argsort(jnp.array(order))].reshape(nrow, ng, rows, LANES)
    fields = by_source[:, :, :run].reshape(tiles, run * LANES)
    blocks = by_source[:, :, run : run + ritz_rows].reshape(nrow, ng, ritz_rows * per_row, width)

    def partial_sums(distance):
        holders = panel // columns
        block = lax.axis_index("row") * cores + lax.rem(lax.axis_index("core") + distance, cores)
        mine = lax.dynamic_slice_in_dim(blocks, block * holders, holders, axis=1)
        return lax.dot_general(
            jnp.transpose(mine[:, :, :columns, :panel], (0, 3, 1, 2)).reshape(tiles, panel),
            fields,
            (((0,), (0,)), ((), ())),
            precision=lax.Precision.HIGHEST,
            preferred_element_type=jnp.float32,
        )

    total = partial_sums(0)
    if cores == 2:
        total = lax.ppermute(partial_sums(1), "core", across) + total
    return total


def solution(mesh):
    bands, ng = mesh.shape["band"], mesh.shape["grid"]
    cores = 2 if bands % 2 == 0 else 1
    nrow = bands // cores
    split = jax.sharding.Mesh(mesh.devices.reshape(nrow, cores, ng), ("row", "core", "grid"))
    return jax.shard_map(
        functools.partial(shards, nrow, cores, ng),
        mesh=split,
        in_specs=(P(("row", "core", "grid"), None, None, None), P(), P(), P(), P(("row", "core"), "grid")),
        out_specs=P(("row", "core"), "grid"),
        check_vma=False,
    )
```

time: 15.8 us -> 16.7 us (1.057)
  blocking collectives: 12.3 us -> 13.5 us
  waiting for transfers between devices: 1.05 us -> 0.02 us
  Pallas kernels: 1.54 us -> 2.49 us
  other arithmetic: 0.61 us -> 0 us
  starting transfers between devices: 0.07 us -> 0.51 us
    all_to_all x1, blocking collectives: 12.3 us -> 13.5 us  [exchange(): lax.all_to_all(packed.reshape(tiles, height, LANES), ('row', 'grid'), spl...]
    ppermute x1 -> x2, waiting for transfers between devices: 1.05 us -> 0.02 us  [the longest x1 0.02 us: shards(): other_ritz = lax.ppermute(ritz, 'core', across).T]
    pallas_call x3, Pallas kernels: 1.54 us -> 2.49 us  [the longest x1 1.28 us: shards(): pl.pallas_call(functools.partial(own_kernel, ng, rows, run, width, cores)...]
    add x1 -> x0, other arithmetic: 0.61 us -> none  [shards(): return functools.reduce(jnp.add, terms)]
    ppermute x1 -> x2, starting transfers between devices: 0.07 us -> 0.51 us  [the longest x1 0.45 us: shards(): lax.ppermute(orbitals, 'core', across)[0]]
  transfers between devices with their start and end apart: 1 -> 2, of which waited for: 1 -> 0; matrix products, arithmetic and copies ran while one was open for 0% -> 0% of each run, Pallas kernels for 1% -> 8%
where the time goes in v24:
time: 16.7 us; the launch traced here: 16.5 us
  blocking collectives  13.5 us (81%)
  Pallas kernels  2.49 us (15%)
  starting transfers between devices  0.51 us (3%)
    all_to_all x1, blocking collectives, exchange(): lax.all_to_all(packed.reshape(tiles, height, LANES), ('row', 'grid'), spl...  13.5 us
    pallas_call x1, Pallas kernels, shards(): pl.pallas_call(functools.partial(own_kernel, ng, rows, run, width, cores)...  1.28 us
    pallas_call x1, Pallas kernels, shards(): pl.pallas_call(functools.partial(rotate_kernel, nrow, ng, rows, run, widt...  0.78 us
    ppermute x1, starting transfers between devices, shards(): lax.ppermute(orbitals, 'core', across)[0]  0.45 us
    pallas_call x1, Pallas kernels, shards(): pl.pallas_call(functools.partial(other_kernel, ng, rows, run, width, orde...  0.43 us
  transfers between devices with their start and end apart: 2, of which 0 were waited for; matrix products, arithmetic and copies ran while one was open for 0% of the time, Pallas kernels for 8%

profile of v24, /device:TPU:0, one launch (start us, length us, event | category | flops | bytes accessed | tf_op | source)
XLA Modules:
  0.0 16.5 jit_solution(7621768160264527957)
XLA Ops:
  0.0 0.5 %collective-permute-start = (f32[1,8,6,128]{3,1,2,0:T(8,128)}, f32[1,8,6,128]{3,1,2,0:T(8,128)S(1)}, u32[]{:S(2)}, u32[]{:S(2)}) collective-permute-start(f32[1,8,6,128]{3,1,2,0:T(8,128)} %param.5), channel_id=1, source_target_pairs={{0,8},{8,0},{1,9},{9,1},{2,10},{10,2},{3,11},{11,3},{4,12},{12,4},... | collective-permute-start | bytes 73736 | tf_op jit(solution)/shard_map/ppermute | solution.py:214
  0.5 0.1 collective-permute-start.1
  0.5 1.3 %own_filter.1 = (f32[64,128]{1,0:T(8,128)S(1)}, f32[6,8,128]{2,1,0:T(8,128)S(1)}, f32[8,128]{1,0:T(8,128)S(1)}) custom-call(f32[6,8,128]{2,1,0:T(8,128)} %bitcast.14, s32[6,8,128]{2,1,0:T(8,128)} %bitcast.13, f32[16]{0:T(128)} %refs_2_.1, s32[4]{0:T(128)} %refs_3_.1, f32[4,8]{1,0:T(4,128)} %bitcast.15), custom_call_target="tpu_custom_call" | custom-call | tf_op jit(solution)/shard_map/own_filter/pallas_call | solution.py:216
  1.8 0.0 collective-permute-done.1
  1.8 0.0 collective-permute-done
  1.8 0.4 %other_filter.1 = f32[256,128]{1,0:T(8,128)S(1)} custom-call(f32[6,8,128]{2,1,0:T(8,128)S(1)} %bitcast.11, f32[4,8]{1,0:T(4,128)S(1)} %bitcast.12, f32[64,128]{1,0:T(8,128)S(1)} %get-tuple-element.8.natural_ref, f32[6,8,128]{2,1,0:T(8,128)S(1)} %get-tuple-element.9.diagonal_ref, f32[8,128]{1,0:T(8,128)S(1)} %get-tuple-element.10.mask_ref), custom_call_target="tpu_custom_call" | custom-call | tf_op jit(solution)/shard_map/other_filter/pallas_call | solution.py:229
  2.3 13.5 %all_to_all.5.got_ref = f32[16,16,128]{2,1,0:T(8,128)S(1)} all-to-all(f32[16,16,128]{2,1,0:T(8,128)S(1)} %bitcast.10), channel_id=1, replica_groups={{23,0,22,1,21,2,20,3,7,16,6,17,5,18,4,19},{31,8,30,9,29,10,28,11,15,24,..., dimensions={0} | all-to-all | bytes 262144 | tf_op jit(solution)/shard_map/all_to_all | solution.py:208
  15.7 0.8 %ritz_rotation.1 = f32[8,768]{1,0:T(8,128)} custom-call(f32[16,16,128]{2,1,0:T(8,128)S(1)} %all_to_all.5.got_ref), custom_call_target="tpu_custom_call" | custom-call | tf_op jit(solution)/shard_map/ritz_rotation/pallas_call | solution.py:238
Async XLA Ops:
  0.0 1.8 %collective-permute-start = (f32[1,8,6,128]{3,1,2,0:T(8,128)}, f32[1,8,6,128]{3,1,2,0:T(8,128)S(1)}, u32[]{:S(2)}, u32[]{:S(2)}) collective-permute-start(f32[1,8,6,128]{3,1,2,0:T(8,128)} %param.5), channel_id=1, source_target_pairs={{0,8},{8,0},{1,9},{9,1},{2,10},{10,2},{3,11},{11,3},{4,12},{12,4},... | collective-permute-start | bytes 73736 | tf_op jit(solution)/shard_map/ppermute | solution.py:214
  0.5 1.4 %collective-permute-start.1 = (f32[8,4]{0,1:T(4,128)}, f32[8,4]{0,1:T(4,128)S(1)}, u32[]{:S(2)}, u32[]{:S(2)}) collective-permute-start(f32[8,4]{0,1:T(4,128)} %param.9), channel_id=1, source_target_pairs={{0,8},{8,0},{1,9},{9,1},{2,10},{10,2},{3,11},{11,3},{4,12},{12,4},... | collective-permute-start | bytes 392 | tf_op jit(solution)/shard_map/ppermute | solution.py:215

commit v25 on v18

--- a/solution.py
+++ b/solution.py
@@ -65,7 +65,7 @@
     return results
 
 
-def filter_kernel(ng, copies, rows, run, width, cores, order, *refs):
+def filter_kernel(ng, copies, rows, used, run, width, cores, order, *refs):
     sources, out_ref, held, sems, natural_ref = refs[:5], refs[5], refs[6:11], refs[11], refs[12]
     orb_ref, region_ref, table_ref, counts_ref, ritz_ref = held
     transfers = [
@@ -111,12 +111,12 @@
     for copy in range(copies):
         for tile in range(ng):
             place = order.index(copy * ng + tile)
-            out_ref[pl.ds(place * rows, rows), :] = natural_ref[pl.ds(tile * rows, rows), :]
-
-
-def partial_kernel(nrow, ng, run, width, columns, cores, order, distance, got_ref, out_ref, ritz_ref):
+            out_ref[pl.ds(place * used, used), :] = natural_ref[pl.ds(tile * rows, used), :]
+
+
+def partial_kernel(nrow, ng, used, run, width, columns, cores, order, distance, got_ref, out_ref, ritz_ref):
     for place, source in enumerate(order):
-        ritz_ref[source] = got_ref[place, pl.ds(run, 1), :]
+        ritz_ref[source] = got_ref[pl.ds(place * used + run, 1), :]
     wanted = out_ref.shape[0]
     holders = wanted // columns
     sublane = lax.broadcasted_iota(jnp.int32, (wanted, LANES), 0)
@@ -130,7 +130,7 @@
         for r in range(ng):
             weight = jnp.take_along_axis(lines, sublane % columns * width + r, axis=1)
             for y in range(run):
-                acc[y] = acc[y] + weight * got_ref[order.index(row * ng + r), pl.ds(y, 1), :]
+                acc[y] = acc[y] + weight * got_ref[pl.ds(order.index(row * ng + r) * used + y, 1), :]
     for y in range(run):
         out_ref[:, pl.ds(y * LANES, LANES)] = acc[y]
 
@@ -145,7 +145,8 @@
         width *= 2
     per_row = LANES // width
     ritz_rows = -(-columns // per_row)
-    rows = -(-(run + ritz_rows) // SUBLANES) * SUBLANES
+    used = run + ritz_rows
+    rows = -(-used // SUBLANES) * SUBLANES
     tiles = nrow * ng
     vmem = pl.BlockSpec(memory_space=pltpu.VMEM)
     hbm = pl.BlockSpec(memory_space=pltpu.HBM)
@@ -159,8 +160,8 @@
     order = [place for pair in zip(late, late[::-1]) for place in pair][:tiles]
     packed_bytes = 4 * tiles * rows * LANES
     packed = pl.pallas_call(
-        functools.partial(filter_kernel, ng, nrow, rows, run, width, cores, order),
-        out_shape=jax.ShapeDtypeStruct((tiles * rows, LANES), jnp.float32),
+        functools.partial(filter_kernel, ng, nrow, rows, used, run, width, cores, order),
+        out_shape=jax.ShapeDtypeStruct((tiles * used, LANES), jnp.float32),
         in_specs=[hbm] * 5,
         out_specs=vmem,
         scratch_shapes=[
@@ -176,14 +177,14 @@
         name="chebyshev_filter",
     )(*inputs)
     got = lax.all_to_all(
-        packed.reshape(tiles, rows, LANES), ("row", "grid"), split_axis=0, concat_axis=0, tiled=True,
+        packed.reshape(tiles * used, 1, LANES), ("row", "grid"), split_axis=0, concat_axis=0, tiled=True,
         axis_index_groups=[order],
-    )
+    ).reshape(tiles * used, LANES)
     sum_shape = jax.ShapeDtypeStruct((panel, run * LANES), jnp.float32)
     if columns * width <= LANES and tiles <= 64 and panel == ng and panel <= 16:
         def partial_sums(distance):
             return pl.pallas_call(
-                functools.partial(partial_kernel, nrow, ng, run, width, columns, cores, order, distance),
+                functools.partial(partial_kernel, nrow, ng, used, run, width, columns, cores, order, distance),
                 out_shape=sum_shape,
                 in_specs=[vmem],
                 out_specs=vmem,
@@ -194,7 +195,7 @@
 
     else:
         holders = panel // columns
-        by_source = got[jnp.argsort(jnp.array(order))].reshape(nrow, ng, rows, LANES)
+        by_source = got.reshape(tiles, used, LANES)[jnp.argsort(jnp.array(order))].reshape(nrow, ng, used, LANES)
         fields = by_source[:, :, :run].reshape(tiles, run * LANES)
         blocks = by_source[:, :, run : run + ritz_rows].reshape(nrow, ng, ritz_rows * per_row, width)
 

time: 15.8 us -> 15.7 us (level)
  no operation moved by 1% of the time
where the time goes in v25:
time: 15.7 us; the launch traced here: 15.5 us
  blocking collectives  12.2 us (78%)
  Pallas kernels  1.54 us (10%)
  waiting for transfers between devices  1.05 us (7%)
  other arithmetic  0.61 us (4%)
    all_to_all x1, blocking collectives, shards(): lax.all_to_all(packed.reshape(tiles * used, 1, LANES), ('row', 'grid'), s...  12.2 us
    pallas_call x1, Pallas kernels, shards(): pl.pallas_call(functools.partial(filter_kernel, ng, nrow, rows, used, run...  1.3 us
    ppermute x1, waiting for transfers between devices, shards(): terms.append(lax.ppermute(partial_sums(distance), 'core', pairs))  1.05 us
    add x1, other arithmetic, shards(): return functools.reduce(jnp.add, terms)  0.61 us
  transfers between devices with their start and end apart: 1, of which 1 were waited for; matrix products, arithmetic and copies ran while one was open for 0% of the time, Pallas kernels for 1%

profile of v25, /device:TPU:0, one launch (start us, length us, event | category | flops | bytes accessed | tf_op | source)
XLA Modules:
  0.0 15.5 jit_solution(16200275028783912333)
XLA Ops:
  0.0 1.3 %chebyshev_filter.1 = f32[112,128]{1,0:T(8,128)S(1)} custom-call(f32[6,8,128]{2,1,0:T(8,128)} %bitcast.12, s32[6,8,128]{2,1,0:T(8,128)} %bitcast.13, f32[16]{0:T(128)} %refs_2_.1, s32[4]{0:T(128)} %refs_3_.1, f32[4,8]{1,0:T(4,128)} %bitcast.14), custom_call_target="tpu_custom_call" | custom-call | tf_op jit(solution)/shard_map/chebyshev_filter/pallas_call | solution.py:162
  1.3 12.2 %all_to_all.5 = f32[112,1,128]{2,1,0:T(1,128)S(1)} all-to-all(f32[112,1,128]{2,1,0:T(1,128)S(1)} %bitcast.11), channel_id=1, replica_groups={{23,0,22,1,21,2,20,3,7,16,6,17,5,18,4,19},{31,8,30,9,29,10,28,11,15,24,..., dimensions={0} | all-to-all | bytes 114688 | tf_op jit(solution)/shard_map/all_to_all | solution.py:179
  13.5 0.1 ritz_partial_sums.2
  13.6 0.1 collective-permute-start
  13.7 0.1 ritz_partial_sums.3
  13.8 1.1 %collective-permute-done = f32[8,768]{1,0:T(8,128)S(1)} collective-permute-done((f32[8,768]{1,0:T(8,128)S(1)}, f32[8,768]{1,0:T(8,128)S(1)}, u32[]{:S(2)}, u32[]{:S(2)}) %collective-permute-start) | collective-permute-done | bytes 24608 | tf_op jit(solution)/shard_map/ppermute | solution.py:216
  14.9 0.6 %add.3 = f32[8,768]{1,0:T(8,128)} add(f32[8,768]{1,0:T(8,128)S(1)} %collective-permute-done, f32[8,768]{1,0:T(8,128)S(1)} %ritz_partial_sums.3) | non-fusion elementwise | flops 6144 | bytes 73728 | tf_op jit(solution)/shard_map/add | solution.py:218
Async XLA Ops:
  13.6 1.3 %collective-permute-start = (f32[8,768]{1,0:T(8,128)S(1)}, f32[8,768]{1,0:T(8,128)S(1)}, u32[]{:S(2)}, u32[]{:S(2)}) collective-permute-start(f32[8,768]{1,0:T(8,128)S(1)} %ritz_partial_sums.2), channel_id=1, source_target_pairs={{0,8},{8,0},{1,9},{9,1},{2,10},{10,2},{3,11},{11,3},{4,12},{12,4},... | collective-permute-start | bytes 73736 | tf_op jit(solution)/shard_map/ppermute | solution.py:216

commit v26 on v25

--- a/solution.py
+++ b/solution.py
@@ -63,6 +63,13 @@
                 )
         results.append(total)
     return results
+
+
+def place_of(chip, order):
+    place = order.index(chip)
+    if place == 0:
+        return place
+    return jnp.where(lax.axis_index("core") == 0, place, len(order) - place)
 
 
 def filter_kernel(ng, copies, rows, used, run, width, cores, order, *refs):
@@ -110,13 +117,14 @@
         natural_ref[pl.ds((y // run) * rows + y % run, planes, stride=blocks * rows), :] = current[y]
     for copy in range(copies):
         for tile in range(ng):
-            place = order.index(copy * ng + tile)
+            place = place_of(copy * ng + tile, order)
             out_ref[pl.ds(place * used, used), :] = natural_ref[pl.ds(tile * rows, used), :]
 
 
 def partial_kernel(nrow, ng, used, run, width, columns, cores, order, distance, got_ref, out_ref, ritz_ref):
-    for place, source in enumerate(order):
-        ritz_ref[source] = got_ref[pl.ds(place * used + run, 1), :]
+    places = [place_of(chip, order) for chip in range(nrow * ng)]
+    for chip, place in enumerate(places):
+        ritz_ref[chip] = got_ref[pl.ds(place * used + run, 1), :]
     wanted = out_ref.shape[0]
     holders = wanted // columns
     sublane = lax.broadcasted_iota(jnp.int32, (wanted, LANES), 0)
@@ -130,7 +138,7 @@
         for r in range(ng):
             weight = jnp.take_along_axis(lines, sublane % columns * width + r, axis=1)
             for y in range(run):
-                acc[y] = acc[y] + weight * got_ref[pl.ds(order.index(row * ng + r) * used + y, 1), :]
+                acc[y] = acc[y] + weight * got_ref[pl.ds(places[row * ng + r] * used + y, 1), :]
     for y in range(run):
         out_ref[:, pl.ds(y * LANES, LANES)] = acc[y]
 
@@ -177,8 +185,11 @@
         name="chebyshev_filter",
     )(*inputs)
     got = lax.all_to_all(
-        packed.reshape(tiles * used, 1, LANES), ("row", "grid"), split_axis=0, concat_axis=0, tiled=True,
-        axis_index_groups=[order],
+        packed.reshape(tiles * used, 1, LANES), ("row", "core", "grid"), split_axis=0, concat_axis=0, tiled=True,
+        axis_index_groups=[
+            [(chip // ng * cores + core) * ng + chip % ng for chip in (order[:1] + order[:0:-1] if core else order)]
+            for core in range(cores)
+        ],
     ).reshape(tiles * used, LANES)
     sum_shape = jax.ShapeDtypeStruct((panel, run * LANES), jnp.float32)
     if columns * width <= LANES and tiles <= 64 and panel == ng and panel <= 16:
@@ -195,7 +206,7 @@
 
     else:
         holders = panel // columns
-        by_source = got.reshape(tiles, used, LANES)[jnp.argsort(jnp.array(order))].reshape(nrow, ng, used, LANES)
+        by_source = got.reshape(tiles, used, LANES)[jnp.stack([place_of(chip, order) for chip in range(tiles)])].reshape(nrow, ng, used, LANES)
         fields = by_source[:, :, :run].reshape(tiles, run * LANES)
         blocks = by_source[:, :, run : run + ritz_rows].reshape(nrow, ng, ritz_rows * per_row, width)
 

time: 15.7 us -> 15.7 us (level)
  no operation moved by 1% of the time
where the time goes in v26:
time: 15.7 us; the launch traced here: 15.5 us
  blocking collectives  12.2 us (78%)
  Pallas kernels  1.56 us (10%)
  waiting for transfers between devices  1.05 us (7%)
  other arithmetic  0.61 us (4%)
    all_to_all x1, blocking collectives, shards(): lax.all_to_all(packed.reshape(tiles * used, 1, LANES), ('row', 'core', 'g...  12.2 us
    pallas_call x1, Pallas kernels, shards(): pl.pallas_call(functools.partial(filter_kernel, ng, nrow, rows, used, run...  1.3 us
    ppermute x1, waiting for transfers between devices, shards(): terms.append(lax.ppermute(partial_sums(distance), 'core', pairs))  1.05 us
    add x1, other arithmetic, shards(): return functools.reduce(jnp.add, terms)  0.61 us
  transfers between devices with their start and end apart: 1, of which 1 were waited for; matrix products, arithmetic and copies ran while one was open for 0% of the time, Pallas kernels for 1%

profile of v26, /device:TPU:0, one launch (start us, length us, event | category | flops | bytes accessed | tf_op | source)
XLA Modules:
  0.0 15.5 jit_solution(1081298036669906515)
XLA Ops:
  0.0 1.3 %chebyshev_filter.1 = f32[112,128]{1,0:T(8,128)S(1)} custom-call(f32[6,8,128]{2,1,0:T(8,128)} %bitcast.12, s32[6,8,128]{2,1,0:T(8,128)} %bitcast.13, f32[16]{0:T(128)} %refs_2_.1, s32[4]{0:T(128)} %refs_3_.1, f32[4,8]{1,0:T(4,128)} %bitcast.14), custom_call_target="tpu_custom_call" | custom-call | tf_op jit(solution)/shard_map/chebyshev_filter/pallas_call | solution.py:170
  1.3 12.2 %all_to_all.5 = f32[112,1,128]{2,1,0:T(1,128)S(1)} all-to-all(f32[112,1,128]{2,1,0:T(1,128)S(1)} %bitcast.11), channel_id=1, replica_groups={{23,0,22,1,21,2,20,3,7,16,6,17,5,18,4,19},{31,27,12,26,13,25,14,24,15,1..., dimensions={0} | all-to-all | bytes 114688 | tf_op jit(solution)/shard_map/all_to_all | solution.py:187
  13.5 0.1 ritz_partial_sums.2
  13.6 0.1 collective-permute-start
  13.7 0.1 ritz_partial_sums.3
  13.9 1.0 %collective-permute-done = f32[8,768]{1,0:T(8,128)S(1)} collective-permute-done((f32[8,768]{1,0:T(8,128)S(1)}, f32[8,768]{1,0:T(8,128)S(1)}, u32[]{:S(2)}, u32[]{:S(2)}) %collective-permute-start) | collective-permute-done | bytes 24608 | tf_op jit(solution)/shard_map/ppermute | solution.py:227
  14.9 0.6 %add.3 = f32[8,768]{1,0:T(8,128)} add(f32[8,768]{1,0:T(8,128)S(1)} %collective-permute-done, f32[8,768]{1,0:T(8,128)S(1)} %ritz_partial_sums.3) | non-fusion elementwise | flops 6144 | bytes 73728 | tf_op jit(solution)/shard_map/add | solution.py:229
Async XLA Ops:
  13.6 1.3 %collective-permute-start = (f32[8,768]{1,0:T(8,128)S(1)}, f32[8,768]{1,0:T(8,128)S(1)}, u32[]{:S(2)}, u32[]{:S(2)}) collective-permute-start(f32[8,768]{1,0:T(8,128)S(1)} %ritz_partial_sums.2), channel_id=1, source_target_pairs={{0,8},{8,0},{1,9},{9,1},{2,10},{10,2},{3,11},{11,3},{4,12},{12,4},... | collective-permute-start | bytes 73736 | tf_op jit(solution)/shard_map/ppermute | solution.py:227

commit v27 on v25

--- a/solution.py
+++ b/solution.py
@@ -91,23 +91,25 @@
     centre_weight = 3.0 * COEFFICIENTS[0] + sum(pair_weights(n)[0] for n in (planes, ys, xs))
     scale = 2.0 / HALF
     hop = -0.5 / (SPACING * SPACING) * scale
+    regions = table_ref.shape[1]
+    values = jnp.concatenate([table_ref[...], jnp.zeros((1, xs - regions), jnp.float32)], axis=1)
+    values = jnp.broadcast_to(values, (planes, xs))
     diagonal = []
     for y in range(ys):
-        region = region_ref[y]
-        potential = jnp.zeros((planes, xs), jnp.float32)
-        for index in range(table_ref.shape[0]):
-            potential = jnp.where(region == index, table_ref[index], potential)
+        potential = jnp.take_along_axis(values, region_ref[y], axis=1)
         diagonal.append(scale * potential + (hop * centre_weight - scale * CENTRE))
     band_pos = lax.axis_index("row") * cores + lax.axis_index("core")
-    live = (lax.axis_index("grid") < counts_ref[band_pos]).astype(jnp.float32)
-    previous = [live * orb_ref[y] for y in range(ys)]
+    band = lax.broadcasted_iota(jnp.int32, counts_ref.shape, 1)
+    count = jnp.sum(jnp.where(band == band_pos, counts_ref[...], 0), axis=1, keepdims=True)
+    live = (lax.axis_index("grid") < count).astype(jnp.float32)
+    previous = [orb_ref[y] for y in range(ys)]
     current = apply(previous, [0.5 * value for value in diagonal], 0.5 * hop, None)
     for _ in range(DEGREE - 1):
         previous, current = current, apply(current, diagonal, hop, previous)
 
     blocks = ys // run
     for y in range(ys):
-        natural_ref[pl.ds((y // run) * rows + y % run, planes, stride=blocks * rows), :] = current[y]
+        natural_ref[pl.ds((y // run) * rows + y % run, planes, stride=blocks * rows), :] = live * current[y]
     for copy in range(copies):
         for tile in range(ng):
             place = order.index(copy * ng + tile)
@@ -153,7 +155,7 @@
     inputs = [
         pltpu.with_memory_space_constraint(value, pltpu.HBM)
         for value in (
-            jnp.transpose(orbitals[0], (1, 0, 2)), jnp.transpose(region, (1, 0, 2)), potential_table, counts, ritz.T
+            jnp.transpose(orbitals[0], (1, 0, 2)), jnp.transpose(region, (1, 0, 2)), potential_table[None], counts[None], ritz.T
         )
     ]
     late = sorted(range(tiles), key=lambda place: (place % ng // (ng // 2), place // ng, place % ng), reverse=True)
@@ -167,8 +169,8 @@
         scratch_shapes=[
             pltpu.VMEM((ys, planes, xs), jnp.float32),
             pltpu.VMEM((ys, planes, xs), jnp.int32),
-            pltpu.SMEM(potential_table.shape, jnp.float32),
-            pltpu.SMEM(counts.shape, jnp.int32),
+            pltpu.VMEM((1,) + potential_table.shape, jnp.float32),
+            pltpu.VMEM((1,) + counts.shape, jnp.int32),
             pltpu.VMEM((columns, panel), jnp.float32),
             pltpu.SemaphoreType.DMA((5,)),
             pltpu.VMEM((ng * rows, LANES), jnp.float32),

time: 15.7 us -> 15.7 us (level)
  no operation moved by 1% of the time
where the time goes in v27:
time: 15.7 us; the launch traced here: 15.5 us
  blocking collectives  12.2 us (78%)
  Pallas kernels  1.53 us (10%)
  waiting for transfers between devices  1.05 us (7%)
  other arithmetic  0.61 us (4%)
    all_to_all x1, blocking collectives, shards(): lax.all_to_all(packed.reshape(tiles * used, 1, LANES), ('row', 'grid'), s...  12.2 us
    pallas_call x1, Pallas kernels, shards(): pl.pallas_call(functools.partial(filter_kernel, ng, nrow, rows, used, run...  1.29 us
    ppermute x1, waiting for transfers between devices, shards(): terms.append(lax.ppermute(partial_sums(distance), 'core', pairs))  1.05 us
    add x1, other arithmetic, shards(): return functools.reduce(jnp.add, terms)  0.61 us
  transfers between devices with their start and end apart: 1, of which 1 were waited for; matrix products, arithmetic and copies ran while one was open for 0% of the time, Pallas kernels for 1%

profile of v27, /device:TPU:0, one launch (start us, length us, event | category | flops | bytes accessed | tf_op | source)
XLA Modules:
  0.0 15.5 jit_solution(6876441116668733105)
XLA Ops:
  0.0 1.3 %chebyshev_filter.1 = f32[112,128]{1,0:T(8,128)S(1)} custom-call(f32[6,8,128]{2,1,0:T(8,128)} %bitcast.14, s32[6,8,128]{2,1,0:T(8,128)} %bitcast.15, f32[1,16]{1,0:T(1,128)} %bitcast.17, s32[1,4]{1,0:T(1,128)} %bitcast.18, f32[4,8]{1,0:T(4,128)} %bitcast.16), custom_call_target="tpu_custom_call" | custom-call | tf_op jit(solution)/shard_map/chebyshev_filter/pallas_call | solution.py:164
  1.3 12.2 %all_to_all.5 = f32[112,1,128]{2,1,0:T(1,128)S(1)} all-to-all(f32[112,1,128]{2,1,0:T(1,128)S(1)} %bitcast.13), channel_id=1, replica_groups={{23,0,22,1,21,2,20,3,7,16,6,17,5,18,4,19},{31,8,30,9,29,10,28,11,15,24,..., dimensions={0} | all-to-all | bytes 114688 | tf_op jit(solution)/shard_map/all_to_all | solution.py:181
  13.5 0.1 ritz_partial_sums.2
  13.6 0.1 collective-permute-start
  13.7 0.1 ritz_partial_sums.3
  13.8 1.1 %collective-permute-done = f32[8,768]{1,0:T(8,128)S(1)} collective-permute-done((f32[8,768]{1,0:T(8,128)S(1)}, f32[8,768]{1,0:T(8,128)S(1)}, u32[]{:S(2)}, u32[]{:S(2)}) %collective-permute-start) | collective-permute-done | bytes 24608 | tf_op jit(solution)/shard_map/ppermute | solution.py:218
  14.9 0.6 %add.3 = f32[8,768]{1,0:T(8,128)} add(f32[8,768]{1,0:T(8,128)S(1)} %collective-permute-done, f32[8,768]{1,0:T(8,128)S(1)} %ritz_partial_sums.3) | non-fusion elementwise | flops 6144 | bytes 73728 | tf_op jit(solution)/shard_map/add | solution.py:220
Async XLA Ops:
  13.6 1.3 %collective-permute-start = (f32[8,768]{1,0:T(8,128)S(1)}, f32[8,768]{1,0:T(8,128)S(1)}, u32[]{:S(2)}, u32[]{:S(2)}) collective-permute-start(f32[8,768]{1,0:T(8,128)S(1)} %ritz_partial_sums.2), channel_id=1, source_target_pairs={{0,8},{8,0},{1,9},{9,1},{2,10},{10,2},{3,11},{11,3},{4,12},{12,4},... | collective-permute-start | bytes 73736 | tf_op jit(solution)/shard_map/ppermute | solution.py:218

commit v28 on v27

--- a/solution.py
+++ b/solution.py
@@ -74,9 +74,24 @@
     ]
     for transfer in transfers:
         transfer.start()
-    for transfer in transfers:
+    for transfer in transfers[:3]:
         transfer.wait()
     ys, planes, xs = orb_ref.shape
+
+    centre_weight = 3.0 * COEFFICIENTS[0] + sum(pair_weights(n)[0] for n in (planes, ys, xs))
+    scale = 2.0 / HALF
+    hop = -0.5 / (SPACING * SPACING) * scale
+    regions = table_ref.shape[1]
+    values = jnp.concatenate([table_ref[...], jnp.zeros((1, xs - regions), jnp.float32)], axis=1)
+    values = jnp.broadcast_to(values, (planes, xs))
+    diagonal = []
+    for y in range(ys):
+        potential = jnp.take_along_axis(values, region_ref[y], axis=1)
+        diagonal.append(scale * potential + (hop * centre_weight - scale * CENTRE))
+    previous = [orb_ref[y] for y in range(ys)]
+    current = apply(previous, [0.5 * value for value in diagonal], 0.5 * hop, None)
+    for transfer in transfers[3:]:
+        transfer.wait()
     columns, panel = ritz_ref.shape
     per_row = LANES // width
     for row in range(-(-columns // per_row)):
@@ -87,23 +102,10 @@
             )
             line = line + (pltpu.roll(piece, slot * width, 1) if slot else piece)
         natural_ref[pl.ds(run + row, ng, stride=rows), :] = jnp.broadcast_to(line, (ng, LANES))
-
-    centre_weight = 3.0 * COEFFICIENTS[0] + sum(pair_weights(n)[0] for n in (planes, ys, xs))
-    scale = 2.0 / HALF
-    hop = -0.5 / (SPACING * SPACING) * scale
-    regions = table_ref.shape[1]
-    values = jnp.concatenate([table_ref[...], jnp.zeros((1, xs - regions), jnp.float32)], axis=1)
-    values = jnp.broadcast_to(values, (planes, xs))
-    diagonal = []
-    for y in range(ys):
-        potential = jnp.take_along_axis(values, region_ref[y], axis=1)
-        diagonal.append(scale * potential + (hop * centre_weight - scale * CENTRE))
     band_pos = lax.axis_index("row") * cores + lax.axis_index("core")
     band = lax.broadcasted_iota(jnp.int32, counts_ref.shape, 1)
     count = jnp.sum(jnp.where(band == band_pos, counts_ref[...], 0), axis=1, keepdims=True)
     live = (lax.axis_index("grid") < count).astype(jnp.float32)
-    previous = [orb_ref[y] for y in range(ys)]
-    current = apply(previous, [0.5 * value for value in diagonal], 0.5 * hop, None)
     for _ in range(DEGREE - 1):
         previous, current = current, apply(current, diagonal, hop, previous)
 

time: 15.7 us -> 15.8 us (level)
  no operation moved by 1% of the time
where the time goes in v28:
time: 15.8 us; the launch traced here: 15.6 us
  blocking collectives  12.2 us (77%)
  Pallas kernels  1.59 us (10%)
  waiting for transfers between devices  1.05 us (7%)
  other arithmetic  0.61 us (4%)
    all_to_all x1, blocking collectives, shards(): lax.all_to_all(packed.reshape(tiles * used, 1, LANES), ('row', 'grid'), s...  12.2 us
    pallas_call x1, Pallas kernels, shards(): pl.pallas_call(functools.partial(filter_kernel, ng, nrow, rows, used, run...  1.35 us
    ppermute x1, waiting for transfers between devices, shards(): terms.append(lax.ppermute(partial_sums(distance), 'core', pairs))  1.05 us
    add x1, other arithmetic, shards(): return functools.reduce(jnp.add, terms)  0.61 us
  transfers between devices with their start and end apart: 1, of which 1 were waited for; matrix products, arithmetic and copies ran while one was open for 0% of the time, Pallas kernels for 1%

profile of v28, /device:TPU:0, one launch (start us, length us, event | category | flops | bytes accessed | tf_op | source)
XLA Modules:
  0.0 15.6 jit_solution(13013919500078158180)
XLA Ops:
  0.0 1.3 %chebyshev_filter.1 = f32[112,128]{1,0:T(8,128)S(1)} custom-call(f32[6,8,128]{2,1,0:T(8,128)} %bitcast.14, s32[6,8,128]{2,1,0:T(8,128)} %bitcast.15, f32[1,16]{1,0:T(1,128)} %bitcast.17, s32[1,4]{1,0:T(1,128)} %bitcast.18, f32[4,8]{1,0:T(4,128)} %bitcast.16), custom_call_target="tpu_custom_call" | custom-call | tf_op jit(solution)/shard_map/chebyshev_filter/pallas_call | solution.py:166
  1.4 12.2 %all_to_all.5 = f32[112,1,128]{2,1,0:T(1,128)S(1)} all-to-all(f32[112,1,128]{2,1,0:T(1,128)S(1)} %bitcast.13), channel_id=1, replica_groups={{23,0,22,1,21,2,20,3,7,16,6,17,5,18,4,19},{31,8,30,9,29,10,28,11,15,24,..., dimensions={0} | all-to-all | bytes 114688 | tf_op jit(solution)/shard_map/all_to_all | solution.py:183
  13.6 0.1 ritz_partial_sums.2
  13.7 0.1 collective-permute-start
  13.8 0.1 ritz_partial_sums.3
  13.9 1.1 %collective-permute-done = f32[8,768]{1,0:T(8,128)S(1)} collective-permute-done((f32[8,768]{1,0:T(8,128)S(1)}, f32[8,768]{1,0:T(8,128)S(1)}, u32[]{:S(2)}, u32[]{:S(2)}) %collective-permute-start) | collective-permute-done | bytes 24608 | tf_op jit(solution)/shard_map/ppermute | solution.py:220
  14.9 0.6 %add.3 = f32[8,768]{1,0:T(8,128)} add(f32[8,768]{1,0:T(8,128)S(1)} %collective-permute-done, f32[8,768]{1,0:T(8,128)S(1)} %ritz_partial_sums.3) | non-fusion elementwise | flops 6144 | bytes 73728 | tf_op jit(solution)/shard_map/add | solution.py:222
Async XLA Ops:
  13.7 1.3 %collective-permute-start = (f32[8,768]{1,0:T(8,128)S(1)}, f32[8,768]{1,0:T(8,128)S(1)}, u32[]{:S(2)}, u32[]{:S(2)}) collective-permute-start(f32[8,768]{1,0:T(8,128)S(1)} %ritz_partial_sums.2), channel_id=1, source_target_pairs={{0,8},{8,0},{1,9},{9,1},{2,10},{10,2},{3,11},{11,3},{4,12},{12,4},... | collective-permute-start | bytes 73736 | tf_op jit(solution)/shard_map/ppermute | solution.py:220

commit v29 on v27

--- a/solution.py
+++ b/solution.py
@@ -66,16 +66,7 @@
 
 
 def filter_kernel(ng, copies, rows, used, run, width, cores, order, *refs):
-    sources, out_ref, held, sems, natural_ref = refs[:5], refs[5], refs[6:11], refs[11], refs[12]
-    orb_ref, region_ref, table_ref, counts_ref, ritz_ref = held
-    transfers = [
-        pltpu.make_async_copy(source, target, sems.at[index])
-        for index, (source, target) in enumerate(zip(sources, held))
-    ]
-    for transfer in transfers:
-        transfer.start()
-    for transfer in transfers:
-        transfer.wait()
+    orb_ref, region_ref, table_ref, counts_ref, ritz_ref, out_ref, natural_ref = refs
     ys, planes, xs = orb_ref.shape
     columns, panel = ritz_ref.shape
     per_row = LANES // width
@@ -151,7 +142,6 @@
     rows = -(-used // SUBLANES) * SUBLANES
     tiles = nrow * ng
     vmem = pl.BlockSpec(memory_space=pltpu.VMEM)
-    hbm = pl.BlockSpec(memory_space=pltpu.HBM)
     inputs = [
         pltpu.with_memory_space_constraint(value, pltpu.HBM)
         for value in (
@@ -164,15 +154,9 @@
     packed = pl.pallas_call(
         functools.partial(filter_kernel, ng, nrow, rows, used, run, width, cores, order),
         out_shape=jax.ShapeDtypeStruct((tiles * used, LANES), jnp.float32),
-        in_specs=[hbm] * 5,
+        in_specs=[vmem] * 5,
         out_specs=vmem,
         scratch_shapes=[
-            pltpu.VMEM((ys, planes, xs), jnp.float32),
-            pltpu.VMEM((ys, planes, xs), jnp.int32),
-            pltpu.VMEM((1,) + potential_table.shape, jnp.float32),
-            pltpu.VMEM((1,) + counts.shape, jnp.int32),
-            pltpu.VMEM((columns, panel), jnp.float32),
-            pltpu.SemaphoreType.DMA((5,)),
             pltpu.VMEM((ng * rows, LANES), jnp.float32),
         ],
         compiler_params=pltpu.CompilerParams(vmem_limit_bytes=2 * packed_bytes + 64 * cells + 2**20),

time: 15.7 us -> 15.7 us (level)
  no operation moved by 1% of the time
where the time goes in v29:
time: 15.7 us; the launch traced here: 15.5 us
  blocking collectives  12.2 us (78%)
  Pallas kernels  1.5 us (10%)
  waiting for transfers between devices  1.05 us (7%)
  other arithmetic  0.61 us (4%)
    all_to_all x1, blocking collectives, shards(): lax.all_to_all(packed.reshape(tiles * used, 1, LANES), ('row', 'grid'), s...  12.2 us
    pallas_call x1, Pallas kernels, shards(): pl.pallas_call(functools.partial(filter_kernel, ng, nrow, rows, used, run...  1.25 us
    ppermute x1, waiting for transfers between devices, shards(): terms.append(lax.ppermute(partial_sums(distance), 'core', pairs))  1.05 us
    add x1, other arithmetic, shards(): return functools.reduce(jnp.add, terms)  0.61 us
  transfers between devices with their start and end apart: 1, of which 1 were waited for; matrix products, arithmetic and copies ran while one was open for 0% of the time, Pallas kernels for 1%

profile of v29, /device:TPU:0, one launch (start us, length us, event | category | flops | bytes accessed | tf_op | source)
XLA Modules:
  0.0 15.5 jit_solution(18002395074329440576)
XLA Ops:
  0.0 1.3 %chebyshev_filter.1 = f32[112,128]{1,0:T(8,128)S(1)} custom-call(f32[6,8,128]{2,1,0:T(8,128)} %bitcast.14, s32[6,8,128]{2,1,0:T(8,128)} %bitcast.15, f32[1,16]{1,0:T(1,128)} %bitcast.17, s32[1,4]{1,0:T(1,128)} %bitcast.18, f32[4,8]{1,0:T(4,128)} %bitcast.16), custom_call_target="tpu_custom_call" | custom-call | tf_op jit(solution)/shard_map/chebyshev_filter/pallas_call | solution.py:154
  1.3 12.2 %all_to_all.5 = f32[112,1,128]{2,1,0:T(1,128)S(1)} all-to-all(f32[112,1,128]{2,1,0:T(1,128)S(1)} %bitcast.13), channel_id=1, replica_groups={{23,0,22,1,21,2,20,3,7,16,6,17,5,18,4,19},{31,8,30,9,29,10,28,11,15,24,..., dimensions={0} | all-to-all | bytes 114688 | tf_op jit(solution)/shard_map/all_to_all | solution.py:165
  13.5 0.1 ritz_partial_sums.2
  13.6 0.1 collective-permute-start
  13.7 0.1 ritz_partial_sums.3
  13.8 1.1 %collective-permute-done = f32[8,768]{1,0:T(8,128)S(1)} collective-permute-done((f32[8,768]{1,0:T(8,128)S(1)}, f32[8,768]{1,0:T(8,128)S(1)}, u32[]{:S(2)}, u32[]{:S(2)}) %collective-permute-start) | collective-permute-done | bytes 24608 | tf_op jit(solution)/shard_map/ppermute | solution.py:202
  14.8 0.6 %add.3 = f32[8,768]{1,0:T(8,128)} add(f32[8,768]{1,0:T(8,128)S(1)} %collective-permute-done, f32[8,768]{1,0:T(8,128)S(1)} %ritz_partial_sums.3) | non-fusion elementwise | flops 6144 | bytes 73728 | tf_op jit(solution)/shard_map/add | solution.py:204
Async XLA Ops:
  13.6 1.3 %collective-permute-start = (f32[8,768]{1,0:T(8,128)S(1)}, f32[8,768]{1,0:T(8,128)S(1)}, u32[]{:S(2)}, u32[]{:S(2)}) collective-permute-start(f32[8,768]{1,0:T(8,128)S(1)} %ritz_partial_sums.2), channel_id=1, source_target_pairs={{0,8},{8,0},{1,9},{9,1},{2,10},{10,2},{3,11},{11,3},{4,12},{12,4},... | collective-permute-start | bytes 73736 | tf_op jit(solution)/shard_map/ppermute | solution.py:202

commit v30 on v29

--- a/solution.py
+++ b/solution.py
@@ -82,34 +82,30 @@
     centre_weight = 3.0 * COEFFICIENTS[0] + sum(pair_weights(n)[0] for n in (planes, ys, xs))
     scale = 2.0 / HALF
     hop = -0.5 / (SPACING * SPACING) * scale
-    regions = table_ref.shape[1]
-    values = jnp.concatenate([table_ref[...], jnp.zeros((1, xs - regions), jnp.float32)], axis=1)
-    values = jnp.broadcast_to(values, (planes, xs))
     diagonal = []
     for y in range(ys):
-        potential = jnp.take_along_axis(values, region_ref[y], axis=1)
+        region = region_ref[y]
+        potential = jnp.zeros((planes, xs), jnp.float32)
+        for index in range(table_ref.shape[0]):
+            potential = jnp.where(region == index, table_ref[index], potential)
         diagonal.append(scale * potential + (hop * centre_weight - scale * CENTRE))
     band_pos = lax.axis_index("row") * cores + lax.axis_index("core")
-    band = lax.broadcasted_iota(jnp.int32, counts_ref.shape, 1)
-    count = jnp.sum(jnp.where(band == band_pos, counts_ref[...], 0), axis=1, keepdims=True)
-    live = (lax.axis_index("grid") < count).astype(jnp.float32)
-    previous = [orb_ref[y] for y in range(ys)]
+    live = (lax.axis_index("grid") < counts_ref[band_pos]).astype(jnp.float32)
+    previous = [live * orb_ref[y] for y in range(ys)]
     current = apply(previous, [0.5 * value for value in diagonal], 0.5 * hop, None)
     for _ in range(DEGREE - 1):
         previous, current = current, apply(current, diagonal, hop, previous)
 
     blocks = ys // run
     for y in range(ys):
-        natural_ref[pl.ds((y // run) * rows + y % run, planes, stride=blocks * rows), :] = live * current[y]
+        natural_ref[pl.ds((y // run) * rows + y % run, planes, stride=blocks * rows), :] = current[y]
     for copy in range(copies):
         for tile in range(ng):
             place = order.index(copy * ng + tile)
             out_ref[pl.ds(place * used, used), :] = natural_ref[pl.ds(tile * rows, used), :]
 
 
-def partial_kernel(nrow, ng, used, run, width, columns, cores, order, distance, got_ref, out_ref, ritz_ref):
-    for place, source in enumerate(order):
-        ritz_ref[source] = got_ref[pl.ds(place * used + run, 1), :]
+def partial_kernel(nrow, ng, used, run, width, columns, cores, order, distance, got_ref, out_ref):
     wanted = out_ref.shape[0]
     holders = wanted // columns
     sublane = lax.broadcasted_iota(jnp.int32, (wanted, LANES), 0)
@@ -118,7 +114,8 @@
     for row in range(nrow):
         lines = jnp.zeros((wanted, LANES), jnp.float32)
         for k in range(holders):
-            line = ritz_ref[row * ng + block * holders + k]
+            place = order.index(row * ng) - block * holders - k
+            line = got_ref[pl.ds(place * used + run, 1), :]
             lines = jnp.where(sublane // columns == k, jnp.broadcast_to(line, (wanted, LANES)), lines)
         for r in range(ng):
             weight = jnp.take_along_axis(lines, sublane % columns * width + r, axis=1)
@@ -142,19 +139,19 @@
     rows = -(-used // SUBLANES) * SUBLANES
     tiles = nrow * ng
     vmem = pl.BlockSpec(memory_space=pltpu.VMEM)
+    smem = pl.BlockSpec(memory_space=pltpu.SMEM)
     inputs = [
         pltpu.with_memory_space_constraint(value, pltpu.HBM)
         for value in (
-            jnp.transpose(orbitals[0], (1, 0, 2)), jnp.transpose(region, (1, 0, 2)), potential_table[None], counts[None], ritz.T
+            jnp.transpose(orbitals[0], (1, 0, 2)), jnp.transpose(region, (1, 0, 2)), potential_table, counts, ritz.T
         )
     ]
-    late = sorted(range(tiles), key=lambda place: (place % ng // (ng // 2), place // ng, place % ng), reverse=True)
-    order = [place for pair in zip(late, late[::-1]) for place in pair][:tiles]
+    order = list(range(tiles))[::-1]
     packed_bytes = 4 * tiles * rows * LANES
     packed = pl.pallas_call(
         functools.partial(filter_kernel, ng, nrow, rows, used, run, width, cores, order),
         out_shape=jax.ShapeDtypeStruct((tiles * used, LANES), jnp.float32),
-        in_specs=[vmem] * 5,
+        in_specs=[vmem, vmem, smem, smem, vmem],
         out_specs=vmem,
         scratch_shapes=[
             pltpu.VMEM((ng * rows, LANES), jnp.float32),
@@ -174,7 +171,6 @@
                 out_shape=sum_shape,
                 in_specs=[vmem],
                 out_specs=vmem,
-                scratch_shapes=[pltpu.VMEM((tiles, 1, LANES), jnp.float32)],
                 compiler_params=pltpu.CompilerParams(vmem_limit_bytes=packed_bytes + 2**20),
                 name="ritz_partial_sums",
             )(got)

time: 15.7 us -> 15.6 us (level)
  no operation moved by 1% of the time
where the time goes in v30:
time: 15.6 us; the launch traced here: 15.4 us
  blocking collectives  12.2 us (78%)
  Pallas kernels  1.49 us (10%)
  waiting for transfers between devices  1.05 us (7%)
  other arithmetic  0.61 us (4%)
    all_to_all x1, blocking collectives, shards(): lax.all_to_all(packed.reshape(tiles * used, 1, LANES), ('row', 'grid'), s...  12.2 us
    pallas_call x1, Pallas kernels, shards(): pl.pallas_call(functools.partial(filter_kernel, ng, nrow, rows, used, run...  1.25 us
    ppermute x1, waiting for transfers between devices, shards(): terms.append(lax.ppermute(partial_sums(distance), 'core', pairs))  1.05 us
    add x1, other arithmetic, shards(): return functools.reduce(jnp.add, terms)  0.61 us
  transfers between devices with their start and end apart: 1, of which 1 were waited for; matrix products, arithmetic and copies ran while one was open for 0% of the time, Pallas kernels for 1%

profile of v30, /device:TPU:0, one launch (start us, length us, event | category | flops | bytes accessed | tf_op | source)
XLA Modules:
  0.0 15.4 jit_solution(8196537101396789312)
XLA Ops:
  0.0 1.3 %chebyshev_filter.1 = f32[112,128]{1,0:T(8,128)S(1)} custom-call(f32[6,8,128]{2,1,0:T(8,128)} %bitcast.12, s32[6,8,128]{2,1,0:T(8,128)} %bitcast.13, f32[16]{0:T(128)} %refs_2_.1, s32[4]{0:T(128)} %refs_3_.1, f32[4,8]{1,0:T(4,128)} %bitcast.14), custom_call_target="tpu_custom_call" | custom-call | tf_op jit(solution)/shard_map/chebyshev_filter/pallas_call | solution.py:151
  1.3 12.2 %all_to_all.5 = f32[112,1,128]{2,1,0:T(1,128)S(1)} all-to-all(f32[112,1,128]{2,1,0:T(1,128)S(1)} %bitcast.11), channel_id=1, replica_groups={{23,22,21,20,19,18,17,16,7,6,5,4,3,2,1,0},{31,30,29,28,27,26,25,24,15,1..., dimensions={0} | all-to-all | bytes 114688 | tf_op jit(solution)/shard_map/all_to_all | solution.py:162
  13.4 0.1 ritz_partial_sums.2
  13.6 0.1 collective-permute-start
  13.6 0.1 ritz_partial_sums.3
  13.8 1.1 %collective-permute-done = f32[8,768]{1,0:T(8,128)S(1)} collective-permute-done((f32[8,768]{1,0:T(8,128)S(1)}, f32[8,768]{1,0:T(8,128)S(1)}, u32[]{:S(2)}, u32[]{:S(2)}) %collective-permute-start) | collective-permute-done | bytes 24608 | tf_op jit(solution)/shard_map/ppermute | solution.py:198
  14.8 0.6 %add.3 = f32[8,768]{1,0:T(8,128)} add(f32[8,768]{1,0:T(8,128)S(1)} %collective-permute-done, f32[8,768]{1,0:T(8,128)S(1)} %ritz_partial_sums.3) | non-fusion elementwise | flops 6144 | bytes 73728 | tf_op jit(solution)/shard_map/add | solution.py:200
Async XLA Ops:
  13.6 1.3 %collective-permute-start = (f32[8,768]{1,0:T(8,128)S(1)}, f32[8,768]{1,0:T(8,128)S(1)}, u32[]{:S(2)}, u32[]{:S(2)}) collective-permute-start(f32[8,768]{1,0:T(8,128)S(1)} %ritz_partial_sums.2), channel_id=1, source_target_pairs={{0,8},{8,0},{1,9},{9,1},{2,10},{10,2},{3,11},{11,3},{4,12},{12,4},... | collective-permute-start | bytes 73736 | tf_op jit(solution)/shard_map/ppermute | solution.py:198

commit v31 on v29

--- a/solution.py
+++ b/solution.py
@@ -65,8 +65,8 @@
     return results
 
 
-def filter_kernel(ng, copies, rows, used, run, width, cores, order, *refs):
-    orb_ref, region_ref, table_ref, counts_ref, ritz_ref, out_ref, natural_ref = refs
+def filter_kernel(ng, copies, used, run, width, cores, *refs):
+    orb_ref, region_ref, table_ref, counts_ref, ritz_ref, out_ref = refs
     ys, planes, xs = orb_ref.shape
     columns, panel = ritz_ref.shape
     per_row = LANES // width
@@ -77,7 +77,7 @@
                 [ritz_ref[pl.ds(row * per_row + slot, 1), :], jnp.zeros((1, LANES - panel), jnp.float32)], axis=1
             )
             line = line + (pltpu.roll(piece, slot * width, 1) if slot else piece)
-        natural_ref[pl.ds(run + row, ng, stride=rows), :] = jnp.broadcast_to(line, (ng, LANES))
+        out_ref[pl.ds(run + row, copies * ng, stride=used), :] = jnp.broadcast_to(line, (copies * ng, LANES))
 
     centre_weight = 3.0 * COEFFICIENTS[0] + sum(pair_weights(n)[0] for n in (planes, ys, xs))
     scale = 2.0 / HALF
@@ -100,11 +100,13 @@
 
     blocks = ys // run
     for y in range(ys):
-        natural_ref[pl.ds((y // run) * rows + y % run, planes, stride=blocks * rows), :] = live * current[y]
-    for copy in range(copies):
-        for tile in range(ng):
-            place = order.index(copy * ng + tile)
-            out_ref[pl.ds(place * used, used), :] = natural_ref[pl.ds(tile * rows, used), :]
+        masked = live * current[y]
+        for copy in range(copies):
+            first = (copy * ng + y // run + 1) * used + y % run
+            count = planes if copy < copies - 1 or y // run < blocks - 1 else planes - 1
+            out_ref[pl.ds(first, count, stride=blocks * used), :] = masked[:count]
+            if count < planes:
+                out_ref[pl.ds(y % run, 1), :] = masked[count:]
 
 
 def partial_kernel(nrow, ng, used, run, width, columns, cores, order, distance, got_ref, out_ref, ritz_ref):
@@ -139,7 +141,6 @@
     per_row = LANES // width
     ritz_rows = -(-columns // per_row)
     used = run + ritz_rows
-    rows = -(-used // SUBLANES) * SUBLANES
     tiles = nrow * ng
     vmem = pl.BlockSpec(memory_space=pltpu.VMEM)
     inputs = [
@@ -148,17 +149,13 @@
             jnp.transpose(orbitals[0], (1, 0, 2)), jnp.transpose(region, (1, 0, 2)), potential_table[None], counts[None], ritz.T
         )
     ]
-    late = sorted(range(tiles), key=lambda place: (place % ng // (ng // 2), place // ng, place % ng), reverse=True)
-    order = [place for pair in zip(late, late[::-1]) for place in pair][:tiles]
-    packed_bytes = 4 * tiles * rows * LANES
+    order = [tiles - 1] + list(range(tiles - 1))
+    packed_bytes = 4 * tiles * used * LANES
     packed = pl.pallas_call(
-        functools.partial(filter_kernel, ng, nrow, rows, used, run, width, cores, order),
+        functools.partial(filter_kernel, ng, nrow, used, run, width, cores),
         out_shape=jax.ShapeDtypeStruct((tiles * used, LANES), jnp.float32),
         in_specs=[vmem] * 5,
         out_specs=vmem,
-        scratch_shapes=[
-            pltpu.VMEM((ng * rows, LANES), jnp.float32),
-        ],
         compiler_params=pltpu.CompilerParams(vmem_limit_bytes=2 * packed_bytes + 64 * cells + 2**20),
         name="chebyshev_filter",
     )(*inputs)

time: 15.7 us -> 15.7 us (level)
  no operation moved by 1% of the time
where the time goes in v31:
time: 15.7 us; the launch traced here: 15.5 us
  blocking collectives  12.2 us (78%)
  Pallas kernels  1.48 us (9%)
  waiting for transfers between devices  1.05 us (7%)
  other arithmetic  0.61 us (4%)
    all_to_all x1, blocking collectives, shards(): lax.all_to_all(packed.reshape(tiles * used, 1, LANES), ('row', 'grid'), s...  12.2 us
    pallas_call x1, Pallas kernels, shards(): pl.pallas_call(functools.partial(filter_kernel, ng, nrow, used, run, widt...  1.24 us
    ppermute x1, waiting for transfers between devices, shards(): terms.append(lax.ppermute(partial_sums(distance), 'core', pairs))  1.05 us
    add x1, other arithmetic, shards(): return functools.reduce(jnp.add, terms)  0.61 us
  transfers between devices with their start and end apart: 1, of which 1 were waited for; matrix products, arithmetic and copies ran while one was open for 0% of the time, Pallas kernels for 1%

profile of v31, /device:TPU:0, one launch (start us, length us, event | category | flops | bytes accessed | tf_op | source)
XLA Modules:
  0.0 15.5 jit_solution(2209658471740266106)
XLA Ops:
  0.0 1.2 %chebyshev_filter.1 = f32[112,128]{1,0:T(8,128)S(1)} custom-call(f32[6,8,128]{2,1,0:T(8,128)} %bitcast.14, s32[6,8,128]{2,1,0:T(8,128)} %bitcast.15, f32[1,16]{1,0:T(1,128)} %bitcast.17, s32[1,4]{1,0:T(1,128)} %bitcast.18, f32[4,8]{1,0:T(4,128)} %bitcast.16), custom_call_target="tpu_custom_call" | custom-call | tf_op jit(solution)/shard_map/chebyshev_filter/pallas_call | solution.py:154
  1.2 12.2 %all_to_all.5 = f32[112,1,128]{2,1,0:T(1,128)S(1)} all-to-all(f32[112,1,128]{2,1,0:T(1,128)S(1)} %bitcast.13), channel_id=1, replica_groups={{23,0,1,2,3,4,5,6,7,16,17,18,19,20,21,22},{31,8,9,10,11,12,13,14,15,24,..., dimensions={0} | all-to-all | bytes 114688 | tf_op jit(solution)/shard_map/all_to_all | solution.py:162
  13.5 0.1 ritz_partial_sums.2
  13.6 0.1 collective-permute-start
  13.7 0.1 ritz_partial_sums.3
  13.8 1.1 %collective-permute-done = f32[8,768]{1,0:T(8,128)S(1)} collective-permute-done((f32[8,768]{1,0:T(8,128)S(1)}, f32[8,768]{1,0:T(8,128)S(1)}, u32[]{:S(2)}, u32[]{:S(2)}) %collective-permute-start) | collective-permute-done | bytes 24608 | tf_op jit(solution)/shard_map/ppermute | solution.py:199
  14.9 0.6 %add.3 = f32[8,768]{1,0:T(8,128)} add(f32[8,768]{1,0:T(8,128)S(1)} %collective-permute-done, f32[8,768]{1,0:T(8,128)S(1)} %ritz_partial_sums.3) | non-fusion elementwise | flops 6144 | bytes 73728 | tf_op jit(solution)/shard_map/add | solution.py:201
Async XLA Ops:
  13.6 1.3 %collective-permute-start = (f32[8,768]{1,0:T(8,128)S(1)}, f32[8,768]{1,0:T(8,128)S(1)}, u32[]{:S(2)}, u32[]{:S(2)}) collective-permute-start(f32[8,768]{1,0:T(8,128)S(1)} %ritz_partial_sums.2), channel_id=1, source_target_pairs={{0,8},{8,0},{1,9},{9,1},{2,10},{10,2},{3,11},{11,3},{4,12},{12,4},... | collective-permute-start | bytes 73736 | tf_op jit(solution)/shard_map/ppermute | solution.py:199

commit v32 on v29

--- a/solution.py
+++ b/solution.py
@@ -101,10 +101,10 @@
     blocks = ys // run
     for y in range(ys):
         natural_ref[pl.ds((y // run) * rows + y % run, planes, stride=blocks * rows), :] = live * current[y]
-    for copy in range(copies):
-        for tile in range(ng):
-            place = order.index(copy * ng + tile)
-            out_ref[pl.ds(place * used, used), :] = natural_ref[pl.ds(tile * rows, used), :]
+    for tile in range(ng):
+        value = natural_ref[pl.ds(tile * rows, used), :]
+        for copy in range(copies):
+            out_ref[pl.ds(order.index(copy * ng + tile) * used, used), :] = value
 
 
 def partial_kernel(nrow, ng, used, run, width, columns, cores, order, distance, got_ref, out_ref, ritz_ref):

time: 15.7 us -> 15.7 us (level)
  no operation moved by 1% of the time
where the time goes in v32:
time: 15.7 us; the launch traced here: 15.5 us
  blocking collectives  12.2 us (78%)
  Pallas kernels  1.5 us (10%)
  waiting for transfers between devices  1.05 us (7%)
  other arithmetic  0.61 us (4%)
    all_to_all x1, blocking collectives, shards(): lax.all_to_all(packed.reshape(tiles * used, 1, LANES), ('row', 'grid'), s...  12.2 us
    pallas_call x1, Pallas kernels, shards(): pl.pallas_call(functools.partial(filter_kernel, ng, nrow, rows, used, run...  1.25 us
    ppermute x1, waiting for transfers between devices, shards(): terms.append(lax.ppermute(partial_sums(distance), 'core', pairs))  1.05 us
    add x1, other arithmetic, shards(): return functools.reduce(jnp.add, terms)  0.61 us
  transfers between devices with their start and end apart: 1, of which 1 were waited for; matrix products, arithmetic and copies ran while one was open for 0% of the time, Pallas kernels for 1%

profile of v32, /device:TPU:0, one launch (start us, length us, event | category | flops | bytes accessed | tf_op | source)
XLA Modules:
  0.0 15.5 jit_solution(18092939754156184795)
XLA Ops:
  0.0 1.2 %chebyshev_filter.1 = f32[112,128]{1,0:T(8,128)S(1)} custom-call(f32[6,8,128]{2,1,0:T(8,128)} %bitcast.14, s32[6,8,128]{2,1,0:T(8,128)} %bitcast.15, f32[1,16]{1,0:T(1,128)} %bitcast.17, s32[1,4]{1,0:T(1,128)} %bitcast.18, f32[4,8]{1,0:T(4,128)} %bitcast.16), custom_call_target="tpu_custom_call" | custom-call | tf_op jit(solution)/shard_map/chebyshev_filter/pallas_call | solution.py:154
  1.3 12.2 %all_to_all.5 = f32[112,1,128]{2,1,0:T(1,128)S(1)} all-to-all(f32[112,1,128]{2,1,0:T(1,128)S(1)} %bitcast.13), channel_id=1, replica_groups={{23,0,22,1,21,2,20,3,7,16,6,17,5,18,4,19},{31,8,30,9,29,10,28,11,15,24,..., dimensions={0} | all-to-all | bytes 114688 | tf_op jit(solution)/shard_map/all_to_all | solution.py:165
  13.5 0.1 ritz_partial_sums.2
  13.6 0.1 collective-permute-start
  13.7 0.1 ritz_partial_sums.3
  13.8 1.1 %collective-permute-done = f32[8,768]{1,0:T(8,128)S(1)} collective-permute-done((f32[8,768]{1,0:T(8,128)S(1)}, f32[8,768]{1,0:T(8,128)S(1)}, u32[]{:S(2)}, u32[]{:S(2)}) %collective-permute-start) | collective-permute-done | bytes 24608 | tf_op jit(solution)/shard_map/ppermute | solution.py:202
  14.8 0.6 %add.3 = f32[8,768]{1,0:T(8,128)} add(f32[8,768]{1,0:T(8,128)S(1)} %collective-permute-done, f32[8,768]{1,0:T(8,128)S(1)} %ritz_partial_sums.3) | non-fusion elementwise | flops 6144 | bytes 73728 | tf_op jit(solution)/shard_map/add | solution.py:204
Async XLA Ops:
  13.6 1.3 %collective-permute-start = (f32[8,768]{1,0:T(8,128)S(1)}, f32[8,768]{1,0:T(8,128)S(1)}, u32[]{:S(2)}, u32[]{:S(2)}) collective-permute-start(f32[8,768]{1,0:T(8,128)S(1)} %ritz_partial_sums.2), channel_id=1, source_target_pairs={{0,8},{8,0},{1,9},{9,1},{2,10},{10,2},{3,11},{11,3},{4,12},{12,4},... | collective-permute-start | bytes 73736 | tf_op jit(solution)/shard_map/ppermute | solution.py:202

commit v33 on v32

--- a/solution.py
+++ b/solution.py
@@ -44,10 +44,13 @@
     return weights[0], pairs
 
 
-def apply(field, diagonal, hop, before):
+def apply(field, diagonal, hop, before, twice_ref):
     ys = len(field)
     planes, xs = field[0].shape
     along_y, along_planes, along_x = [pair_weights(length)[1] for length in (ys, planes, xs)]
+    for y in range(ys):
+        twice_ref[y, pl.ds(0, planes), :] = field[y]
+        twice_ref[y, pl.ds(planes, planes), :] = field[y]
     results = []
     for y in range(ys):
         tile = field[y]
@@ -56,17 +59,18 @@
             total = total - before[y]
         for shifts, weight in along_y:
             total = total + (hop * weight) * functools.reduce(jnp.add, [field[(y - shift) % ys] for shift in shifts])
-        for pairs, axis in ((along_planes, 0), (along_x, 1)):
-            for shifts, weight in pairs:
-                total = total + (hop * weight) * functools.reduce(
-                    jnp.add, [pltpu.roll(tile, shift, axis) for shift in shifts]
-                )
+        for shifts, weight in along_planes:
+            total = total + (hop * weight) * functools.reduce(
+                jnp.add, [twice_ref[y, pl.ds(planes - shift, planes), :] for shift in shifts]
+            )
+        for shifts, weight in along_x:
+            total = total + (hop * weight) * functools.reduce(jnp.add, [pltpu.roll(tile, shift, 1) for shift in shifts])
         results.append(total)
     return results
 
 
 def filter_kernel(ng, copies, rows, used, run, width, cores, order, *refs):
-    orb_ref, region_ref, table_ref, counts_ref, ritz_ref, out_ref, natural_ref = refs
+    orb_ref, region_ref, table_ref, counts_ref, ritz_ref, out_ref, natural_ref, twice_ref = refs
     ys, planes, xs = orb_ref.shape
     columns, panel = ritz_ref.shape
     per_row = LANES // width
@@ -94,9 +98,9 @@
     count = jnp.sum(jnp.where(band == band_pos, counts_ref[...], 0), axis=1, keepdims=True)
     live = (lax.axis_index("grid") < count).astype(jnp.float32)
     previous = [orb_ref[y] for y in range(ys)]
-    current = apply(previous, [0.5 * value for value in diagonal], 0.5 * hop, None)
+    current = apply(previous, [0.5 * value for value in diagonal], 0.5 * hop, None, twice_ref)
     for _ in range(DEGREE - 1):
-        previous, current = current, apply(current, diagonal, hop, previous)
+        previous, current = current, apply(current, diagonal, hop, previous, twice_ref)
 
     blocks = ys // run
     for y in range(ys):
@@ -158,6 +162,7 @@
         out_specs=vmem,
         scratch_shapes=[
             pltpu.VMEM((ng * rows, LANES), jnp.float32),
+            pltpu.VMEM((ys, 2 * planes, xs), jnp.float32),
         ],
         compiler_params=pltpu.CompilerParams(vmem_limit_bytes=2 * packed_bytes + 64 * cells + 2**20),
         name="chebyshev_filter",

time: 15.7 us -> 15.7 us (level)
  no operation moved by 1% of the time
where the time goes in v33:
time: 15.7 us; the launch traced here: 15.5 us
  blocking collectives  12.2 us (78%)
  Pallas kernels  1.5 us (10%)
  waiting for transfers between devices  1.05 us (7%)
  other arithmetic  0.61 us (4%)
    all_to_all x1, blocking collectives, shards(): lax.all_to_all(packed.reshape(tiles * used, 1, LANES), ('row', 'grid'), s...  12.2 us
    pallas_call x1, Pallas kernels, shards(): pl.pallas_call(functools.partial(filter_kernel, ng, nrow, rows, used, run...  1.25 us
    ppermute x1, waiting for transfers between devices, shards(): terms.append(lax.ppermute(partial_sums(distance), 'core', pairs))  1.05 us
    add x1, other arithmetic, shards(): return functools.reduce(jnp.add, terms)  0.61 us
  transfers between devices with their start and end apart: 1, of which 1 were waited for; matrix products, arithmetic and copies ran while one was open for 0% of the time, Pallas kernels for 1%

profile of v33, /device:TPU:0, one launch (start us, length us, event | category | flops | bytes accessed | tf_op | source)
XLA Modules:
  0.0 15.5 jit_solution(12012323837894473923)
XLA Ops:
  0.0 1.2 %chebyshev_filter.1 = f32[112,128]{1,0:T(8,128)S(1)} custom-call(f32[6,8,128]{2,1,0:T(8,128)} %bitcast.14, s32[6,8,128]{2,1,0:T(8,128)} %bitcast.15, f32[1,16]{1,0:T(1,128)} %bitcast.17, s32[1,4]{1,0:T(1,128)} %bitcast.18, f32[4,8]{1,0:T(4,128)} %bitcast.16), custom_call_target="tpu_custom_call" | custom-call | tf_op jit(solution)/shard_map/chebyshev_filter/pallas_call | solution.py:158
  1.3 12.2 %all_to_all.5 = f32[112,1,128]{2,1,0:T(1,128)S(1)} all-to-all(f32[112,1,128]{2,1,0:T(1,128)S(1)} %bitcast.13), channel_id=1, replica_groups={{23,0,22,1,21,2,20,3,7,16,6,17,5,18,4,19},{31,8,30,9,29,10,28,11,15,24,..., dimensions={0} | all-to-all | bytes 114688 | tf_op jit(solution)/shard_map/all_to_all | solution.py:170
  13.5 0.1 ritz_partial_sums.2
  13.6 0.1 collective-permute-start
  13.7 0.1 ritz_partial_sums.3
  13.8 1.1 %collective-permute-done = f32[8,768]{1,0:T(8,128)S(1)} collective-permute-done((f32[8,768]{1,0:T(8,128)S(1)}, f32[8,768]{1,0:T(8,128)S(1)}, u32[]{:S(2)}, u32[]{:S(2)}) %collective-permute-start) | collective-permute-done | bytes 24608 | tf_op jit(solution)/shard_map/ppermute | solution.py:207
  14.8 0.6 %add.3 = f32[8,768]{1,0:T(8,128)} add(f32[8,768]{1,0:T(8,128)S(1)} %collective-permute-done, f32[8,768]{1,0:T(8,128)S(1)} %ritz_partial_sums.3) | non-fusion elementwise | flops 6144 | bytes 73728 | tf_op jit(solution)/shard_map/add | solution.py:209
Async XLA Ops:
  13.6 1.3 %collective-permute-start = (f32[8,768]{1,0:T(8,128)S(1)}, f32[8,768]{1,0:T(8,128)S(1)}, u32[]{:S(2)}, u32[]{:S(2)}) collective-permute-start(f32[8,768]{1,0:T(8,128)S(1)} %ritz_partial_sums.2), channel_id=1, source_target_pairs={{0,8},{8,0},{1,9},{9,1},{2,10},{10,2},{3,11},{11,3},{4,12},{12,4},... | collective-permute-start | bytes 73736 | tf_op jit(solution)/shard_map/ppermute | solution.py:207

commit v34 on v31

--- a/solution.py
+++ b/solution.py
@@ -95,12 +95,14 @@
     live = (lax.axis_index("grid") < count).astype(jnp.float32)
     previous = [orb_ref[y] for y in range(ys)]
     current = apply(previous, [0.5 * value for value in diagonal], 0.5 * hop, None)
+    previous = [live * value for value in previous]
+    current = [live * value for value in current]
     for _ in range(DEGREE - 1):
         previous, current = current, apply(current, diagonal, hop, previous)
 
     blocks = ys // run
     for y in range(ys):
-        masked = live * current[y]
+        masked = current[y]
         for copy in range(copies):
             first = (copy * ng + y // run + 1) * used + y % run
             count = planes if copy < copies - 1 or y // run < blocks - 1 else planes - 1

time: 15.7 us -> 15.7 us (level)
  no operation moved by 1% of the time
where the time goes in v34:
time: 15.7 us; the launch traced here: 15.5 us
  blocking collectives  12.2 us (78%)
  Pallas kernels  1.48 us (9%)
  waiting for transfers between devices  1.05 us (7%)
  other arithmetic  0.61 us (4%)
    all_to_all x1, blocking collectives, shards(): lax.all_to_all(packed.reshape(tiles * used, 1, LANES), ('row', 'grid'), s...  12.2 us
    pallas_call x1, Pallas kernels, shards(): pl.pallas_call(functools.partial(filter_kernel, ng, nrow, used, run, widt...  1.23 us
    ppermute x1, waiting for transfers between devices, shards(): terms.append(lax.ppermute(partial_sums(distance), 'core', pairs))  1.05 us
    add x1, other arithmetic, shards(): return functools.reduce(jnp.add, terms)  0.61 us
  transfers between devices with their start and end apart: 1, of which 1 were waited for; matrix products, arithmetic and copies ran while one was open for 0% of the time, Pallas kernels for 1%

profile of v34, /device:TPU:0, one launch (start us, length us, event | category | flops | bytes accessed | tf_op | source)
XLA Modules:
  0.0 15.5 jit_solution(142781540481552921)
XLA Ops:
  0.0 1.2 %chebyshev_filter.1 = f32[112,128]{1,0:T(8,128)S(1)} custom-call(f32[6,8,128]{2,1,0:T(8,128)} %bitcast.14, s32[6,8,128]{2,1,0:T(8,128)} %bitcast.15, f32[1,16]{1,0:T(1,128)} %bitcast.17, s32[1,4]{1,0:T(1,128)} %bitcast.18, f32[4,8]{1,0:T(4,128)} %bitcast.16), custom_call_target="tpu_custom_call" | custom-call | tf_op jit(solution)/shard_map/chebyshev_filter/pallas_call | solution.py:156
  1.2 12.2 %all_to_all.5 = f32[112,1,128]{2,1,0:T(1,128)S(1)} all-to-all(f32[112,1,128]{2,1,0:T(1,128)S(1)} %bitcast.13), channel_id=1, replica_groups={{23,0,1,2,3,4,5,6,7,16,17,18,19,20,21,22},{31,8,9,10,11,12,13,14,15,24,..., dimensions={0} | all-to-all | bytes 114688 | tf_op jit(solution)/shard_map/all_to_all | solution.py:164
  13.5 0.1 ritz_partial_sums.2
  13.6 0.1 collective-permute-start
  13.7 0.1 ritz_partial_sums.3
  13.8 1.1 %collective-permute-done = f32[8,768]{1,0:T(8,128)S(1)} collective-permute-done((f32[8,768]{1,0:T(8,128)S(1)}, f32[8,768]{1,0:T(8,128)S(1)}, u32[]{:S(2)}, u32[]{:S(2)}) %collective-permute-start) | collective-permute-done | bytes 24608 | tf_op jit(solution)/shard_map/ppermute | solution.py:201
  14.9 0.6 %add.3 = f32[8,768]{1,0:T(8,128)} add(f32[8,768]{1,0:T(8,128)S(1)} %collective-permute-done, f32[8,768]{1,0:T(8,128)S(1)} %ritz_partial_sums.3) | non-fusion elementwise | flops 6144 | bytes 73728 | tf_op jit(solution)/shard_map/add | solution.py:203
Async XLA Ops:
  13.6 1.3 %collective-permute-start = (f32[8,768]{1,0:T(8,128)S(1)}, f32[8,768]{1,0:T(8,128)S(1)}, u32[]{:S(2)}, u32[]{:S(2)}) collective-permute-start(f32[8,768]{1,0:T(8,128)S(1)} %ritz_partial_sums.2), channel_id=1, source_target_pairs={{0,8},{8,0},{1,9},{9,1},{2,10},{10,2},{3,11},{11,3},{4,12},{12,4},... | collective-permute-start | bytes 73736 | tf_op jit(solution)/shard_map/ppermute | solution.py:201
